TPU v7x, 32 devices: a whole 2x2x4 slice. The times are simulated.
32 devices in a mesh: dp: 4 (over x, core), blk: 2 (over y), mp: 4 (over z).
Axes of the slice: x: 2, y: 2, z: 4, core: 2. Of those that a mesh axis runs over, the one named last changes fastest.
Arguments:
- tokens: bfloat16 [2048, 7168], P('dp', ('blk', 'mp')), may hold values from -6 to 6
- trainer_q: float32 [3584, 7168], P(('mp', 'blk'), 'dp'), may hold values from -0.0625 to 0.0625
- kv_pool: bfloat16 [2, 1024, 3584], P(None, ('dp', 'blk'), 'mp')
- prompt_kv: bfloat16 [2, 2048, 3584], P(None, ('dp', 'blk'), 'mp'), may hold values from -15 to 15
- page_table: int32 [8, 8], P(('dp', 'blk')), may hold values from 0 to 15, as said below
- page_count: int32 [8], P(('dp', 'blk')), may hold values from 1 to 8
- prompt_len: int32 [8], P(('dp', 'blk')), may hold values from 64 to 256
Outputs:
- server_q: bfloat16 [3584, 7168], P('mp', 'blk')
- attn_out: bfloat16 [2048, 3584], P(('dp', 'blk'), 'mp')
Inputs may be any that keep to these rules, and one draw needn't show every extreme that they name: `page_table`: the entries of a row are distinct page numbers of the request's group.
All inputs are finite; a program needn't handle non-finite values.
Results may differ from a plain program's by a relative error of at most 0.012.
The roundings to bfloat16 on the way count: a program that leaves them out, or rounds other values in their place, can miss the bound.
Values may be sent and summed in bfloat16 or wider, within the bound.
No kernel may reach another device: no remote copies, remote signals or barrier semaphores. Data moves between devices by JAX's collectives and lax.ppermute only.
A program may use at most 128 MiB of HBM per device.

v0:
```python
import jax
import jax.numpy as jnp
from jax import lax
from jax.sharding import PartitionSpec as P

HD = 224
PAGE = 16


def attend_block(softmax_state, query_heads, key_heads, value_heads, key_mask):
    running_max, row_total, weighted = softmax_state
    scores = jnp.einsum(
        "thd,khd->htk", query_heads, key_heads, preferred_element_type=jnp.float32
    ) * HD ** (-0.5)
    scores = jnp.where(key_mask[None], scores, -1e30)
    new_max = jnp.maximum(running_max, jnp.max(scores, axis=2))
    weights = jnp.where(key_mask[None], jnp.exp(scores - new_max[:, :, None]), 0.0)
    factor = jnp.exp(running_max - new_max)
    row_total = row_total * factor + jnp.sum(weights, axis=2)
    weighted = weighted * factor[:, :, None] + jnp.einsum(
        "htk,khd->htd",
        weights.astype(jnp.bfloat16),
        value_heads,
        preferred_element_type=jnp.float32,
    )
    return (new_max, row_total, weighted)


def body(tokens, trainer_q, kv_pool, prompt_kv, page_table, page_count, prompt_len):
    trainer_rows = lax.all_gather(trainer_q.astype(jnp.bfloat16), "dp", axis=1, tiled=True)
    server_q = lax.all_to_all(trainer_rows, "blk", split_axis=1, concat_axis=0, tiled=True)
    features = lax.all_gather(tokens, "mp", axis=1, tiled=True)
    own_rows = features.shape[0] // lax.axis_size("blk")
    head_width = server_q.shape[0]
    token_local = lax.all_to_all(features, "blk", split_axis=0, concat_axis=1, tiled=True)
    queries = jnp.einsum(
        "td,hd->th",
        token_local,
        lax.all_gather(server_q, "blk", axis=1, tiled=True),
        preferred_element_type=jnp.float32,
    )
    queries = queries.astype(jnp.bfloat16)
    head_count = head_width // HD
    query_heads = queries.reshape(own_rows, head_count, HD)
    length = prompt_len[0]
    row_pages = page_table[0]
    live_slots = jnp.arange(row_pages.shape[0], dtype=jnp.int32) < page_count[0]
    row_index = jnp.arange(own_rows, dtype=jnp.int32)
    own_mask = (row_index[None, :] <= row_index[:, None]) & (row_index[None, :] < length)
    softmax_state = (
        jnp.full((head_count, own_rows), -1e30, jnp.float32),
        jnp.zeros((head_count, own_rows), jnp.float32),
        jnp.zeros((head_count, own_rows, HD), jnp.float32),
    )
    softmax_state = attend_block(
        softmax_state,
        query_heads,
        prompt_kv[0].reshape(own_rows, head_count, HD),
        prompt_kv[1].reshape(own_rows, head_count, HD),
        own_mask,
    )
    shard_piece = lax.all_gather(kv_pool, "blk", axis=1, tiled=True)
    key_count = shard_piece.shape[1]
    page_ids = jnp.arange(key_count, dtype=jnp.int32) // PAGE
    page_used = jnp.any((row_pages[None, :] == page_ids[:, None]) & live_slots[None, :], axis=1)
    key_mask = jnp.broadcast_to(page_used[None, :], (own_rows, key_count))
    running_max, row_total, weighted = attend_block(
        softmax_state,
        query_heads,
        shard_piece[0].reshape(key_count, head_count, HD),
        shard_piece[1].reshape(key_count, head_count, HD),
        key_mask,
    )
    mixed = weighted / row_total[:, :, None]
    mixed = jnp.where((row_index < length)[None, :, None], mixed, 0.0)
    mixed = jnp.transpose(mixed, (1, 0, 2)).reshape(own_rows, head_width).astype(jnp.bfloat16)
    return (server_q, mixed)


def solution(mesh):
    in_specs = (
        P("dp", ("blk", "mp")),
        P(("mp", "blk"), "dp"),
        P(None, ("dp", "blk"), "mp"),
        P(None, ("dp", "blk"), "mp"),
        P(("dp", "blk"), None),
        P(("dp", "blk")),
        P(("dp", "blk")),
    )
    out_specs = (P("mp", "blk"), P(("dp", "blk"), "mp"))
    return jax.shard_map(body, mesh=mesh, in_specs=in_specs, out_specs=out_specs, check_vma=False)
```

profile of v0, /device:TPU:0, one launch (start us, length us, event | category | flops | bytes accessed | tf_op | source)
XLA Modules:
  0.0 360.0 jit_solution(6316403513609587615)
XLA Ops:
  7.2 0.0 all-gather.4.cloned.1.call-start
  7.2 3.2 convert_element_type.18
  10.4 0.0 all-gather.4.cloned.1.call-update
  10.5 0.0 all-gather.6.cloned.1.call-start
  10.5 0.7 all-gather.6.cloned.1.call-update
  11.2 0.0 all-gather.8.cloned.1.call-start
  11.3 49.2 %all-gather.4.cloned.1.call-done = bf16[448,7168]{1,0:T(8,128)(2,1)} async-done(((bf16[448,1792]{1,0:T(8,128)(2,1)}), bf16[448,7168]{1,0:T(8,128)(2,1)}) %all-gather.4.cloned.1.call-update) | async-done | bytes 6422544 | tf_op jit(solution)/shard_map/all_gather | solution.py:30
  60.4 3.2 copy.52
  63.7 76.0 %all_to_all.38 = bf16[448,2,3584]{2,0,1:T(8,128)(2,1)} all-to-all(bf16[448,2,3584]{2,0,1:T(8,128)(2,1)S(1)} %bitcast.68), channel_id=1, replica_groups=mesh['dp'=4,'blk'=2,'mp'=4] {'blk'}, dimensions={1} | all-to-all | bytes 12845056 | tf_op jit(solution)/shard_map/all_to_all | solution.py:31
  139.6 0.0 copy-start.1
  139.7 0.0 all-gather.8.cloned.1.call-update
  139.7 0.0 copy-start
  139.7 0.0 all-gather.6.cloned.1.call-done
  139.7 0.0 copy-start.2
  139.7 5.5 %all-to-all-start.1 = ((bf16[2,256,3584]{2,1,0:T(8,128)(2,1)}), bf16[2,256,3584]{2,1,0:T(8,128)(2,1)}, u32[]{:S(2)}, u32[]{:S(2)}) async-start(bf16[2,256,3584]{2,1,0:T(8,128)(2,1)} %bitcast.72), calls=%async_computation.1 | async-start | bytes 7340032 | tf_op jit(solution)/shard_map/all_to_all | solution.py:35
  146.6 0.0 copy-done.1
  146.6 91.7 %all_gather.15 = bf16[2,256,896]{2,1,0:T(8,128)(2,1)S(1)} all-gather(bf16[2,128,896]{2,1,0:T(8,128)(2,1)S(1)} %copy-done.1), channel_id=1, replica_groups=mesh['dp'=4,'blk'=2,'mp'=4] {'blk'}, dimensions={1}, use_global_device_ids=true | all-gather | bytes 1376256 | tf_op jit(solution)/shard_map/all_gather | solution.py:62
  238.3 0.1 fusion.29
  238.4 0.2 copy.45
  238.6 0.2 copy.44
  238.9 0.0 copy-done
  238.9 0.1 fusion.30
  238.9 0.2 copy.41
  239.2 0.2 copy.42
  239.4 0.0 copy-done.2
  239.4 0.1 and_reduce_fusion
  239.5 0.1 fusion.20
  239.6 0.0 all-to-all-done.1
  239.6 5.9 %copy.39 = bf16[256,2,3584]{0,2,1:T(8,128)(2,1)} copy(bf16[256,2,3584]{2,0,1:T(8,128)(2,1)} %bitcast.4) | data formatting | bytes 7340032 | tf_op jit(solution)/shard_map/all_to_all | solution.py:35
  245.6 89.0 %all-gather.8.cloned.1.call-done = bf16[896,7168]{1,0:T(8,128)(2,1)} async-done(((bf16[896,3584]{1,0:T(8,128)(2,1)}), bf16[896,7168]{1,0:T(8,128)(2,1)}) %all-gather.8.cloned.1.call-update) | async-done | bytes 12845072 | tf_op jit(solution)/shard_map/all_gather | solution.py:39
  334.5 9.8 %convolution_convert_fusion = bf16[256,896]{1,0:T(8,128)(2,1)S(1)} fusion(bf16[256,7168]{0,1:T(8,128)(2,1)} %bitcast.73, bf16[896,7168]{1,0:T(8,128)(2,1)} %all-gather.8.cloned.1.call-done), kind=kOutput, calls=%fused_computation.12 | convolution fusion | flops 3288563712 | bytes 16973824 | tf_op jit(solution)/shard_map/td,hd->th/dot_general | solution.py:36
  344.3 0.2 copy.40
  344.5 0.4 fusion.31
  344.9 0.4 fusion.32
  345.3 0.4 fusion.8
  345.8 0.4 fusion.6
  346.1 0.4 fusion.7
  346.5 1.0 copy.47
  347.5 6.0 %copy.56 = bf16[896,3584]{1,0:T(8,128)(2,1)} copy(bf16[896,3584]{1,0:T(8,128)(2,1)} %bitcast.67) | data formatting | bytes 12845056
  (5 shorter events, 0.0 us)
Async XLA Ops:
  7.2 53.3 %all-gather.4.cloned.1.call-start = ((), (), s32[]{:S(2)}) async-start(), calls=%async_computation.2 | async-start | bytes 8028160 | tf_op jit(solution)/shard_map/all_gather | solution.py:30
  10.5 129.3 %all-gather.6.cloned.1.call-start = ((), (), s32[]{:S(2)}) async-start(), calls=%async_computation.3 | async-start | bytes 4587520 | tf_op jit(solution)/shard_map/all_gather | solution.py:32
  11.2 323.3 %all-gather.8.cloned.1.call-start = ((), (), s32[]{:S(2)}) async-start(), calls=%async_computation.4 | async-start | bytes 19267584 | tf_op jit(solution)/shard_map/all_gather | solution.py:39
  139.6 6.9 %copy-start.1 = (bf16[2,128,896]{2,1,0:T(8,128)(2,1)S(1)}, bf16[2,128,896]{2,1,0:T(8,128)(2,1)}, u32[]{:S(2)}) copy-start(bf16[2,128,896]{2,1,0:T(8,128)(2,1)} %param.9) | copy-start | bytes 1376260
  139.7 99.2 %copy-start = (bf16[2,256,896]{2,1,0:T(8,128)(2,1)S(1)}, bf16[2,256,896]{2,1,0:T(8,128)(2,1)}, u32[]{:S(2)}) copy-start(bf16[2,256,896]{2,1,0:T(8,128)(2,1)} %param.10) | copy-start | bytes 2752516
  139.7 99.7 %copy-start.2 = (s32[1,8]{1,0:T(1,128)S(1)}, s32[1,8]{1,0:T(1,128)}, u32[]{:S(2)}) copy-start(s32[1,8]{1,0:T(1,128)} %param.11) | copy-start | bytes 100
  139.7 99.9 %all-to-all-start.1 = ((bf16[2,256,3584]{2,1,0:T(8,128)(2,1)}), bf16[2,256,3584]{2,1,0:T(8,128)(2,1)}, u32[]{:S(2)}, u32[]{:S(2)}) async-start(bf16[2,256,3584]{2,1,0:T(8,128)(2,1)} %bitcast.72), calls=%async_computation.1 | async-start | bytes 7340032 | tf_op jit(solution)/shard_map/all_to_all | solution.py:35
Sparse Core Ops, SparseCore 0:
  10.6 49.8 all-gather.3
  62.0 72.1 all-gather.5
  139.8 194.6 all-gather.7
where the time goes:
time: 360 us
  blocking collectives  168 us (47%)
  waiting for transfers between devices  139 us (39%)
  local copies, waits for them, and re-layouts  17.4 us (5%)
  between operations  15.2 us (4%)
  matrix products  11.3 us (3%)
  starting transfers between devices  5.66 us (2%)
  other arithmetic  3.86 us (1%)
    all_gather x1, blocking collectives, body(): shard_piece = lax.all_gather(kv_pool, 'blk', axis=1, tiled=True)  91.7 us
    all_gather x1, waiting for transfers between devices, body(): lax.all_gather(server_q, 'blk', axis=1, tiled=True)  89 us
    all_to_all x1, blocking collectives, body(): lax.all_to_all(trainer_rows, 'blk', split_axis=1, concat_axis=0, tiled=True)  76 us
    all_gather x1, waiting for transfers between devices, body(): lax.all_gather(trainer_q.astype(jnp.bfloat16), 'dp', axis=1, tiled=True)  49.2 us
    dot_general x1, matrix products, body(): jnp.einsum('td,hd->th', token_local, lax.all_gather(server_q, 'blk', axis...  9.78 us
  transfers between devices with their start and end apart: 4, of which 2 were waited for; matrix products, arithmetic and copies ran while one was open for 3% of the time, Pallas kernels for 0%

commit v1 on v0

--- a/solution.py
+++ b/solution.py
@@ -1,10 +1,18 @@
+import functools
+
 import jax
 import jax.numpy as jnp
 from jax import lax
+from jax.experimental import pallas as pl
+from jax.experimental.pallas import tpu as pltpu
 from jax.sharding import PartitionSpec as P
 
 HD = 224
 PAGE = 16
+AXES = ("dp", "blk", "mp")
+BF16 = jnp.bfloat16
+F32 = jnp.float32
+NT = (((1,), (1,)), ((), ()))
 
 
 def attend_block(softmax_state, query_heads, key_heads, value_heads, key_mask):
@@ -77,6 +85,282 @@
     return (server_q, mixed)
 
 
+def pairs(move):
+    def number(pair, core, blk, mp):
+        return ((pair * 2 + core) * 2 + blk) * 4 + mp
+
+    found = []
+    for pair in range(2):
+        for core in range(2):
+            for blk in range(2):
+                for mp in range(4):
+                    target = move(pair, core, blk, mp)
+                    if target is not None:
+                        found.append((number(pair, core, blk, mp), number(*target)))
+    return found
+
+
+RING = {(0, 0): (1, 0), (1, 0): (1, 1), (1, 1): (0, 1), (0, 1): (0, 0)}
+RING_MOVE = pairs(lambda p, c, b, m: (RING[p, b][0], c, RING[p, b][1], m))
+CROSS_MOVE = pairs(lambda p, c, b, m: (p, c, b, m) if p == b else (b, c, p, m))
+CORE_MOVE = pairs(lambda p, c, b, m: (p, 1 - c, b, m))
+BLK_MOVE = pairs(lambda p, c, b, m: (p, c, 1 - b, m))
+PAIR_MOVE = pairs(lambda p, c, b, m: (p, c, b, m ^ 1))
+MID_MOVE = pairs(lambda p, c, b, m: (p, c, b, 3 - m) if m in (1, 2) else None)
+END_MOVE = pairs(lambda p, c, b, m: (p, c, b, m ^ 1) if m in (1, 2) else None)
+
+
+def place_kernel(where_ref, ring, cross, ring_other, cross_other, out, sems):
+    rows, cols = ring.shape
+    core, ring_half = where_ref[0], where_ref[1]
+    copies = []
+    for at, (piece, half, side) in enumerate(
+        (
+            (ring, ring_half, core),
+            (cross, 1 - ring_half, core),
+            (ring_other, ring_half, 1 - core),
+            (cross_other, 1 - ring_half, 1 - core),
+        )
+    ):
+        target = out.at[
+            pl.ds(pl.multiple_of(half * rows, rows), rows),
+            pl.ds(pl.multiple_of(side * cols, cols), cols),
+        ]
+        copies.append(pltpu.make_async_copy(piece, target, sems.at[at]))
+    for copy in copies:
+        copy.start()
+    for copy in copies:
+        copy.wait()
+
+
+def place(where, ring, cross, ring_other, cross_other):
+    rows, cols = ring.shape
+    any_space = pl.BlockSpec(memory_space=pl.ANY)
+    return pl.pallas_call(
+        place_kernel,
+        out_shape=jax.ShapeDtypeStruct((2 * rows, 2 * cols), BF16),
+        in_specs=[pl.BlockSpec(memory_space=pltpu.SMEM)] + [any_space] * 4,
+        out_specs=any_space,
+        scratch_shapes=[pltpu.SemaphoreType.DMA((4,))],
+        cost_estimate=pl.CostEstimate(
+            flops=0, bytes_accessed=16 * rows * cols, transcendentals=0
+        ),
+    )(where, ring, cross, ring_other, cross_other)
+
+
+def query_kernel(count, final, which, weights, *refs):
+    step = pl.program_id(0)
+    pieces, rest = refs[: 2 * count], list(refs[2 * count :])
+    total = rest.pop()
+    before = rest.pop(0) if len(rest) > (2 if final else 1) else None
+
+    @pl.when(step == 0)
+    def _():
+        total[...] = jnp.zeros_like(total) if before is None else before[...]
+
+    for at in range(count):
+        for choice in range(2):
+
+            @pl.when((step == at) & (which[count + at] == choice))
+            def _(at=at, choice=choice):
+                total[...] += lax.dot_general(
+                    pieces[2 * at + choice][...], weights[...], NT, preferred_element_type=F32
+                )
+
+    @pl.when(step == count - 1)
+    def _():
+        if final:
+            own, send = rest
+            half = own.shape[0]
+            blk = which[2 * count]
+            own[...] = total[pl.ds(pl.multiple_of(blk * half, half), half), :]
+            send[...] = total[
+                pl.ds(pl.multiple_of((1 - blk) * half, half), half), :
+            ].astype(BF16)
+        else:
+            rest[0][...] = total[...]
+
+
+def query_part(which, weights, pieces, before=None, final=True):
+    count = len(pieces)
+    rows, depth = pieces[0][0].shape
+    heads = weights.shape[0]
+    flat = [ref for pair in pieces for ref in pair]
+    whole = pl.BlockSpec((rows, depth), lambda k, which: (0, 0))
+    wide = pl.BlockSpec((rows, heads), lambda k, which: (0, 0))
+    in_specs = [pl.BlockSpec((heads, depth), lambda k, which: (0, which[k]))]
+    in_specs += [whole] * len(flat)
+    operands = [weights] + flat
+    if before is not None:
+        in_specs.append(wide)
+        operands.append(before)
+    if final:
+        half = pl.BlockSpec((rows // 2, heads), lambda k, which: (0, 0))
+        out_specs = [half, half]
+        out_shape = [
+            jax.ShapeDtypeStruct((rows // 2, heads), F32),
+            jax.ShapeDtypeStruct((rows // 2, heads), BF16),
+        ]
+    else:
+        out_specs = wide
+        out_shape = jax.ShapeDtypeStruct((rows, heads), F32)
+    return pl.pallas_call(
+        functools.partial(query_kernel, count, final),
+        grid_spec=pltpu.PrefetchScalarGridSpec(
+            num_scalar_prefetch=1,
+            grid=(count,),
+            in_specs=in_specs,
+            out_specs=out_specs,
+            scratch_shapes=[pltpu.VMEM((rows, heads), F32)],
+        ),
+        out_shape=out_shape,
+        compiler_params=pltpu.CompilerParams(vmem_limit_bytes=40 * 1024 * 1024),
+        cost_estimate=pl.CostEstimate(
+            flops=2 * count * rows * depth * heads,
+            bytes_accessed=2 * count * (rows + heads) * depth,
+            transcendentals=0,
+        ),
+    )(which, *operands)
+
+
+def attend_kernel(first_row, facts, table, own_q, other_q, prompt, pool_own, pool_other, out, mixed):
+    rows, width = out.shape
+    heads = width // HD
+    length, page_total, blk = facts[0], facts[1], facts[2]
+    query = (own_q[...] + other_q[...].astype(F32)).astype(BF16)
+    lanes = lax.broadcasted_iota(jnp.int32, (1, width), 1)
+
+    keys_seen = min(prompt.shape[1], -(-(first_row + rows) // 128) * 128)
+    row_at = first_row + lax.broadcasted_iota(jnp.int32, (rows, keys_seen), 0)
+    key_at = lax.broadcasted_iota(jnp.int32, (rows, keys_seen), 1)
+    prompt_bias = jnp.where((key_at <= row_at) & (key_at < length), 0.0, -1e30)
+
+    pool_keys = pool_own.shape[1]
+
+    def pool_bias(side):
+        page = side * (pool_keys // PAGE) + (
+            lax.broadcasted_iota(jnp.int32, (1, pool_keys), 1) // PAGE
+        )
+        used = jnp.zeros((1, pool_keys), jnp.int32)
+        for slot in range(table.shape[1]):
+            hit = (page == table[0, slot]) & (slot < page_total)
+            used = jnp.where(hit, 1, used)
+        return jnp.where(used > 0, 0.0, -1e30)
+
+    parts = (
+        (prompt, keys_seen, prompt_bias),
+        (pool_own, pool_keys, pool_bias(blk)),
+        (pool_other, pool_keys, pool_bias(1 - blk)),
+    )
+    live = first_row + lax.broadcasted_iota(jnp.int32, (rows, 1), 0) < length
+    for head in range(heads):
+        low = head * HD // 128 * 128
+        high = min(width, -(-(head + 1) * HD // 128) * 128)
+        mine = (lanes >= head * HD) & (lanes < (head + 1) * HD)
+        head_q = jnp.where(mine, query, 0)[:, low:high]
+        scores = []
+        for ref, keys, bias in parts:
+            raw = lax.dot_general(
+                head_q, ref[0, :keys, low:high], NT, preferred_element_type=F32
+            )
+            scores.append(jnp.where(bias < 0, -1e30, raw * HD**-0.5))
+        largest = functools.reduce(
+            jnp.maximum, [jnp.max(s, axis=1, keepdims=True) for s in scores]
+        )
+        total = 0.0
+        value = 0.0
+        for (ref, keys, _), score in zip(parts, scores):
+            weights = jnp.exp(score - largest)
+            total = total + jnp.sum(weights, axis=1, keepdims=True)
+            value = value + lax.dot_general(
+                weights.astype(BF16),
+                ref[1, :keys, low:high],
+                (((1,), (0,)), ((), ())),
+                preferred_element_type=F32,
+            )
+        value = jnp.where(live, value / total, 0.0)
+        mixed[:, low:high] = jnp.where(mine[:, low:high], value, mixed[:, low:high])
+    out[...] = mixed[...].astype(BF16)
+
+
+def attend(first_row, facts, table, own_q, other_q, prompt, pool_own, pool_other):
+    rows, width = own_q.shape
+    smem = pl.BlockSpec(memory_space=pltpu.SMEM)
+    vmem = pl.BlockSpec(memory_space=pltpu.VMEM)
+    return pl.pallas_call(
+        functools.partial(attend_kernel, first_row),
+        out_shape=jax.ShapeDtypeStruct((rows, width), BF16),
+        in_specs=[smem, smem] + [vmem] * 5,
+        out_specs=vmem,
+        scratch_shapes=[pltpu.VMEM((rows, width), F32)],
+        compiler_params=pltpu.CompilerParams(vmem_limit_bytes=40 * 1024 * 1024),
+        cost_estimate=pl.CostEstimate(
+            flops=4 * rows * 512 * width, bytes_accessed=8 * 512 * width, transcendentals=rows * 2048
+        ),
+    )(facts, table, own_q, other_q, prompt, pool_own, pool_other)
+
+
+def square_body(tokens, trainer_q, kv_pool, prompt_kv, page_table, page_count, prompt_len):
+    chunks = 2
+    dp, blk, mp = (lax.axis_index(name) for name in AXES)
+    send = functools.partial(lax.ppermute, axis_name=AXES)
+    middle = ((mp == 1) | (mp == 2)).astype(jnp.int32)
+    low = (mp < 2).astype(jnp.int32)
+    zero = jnp.zeros((), jnp.int32)
+
+    rows = tokens.shape[0]
+    by_request = tokens.reshape(2, chunks, rows // (2 * chunks), tokens.shape[1])
+    own = [by_request[:, c].reshape(rows // chunks, -1) for c in range(chunks)]
+    near = [send(piece, perm=PAIR_MOVE) for piece in own]
+    mid_own = [send(piece, perm=MID_MOVE) for piece in own]
+    end_own = [send(piece, perm=END_MOVE) for piece in mid_own]
+    mid_near = [send(piece, perm=MID_MOVE) for piece in near]
+    end_near = [send(piece, perm=END_MOVE) for piece in mid_near]
+
+    own_w = trainer_q.astype(BF16)
+    ring = send(own_w, perm=RING_MOVE)
+    cross = send(own_w, perm=CROSS_MOVE)
+    ring_other = send(ring, perm=CORE_MOVE)
+    cross_other = send(cross, perm=CORE_MOVE)
+    where = jnp.stack([dp % 2, 1 - dp // 2]).astype(jnp.int32)
+    server_q = place(where, ring, cross, ring_other, cross_other)
+
+    pool, _ = lax.optimization_barrier((kv_pool, ring))
+    pool_other = send(pool, perm=BLK_MOVE)
+
+    third = jnp.where(low == 1, 2, 1)
+    last = jnp.where(low == 1, 3, 0)
+    blocks = (mp, mp ^ 1, third, last)
+    picks = (zero, zero, 1 - middle, 1 - middle)
+
+    def which(ids):
+        return jnp.stack(
+            [blocks[i] for i in ids] + [picks[i] for i in ids] + [blk]
+        ).astype(jnp.int32)
+
+    facts = jnp.stack([prompt_len[0], page_count[0], blk]).astype(jnp.int32)
+    outs = []
+    for c in range(chunks):
+        pieces = (
+            (own[c], own[c]),
+            (near[c], near[c]),
+            (mid_own[c], end_own[c]),
+            (mid_near[c], end_near[c]),
+        )
+        if c < chunks - 1:
+            own_q, send_q = query_part(which((0, 1, 2, 3)), server_q, pieces)
+        else:
+            early = query_part(which((0, 1, 2)), server_q, pieces[:3], final=False)
+            own_q, send_q = query_part(which((3,)), server_q, pieces[3:], before=early)
+        other_q = send(send_q, perm=BLK_MOVE)
+        outs.append(
+            attend(
+                c * own_q.shape[0], facts, page_table, own_q, other_q, prompt_kv, kv_pool, pool_other
+            )
+        )
+    return (server_q, jnp.concatenate(outs, axis=0))
+
+
 def solution(mesh):
     in_specs = (
         P("dp", ("blk", "mp")),
@@ -88,4 +372,11 @@
         P(("dp", "blk")),
     )
     out_specs = (P("mp", "blk"), P(("dp", "blk"), "mp"))
-    return jax.shard_map(body, mesh=mesh, in_specs=in_specs, out_specs=out_specs, check_vma=False)
+    square = dict(mesh.shape) == {"dp": 4, "blk": 2, "mp": 4}
+    return jax.shard_map(
+        square_body if square else body,
+        mesh=mesh,
+        in_specs=in_specs,
+        out_specs=out_specs,
+        check_vma=False,
+    )

time: 360 us -> 320 us (0.89)
  the two profiles are of different devices: /device:TPU:0 before, /device:TPU:10 now
where the time goes in v1:
time: 320 us; the launch traced here: 319 us
  Pallas kernels  214 us (67%)
  waiting for transfers between devices  67.2 us (21%)
  starting transfers between devices  29.5 us (9%)
  other arithmetic  3.69 us (1%)
    pallas_call x1, Pallas kernels, place(): pl.pallas_call(place_kernel, out_shape=jax.ShapeDtypeStruct((2 * rows, 2...  196 us
    ppermute x1, waiting for transfers between devices, square_body(): ring = send(own_w, perm=RING_MOVE)  33 us
    ppermute x2, waiting for transfers between devices, square_body(): mid_near = [send(piece, perm=MID_MOVE) for piece in near]  14 us
    pallas_call x3, Pallas kernels, query_part(): pl.pallas_call(functools.partial(query_kernel, count, final), grid_spec=p...  13 us
    ppermute x2, waiting for transfers between devices, square_body(): near = [send(piece, perm=PAIR_MOVE) for piece in own]  11.2 us
    ppermute x2, starting transfers between devices, square_body(): mid_own = [send(piece, perm=MID_MOVE) for piece in own]  8.07 us
  transfers between devices with their start and end apart: 17, of which 8 were waited for; matrix products, arithmetic and copies ran while one was open for 0% of the time, Pallas kernels for 66%

profile of v1, /device:TPU:10, one launch (start us, length us, event | category | flops | bytes accessed | tf_op | source)
XLA Modules:
  0.0 319.4 jit_solution(10905976997998047751)
XLA Ops:
  0.6 2.1 convert_element_type.9
  2.8 0.0 copy-start.2
  2.8 1.6 collective-permute-start
  4.4 2.4 collective-permute-start.1
  6.8 33.0 %collective-permute-done.ring = bf16[448,1792]{1,0:T(8,128)(2,1)} collective-permute-done((bf16[448,1792]{1,0:T(8,128)(2,1)S(1)}, bf16[448,1792]{1,0:T(8,128)(2,1)}, u32[]{:S(2)}, u32[]{:S(2)}) %collective-permute-start) | collective-permute-done | bytes 1605664 | tf_op jit(solution)/shard_map/ppermute | solution.py:321
  39.8 0.0 collective-permute-start.2
  39.8 4.0 %collective-permute-done.1.cross = bf16[448,1792]{1,0:T(8,128)(2,1)} collective-permute-done((bf16[448,1792]{1,0:T(8,128)(2,1)S(1)}, bf16[448,1792]{1,0:T(8,128)(2,1)}, u32[]{:S(2)}, u32[]{:S(2)}) %collective-permute-start.1) | collective-permute-done | bytes 1605664 | tf_op jit(solution)/shard_map/ppermute | solution.py:322
  43.8 0.0 collective-permute-start.3
  43.8 0.1 fusion
  43.9 0.5 collective-permute-start.4
  44.4 4.6 %collective-permute-start.5 = (bf16[256,896]{1,0:T(8,128)(2,1)S(1)}, bf16[256,896]{1,0:T(8,128)(2,1)}, u32[]{:S(2)}, u32[]{:S(2)}) collective-permute-start(bf16[256,896]{1,0:T(8,128)(2,1)S(1)} %bitcast.20), channel_id=1, source_target_pairs={{1,2},{2,1},{5,6},{6,5},{9,10},{10,9},{13,14},{14,13},{17,18},{18,... | collective-permute-start | bytes 1376264 | tf_op jit(solution)/shard_map/ppermute | solution.py:315
  49.0 0.1 collective-permute-start.11
  49.1 8.2 %collective-permute-done.4.refs_2_.refs_3_ = bf16[256,896]{1,0:T(8,128)(2,1)S(1)} collective-permute-done((bf16[256,896]{1,0:T(8,128)(2,1)S(1)}, bf16[256,896]{1,0:T(8,128)(2,1)S(1)}, u32[]{:S(2)}, u32[]{:S(2)}) %collective-permute-start.4) | collective-permute-done | bytes 458784 | tf_op jit(solution)/shard_map/ppermute | solution.py:314
  57.3 3.5 %collective-permute-start.14 = (bf16[256,896]{1,0:T(8,128)(2,1)S(1)}, bf16[256,896]{1,0:T(8,128)(2,1)S(1)}, u32[]{:S(2)}, u32[]{:S(2)}) collective-permute-start(bf16[256,896]{1,0:T(8,128)(2,1)S(1)} %bitcast.16), channel_id=1, source_target_pairs={{1,2},{2,1},{5,6},{6,5},{9,10},{10,9},{13,14},{14,13},{17,18},{18,... | collective-permute-start | bytes 1376264 | tf_op jit(solution)/shard_map/ppermute | solution.py:315
  60.8 0.0 collective-permute-done.5.refs_4_
  60.8 2.9 collective-permute-start.7
  63.7 3.1 collective-permute-done.11.refs_2_.refs_3_
  66.7 3.5 %collective-permute-start.12 = (bf16[256,896]{1,0:T(8,128)(2,1)S(1)}, bf16[256,896]{1,0:T(8,128)(2,1)}, u32[]{:S(2)}, u32[]{:S(2)}) collective-permute-start(bf16[256,896]{1,0:T(8,128)(2,1)S(1)} %collective-permute-done.11.refs_2_.refs_3_), channel_id=1, source_target_pairs={{1,2},{2,1},{5,6},{6,5},{9,10},{10,9},{13,14},{14,13},{17,18},{18,... | collective-permute-start | bytes 1376264 | tf_op jit(solution)/shard_map/ppermute | solution.py:317
  70.2 2.4 collective-permute-done.14.refs_4_
  72.6 2.1 collective-permute-start.6
  74.7 7.8 %collective-permute-done.7.refs_6_ = bf16[256,896]{1,0:T(8,128)(2,1)} collective-permute-done((bf16[256,896]{1,0:T(8,128)(2,1)S(1)}, bf16[256,896]{1,0:T(8,128)(2,1)}, u32[]{:S(2)}, u32[]{:S(2)}) %collective-permute-start.7) | collective-permute-done | bytes 458784 | tf_op jit(solution)/shard_map/ppermute | solution.py:317
  82.6 2.1 collective-permute-start.8
  84.6 6.2 %collective-permute-done.12.refs_0_ = bf16[256,896]{1,0:T(8,128)(2,1)} collective-permute-done((bf16[256,896]{1,0:T(8,128)(2,1)S(1)}, bf16[256,896]{1,0:T(8,128)(2,1)}, u32[]{:S(2)}, u32[]{:S(2)}) %collective-permute-start.12) | collective-permute-done | bytes 458784 | tf_op jit(solution)/shard_map/ppermute | solution.py:317
  90.8 2.1 collective-permute-start.15
  92.9 0.1 stack.61.which
  93.0 0.1 stack.59.which
  93.1 0.0 collective-permute-done.2.ring_other
  93.1 2.1 collective-permute-start.13
  95.2 0.1 add_add_fusion.1.which
  95.2 0.6 pad_add_fusion.where_ref
  95.8 0.0 collective-permute-done.3.cross_other
  95.8 0.0 collective-permute-start.10
  95.8 196.4 %shard_map.86.weights = bf16[896,3584]{1,0:T(8,128)(2,1)} custom-call(s32[2]{0:T(128)} %pad_add_fusion.where_ref, bf16[448,1792]{1,0:T(8,128)(2,1)} %collective-permute-done.ring, bf16[448,1792]{1,0:T(8,128)(2,1)} %collective-permute-done.1.cross, bf16[448,1792]{1,0:T(8,128)(2,1)} %collective-permute-done.2.ring_other, ...), custom_call_target="tpu_custom_call" | custom-call | bytes 12845056 | tf_op jit(solution)/shard_map/pallas_call | solution.py:139
  292.2 0.0 collective-permute-done.6.refs_5_
  292.2 0.0 copy-start
  292.2 2.8 copy-done
  295.1 5.9 %shard_map.87 = (f32[128,896]{1,0:T(8,128)S(1)}, bf16[128,896]{1,0:T(8,128)(2,1)S(1)}) custom-call(s32[9]{0:T(128)S(1)} %stack.59.which, bf16[896,3584]{1,0:T(8,128)(2,1)S(1)} %copy-done, bf16[256,896]{1,0:T(8,128)(2,1)S(1)} %bitcast.21, bf16[256,896]{1,0:T(8,128)(2,1)S(1)} %bitcast.22, bf16[256,896]{1,0:T(8,128)(2,1)S(1)} %collective-permute-done.4.refs_2_.refs_3_, ...), custom_call_target="tpu_custom_call" | custom-call | flops 1644167168 | bytes 8257536 | tf_op jit(solution)/shard_map/pallas_call | solution.py:207
  300.9 2.1 collective-permute-start.9
  303.0 4.4 %shard_map.89.refs_2_ = f32[256,896]{1,0:T(8,128)S(1)} custom-call(s32[7]{0:T(128)S(1)} %stack.61.which, bf16[896,3584]{1,0:T(8,128)(2,1)S(1)} %copy-done, bf16[256,896]{1,0:T(8,128)(2,1)S(1)} %bitcast.17, bf16[256,896]{1,0:T(8,128)(2,1)S(1)} %bitcast.18, bf16[256,896]{1,0:T(8,128)(2,1)S(1)} %collective-permute-done.11.refs_2_.refs_3_, ...), custom_call_target="tpu_custom_call" | custom-call | flops 1233125376 | bytes 6193152 | tf_op jit(solution)/shard_map/pallas_call | solution.py:207
  307.4 0.0 copy-start.1
  307.4 0.0 copy-start.3
  307.4 2.8 shard_map.90
  310.2 0.1 collective-permute-start.16
  311.6 0.1 add_add_fusion.facts
  311.7 2.2 shard_map.88
  313.9 2.4 collective-permute-done.16.other_q
  316.3 2.3 shard_map.91
  318.6 0.8 pad_maximum_fusion
  (11 shorter events, 0.0 us)
Async XLA Ops:
  0.6 43.2 %copy-start.4 = (bf16[512,896]{1,0:T(8,128)(2,1)S(1)}, bf16[512,896]{1,0:T(8,128)(2,1)}, u32[]{:S(2)}) copy-start(bf16[512,896]{1,0:T(8,128)(2,1)} %param.7) | copy-start | bytes 2752516
  2.8 93.0 %copy-start.2 = (bf16[2,128,896]{2,1,0:T(8,128)(2,1)S(1)}, bf16[2,128,896]{2,1,0:T(8,128)(2,1)}, u32[]{:S(2)}) copy-start(bf16[2,128,896]{2,1,0:T(8,128)(2,1)} %pool_own.3) | copy-start | bytes 1376260
  2.8 37.0 %collective-permute-start = (bf16[448,1792]{1,0:T(8,128)(2,1)S(1)}, bf16[448,1792]{1,0:T(8,128)(2,1)}, u32[]{:S(2)}, u32[]{:S(2)}) collective-permute-start(bf16[448,1792]{1,0:T(8,128)(2,1)S(1)} %convert_element_type.9), channel_id=1, source_target_pairs={{0,16},{1,17},{2,18},{3,19},{4,0},{5,1},{6,2},{7,3},{8,24},{9,25},... | collective-permute-start | bytes 4816904 | tf_op jit(solution)/shard_map/ppermute | solution.py:321
  4.4 39.4 %collective-permute-start.1 = (bf16[448,1792]{1,0:T(8,128)(2,1)S(1)}, bf16[448,1792]{1,0:T(8,128)(2,1)}, u32[]{:S(2)}, u32[]{:S(2)}) collective-permute-start(bf16[448,1792]{1,0:T(8,128)(2,1)S(1)} %convert_element_type.9), channel_id=1, source_target_pairs={{0,0},{1,1},{2,2},{3,3},{4,16},{5,17},{6,18},{7,19},{8,8},{9,9},{1... | collective-permute-start | bytes 4816904 | tf_op jit(solution)/shard_map/ppermute | solution.py:322
  39.8 53.3 %collective-permute-start.2 = (bf16[448,1792]{1,0:T(8,128)(2,1)}, bf16[448,1792]{1,0:T(8,128)(2,1)}, u32[]{:S(2)}, u32[]{:S(2)}) collective-permute-start(bf16[448,1792]{1,0:T(8,128)(2,1)} %collective-permute-done.ring), channel_id=1, source_target_pairs={{0,8},{1,9},{2,10},{3,11},{4,12},{5,13},{6,14},{7,15},{8,0},{9,1},... | collective-permute-start | bytes 4816904 | tf_op jit(solution)/shard_map/ppermute | solution.py:323
  43.8 52.0 %collective-permute-start.3 = (bf16[448,1792]{1,0:T(8,128)(2,1)}, bf16[448,1792]{1,0:T(8,128)(2,1)}, u32[]{:S(2)}, u32[]{:S(2)}) collective-permute-start(bf16[448,1792]{1,0:T(8,128)(2,1)} %collective-permute-done.1.cross), channel_id=1, source_target_pairs={{0,8},{1,9},{2,10},{3,11},{4,12},{5,13},{6,14},{7,15},{8,0},{9,1},... | collective-permute-start | bytes 4816904 | tf_op jit(solution)/shard_map/ppermute | solution.py:324
  43.9 13.4 %collective-permute-start.4 = (bf16[256,896]{1,0:T(8,128)(2,1)S(1)}, bf16[256,896]{1,0:T(8,128)(2,1)S(1)}, u32[]{:S(2)}, u32[]{:S(2)}) collective-permute-start(bf16[256,896]{1,0:T(8,128)(2,1)S(1)} %bitcast.19), channel_id=1, source_target_pairs={{0,1},{1,0},{2,3},{3,2},{4,5},{5,4},{6,7},{7,6},{8,9},{9,8},{10,11... | collective-permute-start | bytes 1376264 | tf_op jit(solution)/shard_map/ppermute | solution.py:314
  44.4 16.3 %collective-permute-start.5 = (bf16[256,896]{1,0:T(8,128)(2,1)S(1)}, bf16[256,896]{1,0:T(8,128)(2,1)}, u32[]{:S(2)}, u32[]{:S(2)}) collective-permute-start(bf16[256,896]{1,0:T(8,128)(2,1)S(1)} %bitcast.20), channel_id=1, source_target_pairs={{1,2},{2,1},{5,6},{6,5},{9,10},{10,9},{13,14},{14,13},{17,18},{18,... | collective-permute-start | bytes 1376264 | tf_op jit(solution)/shard_map/ppermute | solution.py:315
  49.0 17.7 %collective-permute-start.11 = (bf16[256,896]{1,0:T(8,128)(2,1)S(1)}, bf16[256,896]{1,0:T(8,128)(2,1)S(1)}, u32[]{:S(2)}, u32[]{:S(2)}) collective-permute-start(bf16[256,896]{1,0:T(8,128)(2,1)S(1)} %bitcast.15), channel_id=1, source_target_pairs={{0,1},{1,0},{2,3},{3,2},{4,5},{5,4},{6,7},{7,6},{8,9},{9,8},{10,11... | collective-permute-start | bytes 1376264 | tf_op jit(solution)/shard_map/ppermute | solution.py:314
  57.3 15.3 %collective-permute-start.14 = (bf16[256,896]{1,0:T(8,128)(2,1)S(1)}, bf16[256,896]{1,0:T(8,128)(2,1)S(1)}, u32[]{:S(2)}, u32[]{:S(2)}) collective-permute-start(bf16[256,896]{1,0:T(8,128)(2,1)S(1)} %bitcast.16), channel_id=1, source_target_pairs={{1,2},{2,1},{5,6},{6,5},{9,10},{10,9},{13,14},{14,13},{17,18},{18,... | collective-permute-start | bytes 1376264 | tf_op jit(solution)/shard_map/ppermute | solution.py:315
  60.8 21.8 %collective-permute-start.7 = (bf16[256,896]{1,0:T(8,128)(2,1)S(1)}, bf16[256,896]{1,0:T(8,128)(2,1)}, u32[]{:S(2)}, u32[]{:S(2)}) collective-permute-start(bf16[256,896]{1,0:T(8,128)(2,1)S(1)} %collective-permute-done.4.refs_2_.refs_3_), channel_id=1, source_target_pairs={{1,2},{2,1},{5,6},{6,5},{9,10},{10,9},{13,14},{14,13},{17,18},{18,... | collective-permute-start | bytes 1376264 | tf_op jit(solution)/shard_map/ppermute | solution.py:317
  66.7 24.1 %collective-permute-start.12 = (bf16[256,896]{1,0:T(8,128)(2,1)S(1)}, bf16[256,896]{1,0:T(8,128)(2,1)}, u32[]{:S(2)}, u32[]{:S(2)}) collective-permute-start(bf16[256,896]{1,0:T(8,128)(2,1)S(1)} %collective-permute-done.11.refs_2_.refs_3_), channel_id=1, source_target_pairs={{1,2},{2,1},{5,6},{6,5},{9,10},{10,9},{13,14},{14,13},{17,18},{18,... | collective-permute-start | bytes 1376264 | tf_op jit(solution)/shard_map/ppermute | solution.py:317
  72.6 219.6 %collective-permute-start.6 = (bf16[256,896]{1,0:T(8,128)(2,1)}, bf16[256,896]{1,0:T(8,128)(2,1)}, u32[]{:S(2)}, u32[]{:S(2)}) collective-permute-start(bf16[256,896]{1,0:T(8,128)(2,1)} %collective-permute-done.5.refs_4_), channel_id=1, source_target_pairs={{1,0},{2,3},{5,4},{6,7},{9,8},{10,11},{13,12},{14,15},{17,16},{18,... | collective-permute-start | bytes 1376264 | tf_op jit(solution)/shard_map/ppermute | solution.py:316
  82.6 209.7 %collective-permute-start.8 = (bf16[256,896]{1,0:T(8,128)(2,1)}, bf16[256,896]{1,0:T(8,128)(2,1)}, u32[]{:S(2)}, u32[]{:S(2)}) collective-permute-start(bf16[256,896]{1,0:T(8,128)(2,1)} %collective-permute-done.7.refs_6_), channel_id=1, source_target_pairs={{1,0},{2,3},{5,4},{6,7},{9,8},{10,11},{13,12},{14,15},{17,16},{18,... | collective-permute-start | bytes 1376264 | tf_op jit(solution)/shard_map/ppermute | solution.py:318
  90.8 212.2 %collective-permute-start.15 = (bf16[256,896]{1,0:T(8,128)(2,1)S(1)}, bf16[256,896]{1,0:T(8,128)(2,1)}, u32[]{:S(2)}, u32[]{:S(2)}) collective-permute-start(bf16[256,896]{1,0:T(8,128)(2,1)S(1)} %collective-permute-done.14.refs_4_), channel_id=1, source_target_pairs={{1,0},{2,3},{5,4},{6,7},{9,8},{10,11},{13,12},{14,15},{17,16},{18,... | collective-permute-start | bytes 1376264 | tf_op jit(solution)/shard_map/ppermute | solution.py:316
  93.1 214.3 %collective-permute-start.13 = (bf16[256,896]{1,0:T(8,128)(2,1)}, bf16[256,896]{1,0:T(8,128)(2,1)}, u32[]{:S(2)}, u32[]{:S(2)}) collective-permute-start(bf16[256,896]{1,0:T(8,128)(2,1)} %collective-permute-done.12.refs_0_), channel_id=1, source_target_pairs={{1,0},{2,3},{5,4},{6,7},{9,8},{10,11},{13,12},{14,15},{17,16},{18,... | collective-permute-start | bytes 1376264 | tf_op jit(solution)/shard_map/ppermute | solution.py:318
  95.8 215.8 %collective-permute-start.10 = (bf16[2,128,896]{2,1,0:T(8,128)(2,1)S(1)}, bf16[2,128,896]{2,1,0:T(8,128)(2,1)S(1)}, u32[]{:S(2)}, u32[]{:S(2)}) collective-permute-start(bf16[2,128,896]{2,1,0:T(8,128)(2,1)S(1)} %copy-done.2), channel_id=1, source_target_pairs={{0,4},{1,5},{2,6},{3,7},{4,0},{5,1},{6,2},{7,3},{8,12},{9,13},{10,... | collective-permute-start | bytes 1376264 | tf_op jit(solution)/shard_map/ppermute | solution.py:329
  292.2 2.8 copy-start
  300.9 10.8 %collective-permute-start.9 = (bf16[128,896]{1,0:T(8,128)(2,1)S(1)}, bf16[128,896]{1,0:T(8,128)(2,1)S(1)}, u32[]{:S(2)}, u32[]{:S(2)}) collective-permute-start(bf16[128,896]{1,0:T(8,128)(2,1)S(1)} %get-tuple-element.8), channel_id=1, source_target_pairs={{0,4},{1,5},{2,6},{3,7},{4,0},{5,1},{6,2},{7,3},{8,12},{9,13},{10,... | collective-permute-start | bytes 688136 | tf_op jit(solution)/shard_map/ppermute | solution.py:355
  307.4 4.3 %copy-start.1 = (bf16[2,256,896]{2,1,0:T(8,128)(2,1)S(1)}, bf16[2,256,896]{2,1,0:T(8,128)(2,1)}, u32[]{:S(2)}) copy-start(bf16[2,256,896]{2,1,0:T(8,128)(2,1)} %prompt.3) | copy-start | bytes 2752516
  307.4 4.3 %copy-start.3 = (s32[1,8]{1,0:T(1,128)S(1)}, s32[1,8]{1,0:T(1,128)}, u32[]{:S(2)}) copy-start(s32[1,8]{1,0:T(1,128)} %table.3) | copy-start | bytes 100
  310.2 6.1 %collective-permute-start.16 = (bf16[128,896]{1,0:T(8,128)(2,1)S(1)}, bf16[128,896]{1,0:T(8,128)(2,1)S(1)}, u32[]{:S(2)}, u32[]{:S(2)}) collective-permute-start(bf16[128,896]{1,0:T(8,128)(2,1)S(1)} %get-tuple-element.11), channel_id=1, source_target_pairs={{0,4},{1,5},{2,6},{3,7},{4,0},{5,1},{6,2},{7,3},{8,12},{9,13},{10,... | collective-permute-start | bytes 688136 | tf_op jit(solution)/shard_map/ppermute | solution.py:355

commit v2 on v0

--- a/solution.py
+++ b/solution.py
@@ -1,10 +1,18 @@
+import functools
+
 import jax
 import jax.numpy as jnp
 from jax import lax
+from jax.experimental import pallas as pl
+from jax.experimental.pallas import tpu as pltpu
 from jax.sharding import PartitionSpec as P
 
 HD = 224
 PAGE = 16
+AXES = ("dp", "blk", "mp")
+BF16 = jnp.bfloat16
+F32 = jnp.float32
+NT = (((1,), (1,)), ((), ()))
 
 
 def attend_block(softmax_state, query_heads, key_heads, value_heads, key_mask):
@@ -77,6 +85,326 @@
     return (server_q, mixed)
 
 
+def pairs(move):
+    def number(pair, core, blk, mp):
+        return ((pair * 2 + core) * 2 + blk) * 4 + mp
+
+    found = []
+    for pair in range(2):
+        for core in range(2):
+            for blk in range(2):
+                for mp in range(4):
+                    target = move(pair, core, blk, mp)
+                    if target is not None:
+                        found.append((number(pair, core, blk, mp), number(*target)))
+    return found
+
+
+RING = {(0, 0): (1, 0), (1, 0): (1, 1), (1, 1): (0, 1), (0, 1): (0, 0)}
+RING_MOVE = pairs(lambda p, c, b, m: (RING[p, b][0], c, RING[p, b][1], m))
+CROSS_MOVE = pairs(lambda p, c, b, m: (p, c, b, m) if p == b else (b, c, p, m))
+CORE_MOVE = pairs(lambda p, c, b, m: (p, 1 - c, b, m))
+BLK_MOVE = pairs(lambda p, c, b, m: (p, c, 1 - b, m))
+PAIR_MOVE = pairs(lambda p, c, b, m: (p, c, b, m ^ 1))
+MID_MOVE = pairs(lambda p, c, b, m: (p, c, b, 3 - m) if m in (1, 2) else None)
+END_MOVE = pairs(lambda p, c, b, m: (p, c, b, m ^ 1) if m in (1, 2) else None)
+
+
+def query_kernel(facts, *refs):
+    wide, sides = refs[:4], (refs[4:6], refs[6:8])
+    total, last_w, server_q, held_t, held_w, got_t, got_w, put_w = refs[8:]
+    middle, ring_half = facts[1], facts[2]
+    rows, depth = sides[0][0].shape[0], held_w.shape[2]
+
+    def fetch_t(k, source):
+        return pltpu.make_async_copy(wide[k + source], held_t.at[k], got_t.at[k])
+
+    def fetch_w(k, side, source):
+        part = ring_half if source == 0 else 1 - ring_half
+        return pltpu.make_async_copy(
+            sides[side][source].at[
+                :, pl.ds(pl.multiple_of(facts[5 + 3 * k] * depth, 128), depth)
+            ],
+            held_w.at[k, pl.ds(pl.multiple_of(part * rows, 16), rows)],
+            got_w.at[k, source],
+        )
+
+    def store_w(k):
+        return pltpu.make_async_copy(
+            held_w.at[k],
+            server_q.at[:, pl.ds(pl.multiple_of(facts[3 + 3 * k] * depth, 128), depth)],
+            put_w.at[k],
+        )
+
+    for k in range(4):
+        for side in range(2):
+
+            @pl.when(facts[4 + 3 * k] == side)
+            def _(k=k, side=side):
+                for source in range(2):
+                    fetch_w(k, side, source).start()
+
+        if k < 2:
+            fetch_t(k, 0).start()
+        elif k == 2:
+            for source in range(2):
+
+                @pl.when(middle == 1 - source)
+                def _(k=k, source=source):
+                    fetch_t(k, source).start()
+
+    for k in range(4):
+        for source in range(2):
+            fetch_w(k, 0, source).wait()
+        store_w(k).start()
+        if k == 3:
+            last_w[...] = held_w[k]
+        else:
+            fetch_t(k, 0).wait()
+            part = lax.dot_general(held_t[k], held_w[k], NT, preferred_element_type=F32)
+            if k == 0:
+                total[...] = part
+            else:
+                total[...] += part
+    for k in range(4):
+        store_w(k).wait()
+
+
+def query_part(facts, wide, sides):
+    rows, depth = wide[0].shape
+    heads = 2 * sides[0].shape[0]
+    vmem = pl.BlockSpec(memory_space=pltpu.VMEM)
+    anywhere = pl.BlockSpec(memory_space=pl.ANY)
+    return pl.pallas_call(
+        query_kernel,
+        out_shape=(
+            jax.ShapeDtypeStruct((rows, heads), F32),
+            jax.ShapeDtypeStruct((heads, depth), BF16),
+            jax.ShapeDtypeStruct((heads, 4 * depth), BF16),
+        ),
+        in_specs=[pl.BlockSpec(memory_space=pltpu.SMEM)] + [anywhere] * 8,
+        out_specs=(vmem, vmem, anywhere),
+        scratch_shapes=[
+            pltpu.VMEM((3, rows, depth), BF16),
+            pltpu.VMEM((4, heads, depth), BF16),
+            pltpu.SemaphoreType.DMA((3,)),
+            pltpu.SemaphoreType.DMA((4, 2)),
+            pltpu.SemaphoreType.DMA((4,)),
+        ],
+        compiler_params=pltpu.CompilerParams(vmem_limit_bytes=40 * 1024 * 1024),
+        cost_estimate=pl.CostEstimate(
+            flops=2 * 3 * rows * depth * heads,
+            bytes_accessed=2 * 4 * (rows + 2 * heads) * depth,
+            transcendentals=0,
+        ),
+    )(facts, *wide, *sides)
+
+
+def last_kernel(chunk, facts, mid_piece, end_piece, so_far, weights, own, send, held_t, held_s, got):
+    middle, blk = facts[1], facts[0]
+    half = own.shape[0]
+    for source, piece in enumerate((mid_piece, end_piece)):
+
+        @pl.when(middle == 1 - source)
+        def _(piece=piece):
+            pltpu.make_async_copy(piece, held_t, got.at[0]).start()
+
+    sums = [
+        pltpu.make_async_copy(
+            so_far.at[pl.ds((2 * request + chunk) * half, half)],
+            held_s.at[request],
+            got.at[1 + request],
+        )
+        for request in range(2)
+    ]
+    for copy in sums:
+        copy.start()
+    pltpu.make_async_copy(mid_piece, held_t, got.at[0]).wait()
+    part = lax.dot_general(held_t[...], weights[...], NT, preferred_element_type=F32)
+    for copy in sums:
+        copy.wait()
+    upper, lower = held_s[0] + part[:half], held_s[1] + part[half:]
+
+    @pl.when(blk == 0)
+    def _():
+        own[...] = upper
+        send[...] = lower.astype(BF16)
+
+    @pl.when(blk == 1)
+    def _():
+        own[...] = lower
+        send[...] = upper.astype(BF16)
+
+
+def query_last(chunk, facts, mid_piece, end_piece, so_far, weights):
+    rows, depth = mid_piece.shape
+    heads = weights.shape[0]
+    vmem = pl.BlockSpec(memory_space=pltpu.VMEM)
+    anywhere = pl.BlockSpec(memory_space=pl.ANY)
+    return pl.pallas_call(
+        functools.partial(last_kernel, chunk),
+        out_shape=(
+            jax.ShapeDtypeStruct((rows // 2, heads), F32),
+            jax.ShapeDtypeStruct((rows // 2, heads), BF16),
+        ),
+        in_specs=[pl.BlockSpec(memory_space=pltpu.SMEM)] + [anywhere] * 3 + [vmem],
+        out_specs=(vmem,) * 2,
+        scratch_shapes=[
+            pltpu.VMEM((rows, depth), BF16),
+            pltpu.VMEM((2, rows // 2, heads), F32),
+            pltpu.SemaphoreType.DMA((3,)),
+        ],
+        compiler_params=pltpu.CompilerParams(vmem_limit_bytes=40 * 1024 * 1024),
+        cost_estimate=pl.CostEstimate(
+            flops=2 * rows * depth * heads,
+            bytes_accessed=2 * (2 * rows + heads) * depth,
+            transcendentals=0,
+        ),
+    )(facts, mid_piece, end_piece, so_far, weights)
+
+
+def attend_kernel(first_row, facts, table, own_q, other_q, prompt, pool_own, pool_other, *refs):
+    out, mixed = refs[-2:]
+    rows, width = out.shape
+    heads = width // HD
+    length, page_total, blk = facts[0], facts[1], facts[2]
+    query = (own_q[...] + other_q[...].astype(F32)).astype(BF16)
+    lanes = lax.broadcasted_iota(jnp.int32, (1, width), 1)
+
+    keys_seen = min(prompt.shape[1], -(-(first_row + rows) // 128) * 128)
+    row_at = first_row + lax.broadcasted_iota(jnp.int32, (rows, keys_seen), 0)
+    key_at = lax.broadcasted_iota(jnp.int32, (rows, keys_seen), 1)
+    prompt_bias = jnp.where((key_at <= row_at) & (key_at < length), 0.0, -1e30)
+
+    pool_keys = pool_own.shape[1]
+
+    def pool_bias(side):
+        page = side * (pool_keys // PAGE) + (
+            lax.broadcasted_iota(jnp.int32, (1, pool_keys), 1) // PAGE
+        )
+        used = jnp.zeros((1, pool_keys), jnp.int32)
+        for slot in range(table.shape[1]):
+            hit = (page == table[0, slot]) & (slot < page_total)
+            used = jnp.where(hit, 1, used)
+        return jnp.where(used > 0, 0.0, -1e30)
+
+    parts = (
+        (prompt, keys_seen, prompt_bias),
+        (pool_own, pool_keys, pool_bias(blk)),
+        (pool_other, pool_keys, pool_bias(1 - blk)),
+    )
+    live = first_row + lax.broadcasted_iota(jnp.int32, (rows, 1), 0) < length
+    for head in range(heads):
+        low = head * HD // 128 * 128
+        high = min(width, -(-(head + 1) * HD // 128) * 128)
+        mine = (lanes >= head * HD) & (lanes < (head + 1) * HD)
+        head_q = jnp.where(mine, query, 0)[:, low:high]
+        scores = []
+        for ref, keys, bias in parts:
+            raw = lax.dot_general(
+                head_q, ref[0, :keys, low:high], NT, preferred_element_type=F32
+            )
+            scores.append(jnp.where(bias < 0, -1e30, raw * HD**-0.5))
+        largest = functools.reduce(
+            jnp.maximum, [jnp.max(s, axis=1, keepdims=True) for s in scores]
+        )
+        total = 0.0
+        value = 0.0
+        for (ref, keys, _), score in zip(parts, scores):
+            weights = jnp.exp(score - largest)
+            total = total + jnp.sum(weights, axis=1, keepdims=True)
+            value = value + lax.dot_general(
+                weights.astype(BF16),
+                ref[1, :keys, low:high],
+                (((1,), (0,)), ((), ())),
+                preferred_element_type=F32,
+            )
+        value = jnp.where(live, value / total, 0.0)
+        mixed[:, low:high] = jnp.where(mine[:, low:high], value, mixed[:, low:high])
+    out[...] = mixed[...].astype(BF16)
+
+
+def attend(first_row, facts, table, own_q, other_q, prompt, pool_own, pool_other, before=None):
+    rows, width = own_q.shape
+    all_rows = prompt.shape[1]
+    smem = pl.BlockSpec(memory_space=pltpu.SMEM)
+    vmem = pl.BlockSpec(memory_space=pltpu.VMEM)
+    in_specs = [smem, smem] + [vmem] * 5
+    operands = [facts, table, own_q, other_q, prompt, pool_own, pool_other]
+    if before is not None:
+        in_specs.append(pl.BlockSpec(memory_space=pl.ANY))
+        operands.append(before)
+    return pl.pallas_call(
+        functools.partial(attend_kernel, first_row),
+        grid=(1,),
+        out_shape=jax.ShapeDtypeStruct((all_rows, width), BF16),
+        in_specs=in_specs,
+        out_specs=pl.BlockSpec((rows, width), lambda i: (first_row // rows, 0)),
+        scratch_shapes=[pltpu.VMEM((rows, width), F32)],
+        input_output_aliases={} if before is None else {7: 0},
+        compiler_params=pltpu.CompilerParams(vmem_limit_bytes=40 * 1024 * 1024),
+        cost_estimate=pl.CostEstimate(
+            flops=4 * rows * 512 * width, bytes_accessed=8 * 512 * width, transcendentals=rows * 2048
+        ),
+    )(*operands)
+
+
+def square_body(tokens, trainer_q, kv_pool, prompt_kv, page_table, page_count, prompt_len):
+    dp, blk, mp = (lax.axis_index(name) for name in AXES)
+    core, ring_half = dp % 2, 1 - dp // 2
+    send = functools.partial(lax.ppermute, axis_name=AXES)
+
+    near = send(tokens, perm=PAIR_MOVE)
+    mid_own = send(tokens, perm=MID_MOVE)
+    end_own = send(mid_own, perm=END_MOVE)
+    by_request = near.reshape(2, 2, near.shape[0] // 4, near.shape[1])
+    mid_near = [
+        send(by_request[:, c].reshape(-1, near.shape[1]), perm=MID_MOVE) for c in range(2)
+    ]
+    end_near = [send(piece, perm=END_MOVE) for piece in mid_near]
+
+    own_w = trainer_q.astype(BF16)
+    ring = send(own_w, perm=RING_MOVE)
+    cross = send(own_w, perm=CROSS_MOVE)
+    ring, cross, pool, _ = lax.optimization_barrier(
+        (ring, cross, kv_pool, (end_own, mid_near[0]))
+    )
+    ring_other = send(ring, perm=CORE_MOVE)
+    cross_other = send(cross, perm=CORE_MOVE)
+    pool_other = send(pool, perm=BLK_MOVE)
+
+    third = jnp.where(mp < 2, 2, 1)
+    last = jnp.where(mp < 2, 3, 0)
+    middle = (mp == 1) | (mp == 2)
+    facts = [blk, middle, ring_half]
+    for place_at in (mp, mp ^ 1, third, last):
+        facts += [place_at, place_at // 2 != core, place_at % 2]
+    facts = jnp.stack([jnp.asarray(f, jnp.int32) for f in facts])
+    so_far, last_w, server_q = query_part(
+        facts, (tokens, near, mid_own, end_own), (ring, cross, ring_other, cross_other)
+    )
+    own_q, send_q = zip(
+        *(query_last(c, facts, mid_near[c], end_near[c], so_far, last_w) for c in range(2))
+    )
+    other_q = [send(piece, perm=BLK_MOVE) for piece in send_q]
+
+    live = jnp.stack([prompt_len[0], page_count[0], blk]).astype(jnp.int32)
+    out = None
+    for c in range(2):
+        out = attend(
+            c * own_q[c].shape[0],
+            live,
+            page_table,
+            own_q[c],
+            other_q[c],
+            prompt_kv,
+            kv_pool,
+            pool_other,
+            out,
+        )
+    return (server_q, out)
+
+
 def solution(mesh):
     in_specs = (
         P("dp", ("blk", "mp")),
@@ -88,4 +416,11 @@
         P(("dp", "blk")),
     )
     out_specs = (P("mp", "blk"), P(("dp", "blk"), "mp"))
-    return jax.shard_map(body, mesh=mesh, in_specs=in_specs, out_specs=out_specs, check_vma=False)
+    square = dict(mesh.shape) == {"dp": 4, "blk": 2, "mp": 4}
+    return jax.shard_map(
+        square_body if square else body,
+        mesh=mesh,
+        in_specs=in_specs,
+        out_specs=out_specs,
+        check_vma=False,
+    )

time: 360 us -> 93.4 us (0.26)
  the two profiles are of different devices: /device:TPU:0 before, /device:TPU:8 now
where the time goes in v2:
time: 93.4 us; the launch traced here: 92.9 us
  waiting for transfers between devices  41 us (44%)
  starting transfers between devices  25.5 us (27%)
  Pallas kernels  17.5 us (19%)
  local copies, waits for them, and re-layouts  4.67 us (5%)
  other arithmetic  2.15 us (2%)
  between operations  2.06 us (2%)
    ppermute x2, waiting for transfers between devices, square_body(): send(by_request[:, c].reshape(-1, near.shape[1]), perm=MID_MOVE)  17.6 us
    ppermute x1, waiting for transfers between devices, square_body(): mid_own = send(tokens, perm=MID_MOVE)  15.2 us
    ppermute x2, starting transfers between devices, square_body(): send(by_request[:, c].reshape(-1, near.shape[1]), perm=MID_MOVE)  6.94 us
    pallas_call x1, Pallas kernels, query_part(): pl.pallas_call(query_kernel, out_shape=(jax.ShapeDtypeStruct((rows, heads...  6.9 us
    pallas_call x2, Pallas kernels, attend(): pl.pallas_call(functools.partial(attend_kernel, first_row), grid=(1,), ou...  5.86 us
    ppermute x2, starting transfers between devices, square_body(): end_near = [send(piece, perm=END_MOVE) for piece in mid_near]  5.18 us
    pallas_call x2, Pallas kernels, query_last(): pl.pallas_call(functools.partial(last_kernel, chunk), out_shape=(jax.Shap...  4.72 us
    unnamed x16, local copies, waits for them, and re-layouts  4.5 us
  transfers between devices with their start and end apart: 14, of which 6 were waited for; matrix products, arithmetic and copies ran while one was open for 2% of the time, Pallas kernels for 16%

profile of v2, /device:TPU:8, one launch (start us, length us, event | category | flops | bytes accessed | tf_op | source)
XLA Modules:
  0.0 92.9 jit_solution(15097083997319027496)
XLA Ops:
  0.6 3.5 %collective-permute-start.1 = (bf16[512,896]{1,0:T(8,128)(2,1)}, bf16[512,896]{1,0:T(8,128)(2,1)S(1)}, u32[]{:S(2)}, u32[]{:S(2)}) collective-permute-start(bf16[512,896]{1,0:T(8,128)(2,1)} %refs_0_.1), channel_id=1, source_target_pairs={{1,2},{2,1},{5,6},{6,5},{9,10},{10,9},{13,14},{14,13},{17,18},{18,... | collective-permute-start | bytes 2752520 | tf_op jit(solution)/shard_map/ppermute | solution.py:358
  4.1 0.1 collective-permute-start
  4.2 2.1 %convert_element_type.2 = bf16[448,1792]{1,0:T(8,128)(2,1)S(1)} convert(f32[448,1792]{1,0:T(8,128)} %param.8) | non-fusion elementwise | flops 802816 | bytes 4816896 | tf_op jit(solution)/shard_map/convert_element_type | solution.py:366
  6.3 0.0 copy-start.1
  6.3 1.5 %collective-permute-start.3 = (bf16[448,1792]{1,0:T(8,128)(2,1)S(1)}, bf16[448,1792]{1,0:T(8,128)(2,1)S(1)}, u32[]{:S(2)}, u32[]{:S(2)}) collective-permute-start(bf16[448,1792]{1,0:T(8,128)(2,1)S(1)} %convert_element_type.2), channel_id=1, source_target_pairs={{0,16},{1,17},{2,18},{3,19},{4,0},{5,1},{6,2},{7,3},{8,24},{9,25},... | collective-permute-start | bytes 4816904 | tf_op jit(solution)/shard_map/ppermute | solution.py:367
  7.8 1.8 %collective-permute-start.4 = (bf16[448,1792]{1,0:T(8,128)(2,1)S(1)}, bf16[448,1792]{1,0:T(8,128)(2,1)}, u32[]{:S(2)}, u32[]{:S(2)}) collective-permute-start(bf16[448,1792]{1,0:T(8,128)(2,1)S(1)} %convert_element_type.2), channel_id=1, source_target_pairs={{0,0},{1,1},{2,2},{3,3},{4,16},{5,17},{6,18},{7,19},{8,8},{9,9},{1... | collective-permute-start | bytes 4816904 | tf_op jit(solution)/shard_map/ppermute | solution.py:368
  9.7 15.2 %collective-permute-done.1.refs_2_ = bf16[512,896]{1,0:T(8,128)(2,1)S(1)} collective-permute-done((bf16[512,896]{1,0:T(8,128)(2,1)}, bf16[512,896]{1,0:T(8,128)(2,1)S(1)}, u32[]{:S(2)}, u32[]{:S(2)}) %collective-permute-start.1) | collective-permute-done | bytes 917536 | tf_op jit(solution)/shard_map/ppermute | solution.py:358
  24.8 1.3 %collective-permute-start.2 = (bf16[512,896]{1,0:T(8,128)(2,1)S(1)}, bf16[512,896]{1,0:T(8,128)(2,1)S(1)}, u32[]{:S(2)}, u32[]{:S(2)}) collective-permute-start(bf16[512,896]{1,0:T(8,128)(2,1)S(1)} %collective-permute-done.1.refs_2_), channel_id=1, source_target_pairs={{1,0},{2,3},{5,4},{6,7},{9,8},{10,11},{13,12},{14,15},{17,16},{18,... | collective-permute-start | bytes 2752520 | tf_op jit(solution)/shard_map/ppermute | solution.py:359
  26.2 0.0 collective-permute-done.refs_1_
  26.2 0.1 fusion
  26.3 3.5 %collective-permute-start.5 = (bf16[256,896]{1,0:T(8,128)(2,1)S(1)}, bf16[256,896]{1,0:T(8,128)(2,1)S(1)}, u32[]{:S(2)}, u32[]{:S(2)}) collective-permute-start(bf16[256,896]{1,0:T(8,128)(2,1)S(1)} %bitcast.24), channel_id=1, source_target_pairs={{1,2},{2,1},{5,6},{6,5},{9,10},{10,9},{13,14},{14,13},{17,18},{18,... | collective-permute-start | bytes 1376264 | tf_op jit(solution)/shard_map/ppermute | solution.py:362
  29.8 9.8 %collective-permute-done.5.mid_piece = bf16[256,896]{1,0:T(8,128)(2,1)S(1)} collective-permute-done((bf16[256,896]{1,0:T(8,128)(2,1)S(1)}, bf16[256,896]{1,0:T(8,128)(2,1)S(1)}, u32[]{:S(2)}, u32[]{:S(2)}) %collective-permute-start.5) | collective-permute-done | bytes 458784 | tf_op jit(solution)/shard_map/ppermute | solution.py:362
  39.5 3.3 %collective-permute-done.3.refs_4_ = bf16[448,1792]{1,0:T(8,128)(2,1)S(1)} collective-permute-done((bf16[448,1792]{1,0:T(8,128)(2,1)S(1)}, bf16[448,1792]{1,0:T(8,128)(2,1)S(1)}, u32[]{:S(2)}, u32[]{:S(2)}) %collective-permute-start.3) | collective-permute-done | bytes 1605664 | tf_op jit(solution)/shard_map/ppermute | solution.py:367
  42.9 0.0 collective-permute-done.4.refs_5_
  42.9 0.0 copy-done.3
  42.9 2.2 %collective-permute-done.2.refs_3_ = bf16[512,896]{1,0:T(8,128)(2,1)S(1)} collective-permute-done((bf16[512,896]{1,0:T(8,128)(2,1)S(1)}, bf16[512,896]{1,0:T(8,128)(2,1)S(1)}, u32[]{:S(2)}, u32[]{:S(2)}) %collective-permute-start.2) | collective-permute-done | bytes 917536 | tf_op jit(solution)/shard_map/ppermute | solution.py:359
  45.1 0.9 %copy-done.5 = bf16[512,896]{1,0:T(8,128)(2,1)} copy-done((bf16[512,896]{1,0:T(8,128)(2,1)}, bf16[512,896]{1,0:T(8,128)(2,1)S(1)}, u32[]{:S(2)}) %copy-start.5) | copy-done | bytes 917528
  46.1 0.0 collective-permute-start.6
  46.1 0.5 collective-permute-start.7
  46.6 3.5 %collective-permute-start.8 = (bf16[256,896]{1,0:T(8,128)(2,1)S(1)}, bf16[256,896]{1,0:T(8,128)(2,1)}, u32[]{:S(2)}, u32[]{:S(2)}) collective-permute-start(bf16[256,896]{1,0:T(8,128)(2,1)S(1)} %bitcast.23), channel_id=1, source_target_pairs={{1,2},{2,1},{5,6},{6,5},{9,10},{10,9},{13,14},{14,13},{17,18},{18,... | collective-permute-start | bytes 1376264 | tf_op jit(solution)/shard_map/ppermute | solution.py:362
  50.1 3.1 %collective-permute-start.12 = (bf16[256,896]{1,0:T(8,128)(2,1)S(1)}, bf16[256,896]{1,0:T(8,128)(2,1)}, u32[]{:S(2)}, u32[]{:S(2)}) collective-permute-start(bf16[256,896]{1,0:T(8,128)(2,1)S(1)} %collective-permute-done.5.mid_piece), channel_id=1, source_target_pairs={{1,0},{2,3},{5,4},{6,7},{9,8},{10,11},{13,12},{14,15},{17,16},{18,... | collective-permute-start | bytes 1376264 | tf_op jit(solution)/shard_map/ppermute | solution.py:364
  53.2 7.8 %collective-permute-done.8.mid_piece = bf16[256,896]{1,0:T(8,128)(2,1)} collective-permute-done((bf16[256,896]{1,0:T(8,128)(2,1)S(1)}, bf16[256,896]{1,0:T(8,128)(2,1)}, u32[]{:S(2)}, u32[]{:S(2)}) %collective-permute-start.8) | collective-permute-done | bytes 458784 | tf_op jit(solution)/shard_map/ppermute | solution.py:362
  61.0 2.1 %collective-permute-start.9 = (bf16[256,896]{1,0:T(8,128)(2,1)}, bf16[256,896]{1,0:T(8,128)(2,1)}, u32[]{:S(2)}, u32[]{:S(2)}) collective-permute-start(bf16[256,896]{1,0:T(8,128)(2,1)} %collective-permute-done.8.mid_piece), channel_id=1, source_target_pairs={{1,0},{2,3},{5,4},{6,7},{9,8},{10,11},{13,12},{14,15},{17,16},{18,... | collective-permute-start | bytes 1376264 | tf_op jit(solution)/shard_map/ppermute | solution.py:364
  63.1 0.1 stack.87.facts
  63.1 0.0 copy-done.1
  63.2 2.5 %collective-permute-start.11 = (bf16[2,128,896]{2,1,0:T(8,128)(2,1)S(1)}, bf16[2,128,896]{2,1,0:T(8,128)(2,1)S(1)}, u32[]{:S(2)}, u32[]{:S(2)}) collective-permute-start(bf16[2,128,896]{2,1,0:T(8,128)(2,1)S(1)} %copy-done.1), channel_id=1, source_target_pairs={{0,4},{1,5},{2,6},{3,7},{4,0},{5,1},{6,2},{7,3},{8,12},{9,13},{10,... | collective-permute-start | bytes 1376264 | tf_op jit(solution)/shard_map/ppermute | solution.py:374
  65.6 0.0 collective-permute-done.6.refs_6_
  65.6 0.0 collective-permute-done.7.refs_7_
  65.7 1.2 %copy-done.2 = bf16[512,896]{1,0:T(8,128)(2,1)S(1)} copy-done((bf16[512,896]{1,0:T(8,128)(2,1)S(1)}, bf16[512,896]{1,0:T(8,128)(2,1)}, u32[]{:S(2)}) %copy-start.2) | copy-done | bytes 917528
  66.8 1.2 %copy-done.4 = bf16[512,896]{1,0:T(8,128)(2,1)S(1)} copy-done((bf16[512,896]{1,0:T(8,128)(2,1)S(1)}, bf16[512,896]{1,0:T(8,128)(2,1)}, u32[]{:S(2)}) %copy-start.4) | copy-done | bytes 917528
  68.0 1.2 %copy-done.6 = bf16[512,896]{1,0:T(8,128)(2,1)S(1)} copy-done((bf16[512,896]{1,0:T(8,128)(2,1)S(1)}, bf16[512,896]{1,0:T(8,128)(2,1)}, u32[]{:S(2)}) %copy-start.6) | copy-done | bytes 917528
  69.2 6.9 %shard_map.86 = (f32[512,896]{1,0:T(8,128)S(1)}, bf16[896,896]{1,0:T(8,128)(2,1)S(1)}, bf16[896,3584]{1,0:T(8,128)(2,1)}) custom-call(s32[15]{0:T(128)S(1)} %stack.87.facts, bf16[512,896]{1,0:T(8,128)(2,1)S(1)} %copy-done.2, bf16[512,896]{1,0:T(8,128)(2,1)S(1)} %collective-permute-done.refs_1_, bf16[512,896]{1,0:T(8,128)(2,1)S(1)} %copy-done.4, ...), custom_call_target="tpu_custom_call" | custom-call | flops 2466250752 | bytes 16515072 | tf_op jit(solution)/shard_map/pallas_call | solution.py:178
  76.1 0.0 collective-permute-done.12.end_piece
  76.1 2.3 %shard_map.88 = (f32[128,896]{1,0:T(8,128)S(1)}, bf16[128,896]{1,0:T(8,128)(2,1)S(1)}) custom-call(s32[15]{0:T(128)S(1)} %stack.87.facts, bf16[256,896]{1,0:T(8,128)(2,1)S(1)} %collective-permute-done.5.mid_piece, bf16[256,896]{1,0:T(8,128)(2,1)} %collective-permute-done.12.end_piece, f32[512,896]{1,0:T(8,128)S(1)} %get-tuple-element.15.so_far, ...), custom_call_target="tpu_custom_call" | custom-call | flops 411041792 | bytes 2523136 | tf_op jit(solution)/shard_map/pallas_call | solution.py:244
  78.4 0.0 copy-start
  78.4 0.0 copy-start.7
  78.4 0.1 collective-permute-start.13
  78.5 0.0 collective-permute-done.9.end_piece
  78.5 2.5 %shard_map.87 = (f32[128,896]{1,0:T(8,128)S(1)}, bf16[128,896]{1,0:T(8,128)(2,1)S(1)}) custom-call(s32[15]{0:T(128)S(1)} %stack.87.facts, bf16[256,896]{1,0:T(8,128)(2,1)} %collective-permute-done.8.mid_piece, bf16[256,896]{1,0:T(8,128)(2,1)} %collective-permute-done.9.end_piece, f32[512,896]{1,0:T(8,128)S(1)} %get-tuple-element.15.so_far, ...), custom_call_target="tpu_custom_call" | custom-call | flops 411041792 | bytes 2523136 | tf_op jit(solution)/shard_map/pallas_call | solution.py:244
  81.0 2.1 %collective-permute-start.10 = (bf16[128,896]{1,0:T(8,128)(2,1)S(1)}, bf16[128,896]{1,0:T(8,128)(2,1)S(1)}, u32[]{:S(2)}, u32[]{:S(2)}) collective-permute-start(bf16[128,896]{1,0:T(8,128)(2,1)S(1)} %get-tuple-element.18), channel_id=1, source_target_pairs={{0,4},{1,5},{2,6},{3,7},{4,0},{5,1},{6,2},{7,3},{8,12},{9,13},{10,... | collective-permute-start | bytes 688136 | tf_op jit(solution)/shard_map/ppermute | solution.py:389
  84.3 0.1 pad_add_fusion.facts
  84.4 0.0 collective-permute-done.11.pool_other
  84.4 2.6 %collective-permute-done.13.other_q = bf16[128,896]{1,0:T(8,128)(2,1)S(1)} collective-permute-done((bf16[128,896]{1,0:T(8,128)(2,1)S(1)}, bf16[128,896]{1,0:T(8,128)(2,1)S(1)}, u32[]{:S(2)}, u32[]{:S(2)}) %collective-permute-start.13) | collective-permute-done | bytes 229408 | tf_op jit(solution)/shard_map/ppermute | solution.py:389
  87.0 0.0 copy-done
  87.0 0.0 copy-done.7
  87.0 2.9 %shard_map.89.refs_0_ = bf16[256,896]{1,0:T(8,128)(2,1)} custom-call(s32[3]{0:T(128)S(1)} %pad_add_fusion.facts, s32[1,8]{1,0:T(1,128)S(1)} %copy-done.7, f32[128,896]{1,0:T(8,128)S(1)} %get-tuple-element.20.own_q, bf16[128,896]{1,0:T(8,128)(2,1)S(1)} %collective-permute-done.13.other_q, bf16[2,256,896]{2,1,0:T(8,128)(2,1)S(1)} %copy-done, ...), custom_call_target="tpu_custom_call" | custom-call | flops 234881024 | bytes 3670016 | tf_op jit(solution)/shard_map/pallas_call | solution.py:337
  89.9 0.0 collective-permute-done.10.other_q
  89.9 3.0 %shard_map.90 = bf16[256,896]{1,0:T(8,128)(2,1)} custom-call(s32[3]{0:T(128)S(1)} %pad_add_fusion.facts, s32[1,8]{1,0:T(1,128)S(1)} %copy-done.7, f32[128,896]{1,0:T(8,128)S(1)} %get-tuple-element.17.own_q, bf16[128,896]{1,0:T(8,128)(2,1)S(1)} %collective-permute-done.10.other_q, bf16[2,256,896]{2,1,0:T(8,128)(2,1)S(1)} %copy-done, ...), custom_call_target="tpu_custom_call", output_to_operand_aliasing={{}: (7, {})} | custom-call | flops 234881024 | bytes 3670016 | tf_op jit(solution)/shard_map/pallas_call | solution.py:337
  (5 shorter events, 0.0 us)
Async XLA Ops:
  0.6 24.2 %collective-permute-start.1 = (bf16[512,896]{1,0:T(8,128)(2,1)}, bf16[512,896]{1,0:T(8,128)(2,1)S(1)}, u32[]{:S(2)}, u32[]{:S(2)}) collective-permute-start(bf16[512,896]{1,0:T(8,128)(2,1)} %refs_0_.1), channel_id=1, source_target_pairs={{1,2},{2,1},{5,6},{6,5},{9,10},{10,9},{13,14},{14,13},{17,18},{18,... | collective-permute-start | bytes 2752520 | tf_op jit(solution)/shard_map/ppermute | solution.py:358
  4.1 22.1 %collective-permute-start = (bf16[512,896]{1,0:T(8,128)(2,1)}, bf16[512,896]{1,0:T(8,128)(2,1)S(1)}, u32[]{:S(2)}, u32[]{:S(2)}) collective-permute-start(bf16[512,896]{1,0:T(8,128)(2,1)} %refs_0_.1), channel_id=1, source_target_pairs={{0,1},{1,0},{2,3},{3,2},{4,5},{5,4},{6,7},{7,6},{8,9},{9,8},{10,11... | collective-permute-start | bytes 2752520 | tf_op jit(solution)/shard_map/ppermute | solution.py:357
  6.3 56.9 %copy-start.1 = (bf16[2,128,896]{2,1,0:T(8,128)(2,1)S(1)}, bf16[2,128,896]{2,1,0:T(8,128)(2,1)}, u32[]{:S(2)}) copy-start(bf16[2,128,896]{2,1,0:T(8,128)(2,1)} %pool_own.3) | copy-start | bytes 1376260
  6.3 36.6 %collective-permute-start.3 = (bf16[448,1792]{1,0:T(8,128)(2,1)S(1)}, bf16[448,1792]{1,0:T(8,128)(2,1)S(1)}, u32[]{:S(2)}, u32[]{:S(2)}) collective-permute-start(bf16[448,1792]{1,0:T(8,128)(2,1)S(1)} %convert_element_type.2), channel_id=1, source_target_pairs={{0,16},{1,17},{2,18},{3,19},{4,0},{5,1},{6,2},{7,3},{8,24},{9,25},... | collective-permute-start | bytes 4816904 | tf_op jit(solution)/shard_map/ppermute | solution.py:367
  7.8 35.1 %collective-permute-start.4 = (bf16[448,1792]{1,0:T(8,128)(2,1)S(1)}, bf16[448,1792]{1,0:T(8,128)(2,1)}, u32[]{:S(2)}, u32[]{:S(2)}) collective-permute-start(bf16[448,1792]{1,0:T(8,128)(2,1)S(1)} %convert_element_type.2), channel_id=1, source_target_pairs={{0,0},{1,1},{2,2},{3,3},{4,16},{5,17},{6,18},{7,19},{8,8},{9,9},{1... | collective-permute-start | bytes 4816904 | tf_op jit(solution)/shard_map/ppermute | solution.py:368
  24.8 18.1 %copy-start.3 = (bf16[512,896]{1,0:T(8,128)(2,1)}, bf16[512,896]{1,0:T(8,128)(2,1)S(1)}, u32[]{:S(2)}) copy-start(bf16[512,896]{1,0:T(8,128)(2,1)S(1)} %collective-permute-done.1.refs_2_) | copy-start | bytes 2752516
  24.8 20.3 %collective-permute-start.2 = (bf16[512,896]{1,0:T(8,128)(2,1)S(1)}, bf16[512,896]{1,0:T(8,128)(2,1)S(1)}, u32[]{:S(2)}, u32[]{:S(2)}) collective-permute-start(bf16[512,896]{1,0:T(8,128)(2,1)S(1)} %collective-permute-done.1.refs_2_), channel_id=1, source_target_pairs={{1,0},{2,3},{5,4},{6,7},{9,8},{10,11},{13,12},{14,15},{17,16},{18,... | collective-permute-start | bytes 2752520 | tf_op jit(solution)/shard_map/ppermute | solution.py:359
  26.3 13.3 %collective-permute-start.5 = (bf16[256,896]{1,0:T(8,128)(2,1)S(1)}, bf16[256,896]{1,0:T(8,128)(2,1)S(1)}, u32[]{:S(2)}, u32[]{:S(2)}) collective-permute-start(bf16[256,896]{1,0:T(8,128)(2,1)S(1)} %bitcast.24), channel_id=1, source_target_pairs={{1,2},{2,1},{5,6},{6,5},{9,10},{10,9},{13,14},{14,13},{17,18},{18,... | collective-permute-start | bytes 1376264 | tf_op jit(solution)/shard_map/ppermute | solution.py:362
  45.1 0.9 %copy-start.5 = (bf16[512,896]{1,0:T(8,128)(2,1)}, bf16[512,896]{1,0:T(8,128)(2,1)S(1)}, u32[]{:S(2)}) copy-start(bf16[512,896]{1,0:T(8,128)(2,1)S(1)} %collective-permute-done.2.refs_3_) | copy-start | bytes 2752516
  46.1 19.6 %collective-permute-start.6 = (bf16[448,1792]{1,0:T(8,128)(2,1)S(1)}, bf16[448,1792]{1,0:T(8,128)(2,1)}, u32[]{:S(2)}, u32[]{:S(2)}) collective-permute-start(bf16[448,1792]{1,0:T(8,128)(2,1)S(1)} %collective-permute-done.3.refs_4_), channel_id=1, source_target_pairs={{0,8},{1,9},{2,10},{3,11},{4,12},{5,13},{6,14},{7,15},{8,0},{9,1},... | collective-permute-start | bytes 4816904 | tf_op jit(solution)/shard_map/ppermute | solution.py:372
  46.1 19.6 %collective-permute-start.7 = (bf16[448,1792]{1,0:T(8,128)(2,1)}, bf16[448,1792]{1,0:T(8,128)(2,1)}, u32[]{:S(2)}, u32[]{:S(2)}) collective-permute-start(bf16[448,1792]{1,0:T(8,128)(2,1)} %collective-permute-done.4.refs_5_), channel_id=1, source_target_pairs={{0,8},{1,9},{2,10},{3,11},{4,12},{5,13},{6,14},{7,15},{8,0},{9,1},... | collective-permute-start | bytes 4816904 | tf_op jit(solution)/shard_map/ppermute | solution.py:373
  46.6 14.4 %collective-permute-start.8 = (bf16[256,896]{1,0:T(8,128)(2,1)S(1)}, bf16[256,896]{1,0:T(8,128)(2,1)}, u32[]{:S(2)}, u32[]{:S(2)}) collective-permute-start(bf16[256,896]{1,0:T(8,128)(2,1)S(1)} %bitcast.23), channel_id=1, source_target_pairs={{1,2},{2,1},{5,6},{6,5},{9,10},{10,9},{13,14},{14,13},{17,18},{18,... | collective-permute-start | bytes 1376264 | tf_op jit(solution)/shard_map/ppermute | solution.py:362
  50.1 26.0 %collective-permute-start.12 = (bf16[256,896]{1,0:T(8,128)(2,1)S(1)}, bf16[256,896]{1,0:T(8,128)(2,1)}, u32[]{:S(2)}, u32[]{:S(2)}) collective-permute-start(bf16[256,896]{1,0:T(8,128)(2,1)S(1)} %collective-permute-done.5.mid_piece), channel_id=1, source_target_pairs={{1,0},{2,3},{5,4},{6,7},{9,8},{10,11},{13,12},{14,15},{17,16},{18,... | collective-permute-start | bytes 1376264 | tf_op jit(solution)/shard_map/ppermute | solution.py:364
  61.0 17.5 %collective-permute-start.9 = (bf16[256,896]{1,0:T(8,128)(2,1)}, bf16[256,896]{1,0:T(8,128)(2,1)}, u32[]{:S(2)}, u32[]{:S(2)}) collective-permute-start(bf16[256,896]{1,0:T(8,128)(2,1)} %collective-permute-done.8.mid_piece), channel_id=1, source_target_pairs={{1,0},{2,3},{5,4},{6,7},{9,8},{10,11},{13,12},{14,15},{17,16},{18,... | collective-permute-start | bytes 1376264 | tf_op jit(solution)/shard_map/ppermute | solution.py:364
  63.2 21.3 %collective-permute-start.11 = (bf16[2,128,896]{2,1,0:T(8,128)(2,1)S(1)}, bf16[2,128,896]{2,1,0:T(8,128)(2,1)S(1)}, u32[]{:S(2)}, u32[]{:S(2)}) collective-permute-start(bf16[2,128,896]{2,1,0:T(8,128)(2,1)S(1)} %copy-done.1), channel_id=1, source_target_pairs={{0,4},{1,5},{2,6},{3,7},{4,0},{5,1},{6,2},{7,3},{8,12},{9,13},{10,... | collective-permute-start | bytes 1376264 | tf_op jit(solution)/shard_map/ppermute | solution.py:374
  65.7 1.2 %copy-start.2 = (bf16[512,896]{1,0:T(8,128)(2,1)S(1)}, bf16[512,896]{1,0:T(8,128)(2,1)}, u32[]{:S(2)}) copy-start(bf16[512,896]{1,0:T(8,128)(2,1)} %refs_0_.1) | copy-start | bytes 2752516
  66.8 1.2 %copy-start.4 = (bf16[512,896]{1,0:T(8,128)(2,1)S(1)}, bf16[512,896]{1,0:T(8,128)(2,1)}, u32[]{:S(2)}) copy-start(bf16[512,896]{1,0:T(8,128)(2,1)} %copy-done.3) | copy-start | bytes 2752516
  68.0 1.2 %copy-start.6 = (bf16[512,896]{1,0:T(8,128)(2,1)S(1)}, bf16[512,896]{1,0:T(8,128)(2,1)}, u32[]{:S(2)}) copy-start(bf16[512,896]{1,0:T(8,128)(2,1)} %copy-done.5) | copy-start | bytes 2752516
  78.4 8.6 %copy-start = (bf16[2,256,896]{2,1,0:T(8,128)(2,1)S(1)}, bf16[2,256,896]{2,1,0:T(8,128)(2,1)}, u32[]{:S(2)}) copy-start(bf16[2,256,896]{2,1,0:T(8,128)(2,1)} %prompt.3) | copy-start | bytes 2752516
  78.4 8.6 %copy-start.7 = (s32[1,8]{1,0:T(1,128)S(1)}, s32[1,8]{1,0:T(1,128)}, u32[]{:S(2)}) copy-start(s32[1,8]{1,0:T(1,128)} %table.3) | copy-start | bytes 100
  78.4 8.6 %collective-permute-start.13 = (bf16[128,896]{1,0:T(8,128)(2,1)S(1)}, bf16[128,896]{1,0:T(8,128)(2,1)S(1)}, u32[]{:S(2)}, u32[]{:S(2)}) collective-permute-start(bf16[128,896]{1,0:T(8,128)(2,1)S(1)} %get-tuple-element.21), channel_id=1, source_target_pairs={{0,4},{1,5},{2,6},{3,7},{4,0},{5,1},{6,2},{7,3},{8,12},{9,13},{10,... | collective-permute-start | bytes 688136 | tf_op jit(solution)/shard_map/ppermute | solution.py:389
  81.0 9.0 %collective-permute-start.10 = (bf16[128,896]{1,0:T(8,128)(2,1)S(1)}, bf16[128,896]{1,0:T(8,128)(2,1)S(1)}, u32[]{:S(2)}, u32[]{:S(2)}) collective-permute-start(bf16[128,896]{1,0:T(8,128)(2,1)S(1)} %get-tuple-element.18), channel_id=1, source_target_pairs={{0,4},{1,5},{2,6},{3,7},{4,0},{5,1},{6,2},{7,3},{8,12},{9,13},{10,... | collective-permute-start | bytes 688136 | tf_op jit(solution)/shard_map/ppermute | solution.py:389

commit v3 on v2

v3 whole, which is shorter than its diff:
```python
import functools

import jax
import jax.numpy as jnp
from jax import lax
from jax.experimental import pallas as pl
from jax.experimental.pallas import tpu as pltpu
from jax.sharding import PartitionSpec as P

HD = 224
PAGE = 16
W_PARTS = 1
CUT = 160
AXES = ("dp", "blk", "mp")
BF16 = jnp.bfloat16
F32 = jnp.float32
NT = (((1,), (1,)), ((), ()))


def attend_block(softmax_state, query_heads, key_heads, value_heads, key_mask):
    running_max, row_total, weighted = softmax_state
    scores = jnp.einsum(
        "thd,khd->htk", query_heads, key_heads, preferred_element_type=jnp.float32
    ) * HD ** (-0.5)
    scores = jnp.where(key_mask[None], scores, -1e30)
    new_max = jnp.maximum(running_max, jnp.max(scores, axis=2))
    weights = jnp.where(key_mask[None], jnp.exp(scores - new_max[:, :, None]), 0.0)
    factor = jnp.exp(running_max - new_max)
    row_total = row_total * factor + jnp.sum(weights, axis=2)
    weighted = weighted * factor[:, :, None] + jnp.einsum(
        "htk,khd->htd",
        weights.astype(jnp.bfloat16),
        value_heads,
        preferred_element_type=jnp.float32,
    )
    return (new_max, row_total, weighted)


def body(tokens, trainer_q, kv_pool, prompt_kv, page_table, page_count, prompt_len):
    trainer_rows = lax.all_gather(trainer_q.astype(jnp.bfloat16), "dp", axis=1, tiled=True)
    server_q = lax.all_to_all(trainer_rows, "blk", split_axis=1, concat_axis=0, tiled=True)
    features = lax.all_gather(tokens, "mp", axis=1, tiled=True)
    own_rows = features.shape[0] // lax.axis_size("blk")
    head_width = server_q.shape[0]
    token_local = lax.all_to_all(features, "blk", split_axis=0, concat_axis=1, tiled=True)
    queries = jnp.einsum(
        "td,hd->th",
        token_local,
        lax.all_gather(server_q, "blk", axis=1, tiled=True),
        preferred_element_type=jnp.float32,
    )
    queries = queries.astype(jnp.bfloat16)
    head_count = head_width // HD
    query_heads = queries.reshape(own_rows, head_count, HD)
    length = prompt_len[0]
    row_pages = page_table[0]
    live_slots = jnp.arange(row_pages.shape[0], dtype=jnp.int32) < page_count[0]
    row_index = jnp.arange(own_rows, dtype=jnp.int32)
    own_mask = (row_index[None, :] <= row_index[:, None]) & (row_index[None, :] < length)
    softmax_state = (
        jnp.full((head_count, own_rows), -1e30, jnp.float32),
        jnp.zeros((head_count, own_rows), jnp.float32),
        jnp.zeros((head_count, own_rows, HD), jnp.float32),
    )
    softmax_state = attend_block(
        softmax_state,
        query_heads,
        prompt_kv[0].reshape(own_rows, head_count, HD),
        prompt_kv[1].reshape(own_rows, head_count, HD),
        own_mask,
    )
    shard_piece = lax.all_gather(kv_pool, "blk", axis=1, tiled=True)
    key_count = shard_piece.shape[1]
    page_ids = jnp.arange(key_count, dtype=jnp.int32) // PAGE
    page_used = jnp.any((row_pages[None, :] == page_ids[:, None]) & live_slots[None, :], axis=1)
    key_mask = jnp.broadcast_to(page_used[None, :], (own_rows, key_count))
    running_max, row_total, weighted = attend_block(
        softmax_state,
        query_heads,
        shard_piece[0].reshape(key_count, head_count, HD),
        shard_piece[1].reshape(key_count, head_count, HD),
        key_mask,
    )
    mixed = weighted / row_total[:, :, None]
    mixed = jnp.where((row_index < length)[None, :, None], mixed, 0.0)
    mixed = jnp.transpose(mixed, (1, 0, 2)).reshape(own_rows, head_width).astype(jnp.bfloat16)
    return (server_q, mixed)


def pairs(move):
    def number(pair, core, blk, mp):
        return ((pair * 2 + core) * 2 + blk) * 4 + mp

    found = []
    for pair in range(2):
        for core in range(2):
            for blk in range(2):
                for mp in range(4):
                    target = move(pair, core, blk, mp)
                    if target is not None:
                        found.append((number(pair, core, blk, mp), number(*target)))
    return found


RING = {(0, 0): (1, 0), (1, 0): (1, 1), (1, 1): (0, 1), (0, 1): (0, 0)}
RING_MOVE = pairs(lambda p, c, b, m: (RING[p, b][0], c, RING[p, b][1], m))
CROSS_MOVE = pairs(lambda p, c, b, m: (p, c, b, m) if p == b else (b, c, p, m))
CORE_MOVE = pairs(lambda p, c, b, m: (p, 1 - c, b, m))
BLK_MOVE = pairs(lambda p, c, b, m: (p, c, 1 - b, m))
PAIR_MOVE = pairs(lambda p, c, b, m: (p, c, b, m ^ 1))
MID_MOVE = pairs(lambda p, c, b, m: (p, c, b, 3 - m) if m in (1, 2) else None)
END_MOVE = pairs(lambda p, c, b, m: (p, c, b, m ^ 1) if m in (1, 2) else None)


def cut_kernel(piece, *parts):
    half = piece.shape[0] // 2
    row = 0
    for part in parts:
        rows = part.shape[0] // 2
        for request in range(2):
            part[request * rows : (request + 1) * rows] = piece[
                request * half + row : request * half + row + rows
            ]
        row += rows


def cut(piece, first):
    rows, depth = piece.shape
    vmem = pl.BlockSpec(memory_space=pltpu.VMEM)
    return pl.pallas_call(
        cut_kernel,
        out_shape=(
            pltpu.VMEM((2 * first, depth), piece.dtype),
            pltpu.VMEM((rows - 2 * first, depth), piece.dtype),
        ),
        in_specs=[vmem],
        out_specs=(vmem, vmem),
        compiler_params=pltpu.CompilerParams(vmem_limit_bytes=8 * 1024 * 1024),
        cost_estimate=pl.CostEstimate(
            flops=0, bytes_accessed=4 * rows * depth, transcendentals=0
        ),
    )(piece)


def query_kernel(facts, *refs):
    wide = refs[:4]
    sides = (refs[4 : 4 + 2 * W_PARTS], refs[4 + 2 * W_PARTS : 4 + 4 * W_PARTS])
    total, last_w, server_q, held_t, held_w, got_t, got_w, put_w = refs[4 + 4 * W_PARTS + 1 :]
    middle, ring_half = facts[1], facts[2]
    rows, depth = sides[0][0].shape[0], held_w.shape[2]

    def fetch_t(k, source):
        return pltpu.make_async_copy(wide[k + source], held_t.at[k], got_t.at[k])

    def fetch_w(k, side, source):
        part = ring_half if source < W_PARTS else 1 - ring_half
        first_row = (part * W_PARTS + source % W_PARTS) * rows
        return pltpu.make_async_copy(
            sides[side][source].at[
                :, pl.ds(pl.multiple_of(facts[5 + 3 * k] * depth, 128), depth)
            ],
            held_w.at[k, pl.ds(pl.multiple_of(first_row, 16), rows)],
            got_w.at[k, source],
        )

    def store_w(k):
        return pltpu.make_async_copy(
            held_w.at[k],
            server_q.at[:, pl.ds(pl.multiple_of(facts[3 + 3 * k] * depth, 128), depth)],
            put_w.at[k],
        )

    for k in range(4):
        for side in range(2):

            @pl.when(facts[4 + 3 * k] == side)
            def _(k=k, side=side):
                for source in range(2 * W_PARTS):
                    fetch_w(k, side, source).start()

        if k < 2:
            fetch_t(k, 0).start()
        elif k == 2:
            for source in range(2):

                @pl.when(middle == 1 - source)
                def _(k=k, source=source):
                    fetch_t(k, source).start()

    for k in range(4):
        for source in range(2 * W_PARTS):
            fetch_w(k, 0, source).wait()
        store_w(k).start()
        if k == 3:
            last_w[...] = held_w[k]
        else:
            fetch_t(k, 0).wait()
            part = lax.dot_general(held_t[k], held_w[k], NT, preferred_element_type=F32)
            if k == 0:
                total[...] = part
            else:
                total[...] += part
    for k in range(4):
        store_w(k).wait()


def query_part(facts, wide, sides, token):
    rows, depth = wide[0].shape
    heads = 2 * W_PARTS * sides[0].shape[0]
    in_hbm = functools.partial(pltpu.with_memory_space_constraint, memory_space=pltpu.HBM)
    wide = [in_hbm(piece) for piece in wide]
    sides = [in_hbm(piece) for piece in sides]
    vmem = pl.BlockSpec(memory_space=pltpu.VMEM)
    anywhere = pl.BlockSpec(memory_space=pl.ANY)
    return pl.pallas_call(
        query_kernel,
        out_shape=(
            pltpu.VMEM((rows, heads), F32),
            pltpu.VMEM((heads, depth), BF16),
            jax.ShapeDtypeStruct((heads, 4 * depth), BF16),
        ),
        in_specs=[pl.BlockSpec(memory_space=pltpu.SMEM)] + [anywhere] * (4 + 4 * W_PARTS + 1),
        out_specs=(vmem, vmem, anywhere),
        scratch_shapes=[
            pltpu.VMEM((3, rows, depth), BF16),
            pltpu.VMEM((4, heads, depth), BF16),
            pltpu.SemaphoreType.DMA((3,)),
            pltpu.SemaphoreType.DMA((4, 2 * W_PARTS)),
            pltpu.SemaphoreType.DMA((4,)),
        ],
        compiler_params=pltpu.CompilerParams(vmem_limit_bytes=14 * 1024 * 1024),
        cost_estimate=pl.CostEstimate(
            flops=2 * 3 * rows * depth * heads,
            bytes_accessed=2 * 4 * (rows + 2 * heads) * depth,
            transcendentals=0,
        ),
    )(facts, *wide, *sides, *token)


def last_kernel(first_row, facts, mid_piece, end_piece, so_far, weights, own, send):
    middle, blk = facts[1], facts[0]
    half = own.shape[0]
    piece = jnp.where(middle == 1, mid_piece[...], end_piece[...])
    part = lax.dot_general(piece, weights[...], NT, preferred_element_type=F32)
    whole = so_far.shape[0] // 2
    upper = so_far[first_row : first_row + half] + part[:half]
    lower = so_far[whole + first_row : whole + first_row + half] + part[half:]

    @pl.when(blk == 0)
    def _():
        own[...] = upper
        send[...] = lower.astype(BF16)

    @pl.when(blk == 1)
    def _():
        own[...] = lower
        send[...] = upper.astype(BF16)


def query_last(first_row, facts, mid_piece, end_piece, so_far, weights):
    rows, depth = mid_piece.shape
    heads = weights.shape[0]
    vmem = pl.BlockSpec(memory_space=pltpu.VMEM)
    return pl.pallas_call(
        functools.partial(last_kernel, first_row),
        out_shape=(
            jax.ShapeDtypeStruct((rows // 2, heads), F32),
            jax.ShapeDtypeStruct((rows // 2, heads), BF16),
        ),
        in_specs=[pl.BlockSpec(memory_space=pltpu.SMEM)] + [vmem] * 4,
        out_specs=(vmem,) * 2,
        compiler_params=pltpu.CompilerParams(vmem_limit_bytes=6 * 1024 * 1024),
        cost_estimate=pl.CostEstimate(
            flops=2 * rows * depth * heads,
            bytes_accessed=2 * (2 * rows + heads) * depth,
            transcendentals=0,
        ),
    )(facts, mid_piece, end_piece, so_far, weights)


def window(head, width):
    low = head * HD // 128 * 128
    high = min(width, -(-(head + 1) * HD // 128) * 128)
    return low, high, head * HD - low


def to_front(wide, offset):
    if offset:
        wide = pltpu.roll(wide, wide.shape[1] - offset, 1)
    return wide[:, :256]


def align_kernel(prompt, pool_own, pool_other, out):
    width = prompt.shape[2]
    for kind in range(2):
        row = 0
        for ref in (pool_own, pool_other, prompt):
            rows = ref.shape[1]
            for head in range(width // HD):
                low, high, offset = window(head, width)
                wide = ref[kind, :, low:high].astype(F32)
                out[kind, head, row : row + rows] = to_front(wide, offset).astype(BF16)
            row += rows


def align(prompt, pool_own, pool_other):
    width = prompt.shape[2]
    keys = prompt.shape[1] + pool_own.shape[1] + pool_other.shape[1]
    vmem = pl.BlockSpec(memory_space=pltpu.VMEM)
    return pl.pallas_call(
        align_kernel,
        out_shape=jax.ShapeDtypeStruct((2, width // HD, keys, 256), BF16),
        in_specs=[vmem] * 3,
        out_specs=vmem,
        compiler_params=pltpu.CompilerParams(vmem_limit_bytes=12 * 1024 * 1024),
        cost_estimate=pl.CostEstimate(
            flops=0, bytes_accessed=8 * keys * width, transcendentals=0
        ),
    )(prompt, pool_own, pool_other)


def attend_kernel(first_row, pool_keys, facts, own_q, other_q, aligned, *refs):
    out, done, sem = refs[-3:]
    rows, width = done.shape
    heads = width // HD
    length, page_total, blk = facts[15], facts[16], facts[0]
    query = (own_q[...] + other_q[...].astype(F32)).astype(BF16).astype(F32)

    keys = 2 * pool_keys + first_row + rows
    key_at = lax.broadcasted_iota(jnp.int32, (1, keys), 1)
    own_side = key_at < pool_keys
    pages_here = pool_keys // PAGE
    page = jnp.where(own_side, blk, -blk) * pages_here + key_at // PAGE
    used = jnp.zeros((1, keys), jnp.int32)
    for slot in range(facts.shape[0] - 17):
        used = jnp.where((page == facts[17 + slot]) & (slot < page_total), 1, used)
    prompt_at = key_at - 2 * pool_keys
    seen_from = jnp.where(
        prompt_at >= 0,
        jnp.where(prompt_at < length, prompt_at, first_row + rows),
        jnp.where(used > 0, 0, first_row + rows),
    )
    row_at = first_row + lax.broadcasted_iota(jnp.int32, (rows, 1), 0)
    seen = seen_from <= row_at
    live = row_at < length
    lanes = lax.broadcasted_iota(jnp.int32, (1, 256), 1)

    raw = []
    for head in range(heads):
        low, high, offset = window(head, width)
        head_q = jnp.where(lanes < HD, to_front(query[:, low:high], offset), 0.0).astype(BF16)
        raw.append(
            lax.dot_general(head_q, aligned[0, head, :keys], NT, preferred_element_type=F32)
        )
    tiles = [None] * (width // 128)
    for head in range(heads):
        low, high, offset = window(head, width)
        scores = jnp.where(seen, raw[head] * HD**-0.5, -1e30)
        weights = jnp.exp(scores - jnp.max(scores, axis=1, keepdims=True))
        total = jnp.sum(weights, axis=1, keepdims=True)
        value = jnp.dot(
            weights.astype(BF16), aligned[1, head, :keys], preferred_element_type=F32
        )
        value = jnp.where(live, value * (1.0 / total), 0.0)
        if high - low > 256:
            value = jnp.concatenate([value, jnp.zeros((rows, high - low - 256), F32)], axis=1)
        if offset:
            value = pltpu.roll(value, offset, 1)
        for tile in range(low // 128, high // 128):
            part = value[:, tile * 128 - low : (tile + 1) * 128 - low]
            if tiles[tile] is None:
                tiles[tile] = part
            else:
                tiles[tile] = jnp.where(
                    lanes[:, :128] < head * HD - tile * 128, tiles[tile], part
                )
    for tile, part in enumerate(tiles):
        done[:, tile * 128 : (tile + 1) * 128] = part.astype(BF16)
    copy = pltpu.make_async_copy(done, out.at[pl.ds(first_row, rows)], sem)
    copy.start()
    copy.wait()


def attend(first_row, pool_keys, facts, own_q, other_q, aligned, before=None):
    rows, width = own_q.shape
    all_rows = aligned.shape[2] - 2 * pool_keys
    smem = pl.BlockSpec(memory_space=pltpu.SMEM)
    vmem = pl.BlockSpec(memory_space=pltpu.VMEM)
    in_specs = [smem] + [vmem] * 3
    operands = [facts, own_q, other_q, aligned]
    if before is not None:
        in_specs.append(pl.BlockSpec(memory_space=pl.ANY))
        operands.append(before)
    return pl.pallas_call(
        functools.partial(attend_kernel, first_row, pool_keys),
        out_shape=jax.ShapeDtypeStruct((all_rows, width), BF16),
        in_specs=in_specs,
        out_specs=pl.BlockSpec(memory_space=pl.ANY),
        scratch_shapes=[
            pltpu.VMEM((rows, width), BF16),
            pltpu.SemaphoreType.DMA(()),
        ],
        input_output_aliases={} if before is None else {4: 0},
        compiler_params=pltpu.CompilerParams(vmem_limit_bytes=8 * 1024 * 1024),
        cost_estimate=pl.CostEstimate(
            flops=4 * rows * 512 * width, bytes_accessed=8 * 512 * width, transcendentals=rows * 2048
        ),
    )(*operands)


def square_body(tokens, trainer_q, kv_pool, prompt_kv, page_table, page_count, prompt_len):
    dp, blk, mp = (lax.axis_index(name) for name in AXES)
    core, ring_half = dp % 2, 1 - dp // 2
    send = functools.partial(lax.ppermute, axis_name=AXES)

    near = send(tokens, perm=PAIR_MOVE)
    mid_own = send(tokens, perm=MID_MOVE)
    end_own = send(mid_own, perm=END_MOVE)
    parts = cut(near, CUT)
    mid_near = [send(parts[0], perm=MID_MOVE)]
    mid_near.append(send(parts[1], perm=MID_MOVE))
    end_near = [send(piece, perm=END_MOVE) for piece in mid_near]

    token = []
    late = []
    piece = near[:256]
    for _ in range(1):
        piece = send(piece, perm=CORE_MOVE)
    token.append(piece)
    rows = trainer_q.shape[0] // W_PARTS
    own_w = [trainer_q[p * rows : (p + 1) * rows].astype(BF16) for p in range(W_PARTS)]
    ring = [send(piece, perm=RING_MOVE) for piece in own_w]
    cross = [send(piece, perm=CROSS_MOVE) for piece in own_w]
    ring, cross, token, _ = lax.optimization_barrier((ring, cross, token, (end_own, mid_near[0], mid_near[1], )))
    pool = kv_pool
    pool, _ = lax.optimization_barrier((kv_pool, (ring,)))
    ring_other = [send(piece, perm=CORE_MOVE) for piece in ring]
    cross_other = [send(piece, perm=CORE_MOVE) for piece in cross]
    pool_other = send(pool, perm=BLK_MOVE)

    third = jnp.where(mp < 2, 2, 1)
    last = jnp.where(mp < 2, 3, 0)
    middle = (mp == 1) | (mp == 2)
    facts = [blk, middle, ring_half]
    for place_at in (mp, mp ^ 1, third, last):
        facts += [place_at, place_at // 2 != core, place_at % 2]
    facts += [prompt_len[0], page_count[0]]
    facts = jnp.stack([jnp.asarray(f, jnp.int32) for f in facts])
    facts = jnp.concatenate([facts, page_table[0]])
    so_far, last_w, server_q = query_part(
        facts, (tokens, near, mid_own, end_own), (*ring, *cross, *ring_other, *cross_other), token + late
    )
    own_q, send_q = zip(
        *(query_last(c * CUT, facts, mid_near[c], end_near[c], so_far, last_w) for c in range(2))
    )
    other_q = [send(piece, perm=BLK_MOVE) for piece in send_q]

    aligned = align(prompt_kv, kv_pool, pool_other)
    out = None
    for c in range(2):
        out = attend(
            c * CUT,
            kv_pool.shape[1],
            facts,
            own_q[c],
            other_q[c],
            aligned,
            out,
        )
    return (server_q, out)


def solution(mesh):
    in_specs = (
        P("dp", ("blk", "mp")),
        P(("mp", "blk"), "dp"),
        P(None, ("dp", "blk"), "mp"),
        P(None, ("dp", "blk"), "mp"),
        P(("dp", "blk"), None),
        P(("dp", "blk")),
        P(("dp", "blk")),
    )
    out_specs = (P("mp", "blk"), P(("dp", "blk"), "mp"))
    square = dict(mesh.shape) == {"dp": 4, "blk": 2, "mp": 4}
    return jax.shard_map(
        square_body if square else body,
        mesh=mesh,
        in_specs=in_specs,
        out_specs=out_specs,
        check_vma=False,
    )
```

time: 93.4 us -> 84.1 us (0.900)
  the two profiles are of different devices: /device:TPU:8 before, /device:TPU:0 now
where the time goes in v3:
time: 84.1 us; the launch traced here: 83.8 us
  waiting for transfers between devices  41.7 us (50%)
  starting transfers between devices  20.5 us (24%)
  Pallas kernels  16.6 us (20%)
  between operations  2.21 us (3%)
  other arithmetic  2.07 us (2%)
    ppermute x1, waiting for transfers between devices, square_body(): ring = [send(piece, perm=RING_MOVE) for piece in own_w]  14.8 us
    ppermute x1, waiting for transfers between devices, square_body(): near = send(tokens, perm=PAIR_MOVE)  13.5 us
    pallas_call x1, Pallas kernels, query_part(): pl.pallas_call(query_kernel, out_shape=(pltpu.VMEM((rows, heads), F32), p...  8.89 us
    ppermute x2, waiting for transfers between devices, square_body(): end_near = [send(piece, perm=END_MOVE) for piece in mid_near]  7.54 us
    ppermute x1, starting transfers between devices, square_body(): near = send(tokens, perm=PAIR_MOVE)  5.86 us
    pallas_call x2, Pallas kernels, attend(): pl.pallas_call(functools.partial(attend_kernel, first_row, pool_keys), ou...  4.3 us
    ppermute x2, starting transfers between devices, square_body(): other_q = [send(piece, perm=BLK_MOVE) for piece in send_q]  3.18 us
    ppermute x1, waiting for transfers between devices, square_body(): end_own = send(mid_own, perm=END_MOVE)  2.95 us
  transfers between devices with their start and end apart: 15, of which 7 were waited for; matrix products, arithmetic and copies ran while one was open for 3% of the time, Pallas kernels for 17%

profile of v3, /device:TPU:0, one launch (start us, length us, event | category | flops | bytes accessed | tf_op | source)
XLA Modules:
  0.0 83.8 jit_solution(1232066314368370256)
XLA Ops:
  0.6 0.7 collective-permute-start.1
  1.4 5.9 %collective-permute-start = (bf16[512,896]{1,0:T(8,128)(2,1)}, bf16[512,896]{1,0:T(8,128)(2,1)S(1)}, u32[]{:S(2)}, u32[]{:S(2)}) collective-permute-start(bf16[512,896]{1,0:T(8,128)(2,1)} %refs_0_.1), channel_id=1, source_target_pairs={{0,1},{1,0},{2,3},{3,2},{4,5},{5,4},{6,7},{7,6},{8,9},{9,8},{10,11... | collective-permute-start | bytes 2752520 | tf_op jit(solution)/shard_map/ppermute | solution.py:416
  7.2 2.1 %convert_element_type.2 = bf16[448,1792]{1,0:T(8,128)(2,1)S(1)} convert(f32[448,1792]{1,0:T(8,128)} %param.8) | non-fusion elementwise | flops 802816 | bytes 4816896 | tf_op jit(solution)/shard_map/convert_element_type | solution.py:431
  9.3 0.0 copy-start.5
  9.3 0.0 copy-start.2
  9.3 1.5 %collective-permute-start.3 = (bf16[448,1792]{1,0:T(8,128)(2,1)S(1)}, bf16[448,1792]{1,0:T(8,128)(2,1)}, u32[]{:S(2)}, u32[]{:S(2)}) collective-permute-start(bf16[448,1792]{1,0:T(8,128)(2,1)S(1)} %convert_element_type.2), channel_id=1, source_target_pairs={{0,16},{1,17},{2,18},{3,19},{4,0},{5,1},{6,2},{7,3},{8,24},{9,25},... | collective-permute-start | bytes 4816904 | tf_op jit(solution)/shard_map/ppermute | solution.py:432
  10.8 1.8 %collective-permute-start.4 = (bf16[448,1792]{1,0:T(8,128)(2,1)S(1)}, bf16[448,1792]{1,0:T(8,128)(2,1)}, u32[]{:S(2)}, u32[]{:S(2)}) collective-permute-start(bf16[448,1792]{1,0:T(8,128)(2,1)S(1)} %convert_element_type.2), channel_id=1, source_target_pairs={{0,0},{1,1},{2,2},{3,3},{4,16},{5,17},{6,18},{7,19},{8,8},{9,9},{1... | collective-permute-start | bytes 4816904 | tf_op jit(solution)/shard_map/ppermute | solution.py:433
  12.7 0.0 collective-permute-done.1.refs_2_
  12.7 1.3 %collective-permute-start.2 = (bf16[512,896]{1,0:T(8,128)(2,1)S(1)}, bf16[512,896]{1,0:T(8,128)(2,1)S(1)}, u32[]{:S(2)}, u32[]{:S(2)}) collective-permute-start(bf16[512,896]{1,0:T(8,128)(2,1)S(1)} %collective-permute-done.1.refs_2_), channel_id=1, source_target_pairs={{1,0},{2,3},{5,4},{6,7},{9,8},{10,11},{13,12},{14,15},{17,16},{18,... | collective-permute-start | bytes 2752520 | tf_op jit(solution)/shard_map/ppermute | solution.py:418
  13.9 13.5 %collective-permute-done.piece.refs_1_ = bf16[512,896]{1,0:T(8,128)(2,1)S(1)} collective-permute-done((bf16[512,896]{1,0:T(8,128)(2,1)}, bf16[512,896]{1,0:T(8,128)(2,1)S(1)}, u32[]{:S(2)}, u32[]{:S(2)}) %collective-permute-start) | collective-permute-done | bytes 917536 | tf_op jit(solution)/shard_map/ppermute | solution.py:416
  27.5 0.1 shard_map.86
  27.6 0.7 collective-permute-start.7
  28.3 0.7 collective-permute-start.6
  29.0 0.0 collective-permute-done.7.mid_piece
  29.0 0.1 collective-permute-start.5
  29.1 1.8 %collective-permute-done.5.refs_8_ = bf16[256,896]{1,0:T(8,128)(2,1)S(1)} collective-permute-done((bf16[256,896]{1,0:T(8,128)(2,1)S(1)}, bf16[256,896]{1,0:T(8,128)(2,1)S(1)}, u32[]{:S(2)}, u32[]{:S(2)}) %collective-permute-start.5) | collective-permute-done | bytes 458784 | tf_op jit(solution)/shard_map/ppermute | solution.py:428
  30.9 0.0 collective-permute-done.6.mid_piece
  30.9 14.8 %collective-permute-done.3.refs_4_ = bf16[448,1792]{1,0:T(8,128)(2,1)} collective-permute-done((bf16[448,1792]{1,0:T(8,128)(2,1)S(1)}, bf16[448,1792]{1,0:T(8,128)(2,1)}, u32[]{:S(2)}, u32[]{:S(2)}) %collective-permute-start.3) | collective-permute-done | bytes 1605664 | tf_op jit(solution)/shard_map/ppermute | solution.py:432
  45.7 0.0 collective-permute-done.4.refs_5_
  45.7 3.0 %collective-permute-done.2.refs_3_ = bf16[512,896]{1,0:T(8,128)(2,1)S(1)} collective-permute-done((bf16[512,896]{1,0:T(8,128)(2,1)S(1)}, bf16[512,896]{1,0:T(8,128)(2,1)S(1)}, u32[]{:S(2)}, u32[]{:S(2)}) %collective-permute-start.2) | collective-permute-done | bytes 917536 | tf_op jit(solution)/shard_map/ppermute | solution.py:418
  48.7 0.0 collective-permute-start.8
  48.7 0.0 copy-done.3
  48.7 0.5 collective-permute-start.9
  49.2 0.5 copy-done.4
  49.7 1.3 %collective-permute-start.13 = (bf16[320,896]{1,0:T(8,128)(2,1)S(1)}, bf16[320,896]{1,0:T(8,128)(2,1)S(1)}, u32[]{:S(2)}, u32[]{:S(2)}) collective-permute-start(bf16[320,896]{1,0:T(8,128)(2,1)S(1)} %collective-permute-done.6.mid_piece), channel_id=1, source_target_pairs={{1,0},{2,3},{5,4},{6,7},{9,8},{10,11},{13,12},{14,15},{17,16},{18,... | collective-permute-start | bytes 1720328 | tf_op jit(solution)/shard_map/ppermute | solution.py:422
  52.4 0.0 copy-done.5
  52.4 0.1 concatenate.3.facts
  52.5 1.3 %collective-permute-start.10 = (bf16[192,896]{1,0:T(8,128)(2,1)S(1)}, bf16[192,896]{1,0:T(8,128)(2,1)S(1)}, u32[]{:S(2)}, u32[]{:S(2)}) collective-permute-start(bf16[192,896]{1,0:T(8,128)(2,1)S(1)} %collective-permute-done.7.mid_piece), channel_id=1, source_target_pairs={{1,0},{2,3},{5,4},{6,7},{9,8},{10,11},{13,12},{14,15},{17,16},{18,... | collective-permute-start | bytes 1032200 | tf_op jit(solution)/shard_map/ppermute | solution.py:422
  53.8 0.0 copy-done.2
  53.8 1.6 %collective-permute-start.12 = (bf16[2,128,896]{2,1,0:T(8,128)(2,1)S(1)}, bf16[2,128,896]{2,1,0:T(8,128)(2,1)S(1)}, u32[]{:S(2)}, u32[]{:S(2)}) collective-permute-start(bf16[2,128,896]{2,1,0:T(8,128)(2,1)S(1)} %copy-done.2), channel_id=1, source_target_pairs={{0,4},{1,5},{2,6},{3,7},{4,0},{5,1},{6,2},{7,3},{8,12},{9,13},{10,... | collective-permute-start | bytes 1376264 | tf_op jit(solution)/shard_map/ppermute | solution.py:439
  55.5 0.0 collective-permute-done.8.refs_6_
  55.5 0.0 collective-permute-done.9.refs_7_
  55.5 0.0 copy-done
  55.5 8.9 %shard_map.87 = (f32[512,896]{1,0:T(8,128)S(1)}, bf16[896,896]{1,0:T(8,128)(2,1)S(1)}, bf16[896,3584]{1,0:T(8,128)(2,1)}) custom-call(s32[25]{0:T(128)S(1)} %concatenate.3.facts, bf16[512,896]{1,0:T(8,128)(2,1)} %refs_0_.1, bf16[512,896]{1,0:T(8,128)(2,1)} %copy-done, bf16[512,896]{1,0:T(8,128)(2,1)} %copy-done.3, bf16[512,896]{1,0:T(8,128)(2,1)} %copy-done.4, ...), custom_call_target="tpu_custom_call" | custom-call | flops 2466250752 | bytes 16515072 | tf_op jit(solution)/shard_map/pallas_call | solution.py:215
  64.4 4.3 %collective-permute-done.13.end_piece = bf16[320,896]{1,0:T(8,128)(2,1)S(1)} collective-permute-done((bf16[320,896]{1,0:T(8,128)(2,1)S(1)}, bf16[320,896]{1,0:T(8,128)(2,1)S(1)}, u32[]{:S(2)}, u32[]{:S(2)}) %collective-permute-start.13) | collective-permute-done | bytes 573472 | tf_op jit(solution)/shard_map/ppermute | solution.py:422
  68.6 1.5 %shard_map.90 = (f32[160,896]{1,0:T(8,128)S(1)}, bf16[160,896]{1,0:T(8,128)(2,1)S(1)}) custom-call(s32[25]{0:T(128)S(1)} %concatenate.3.facts, bf16[320,896]{1,0:T(8,128)(2,1)S(1)} %collective-permute-done.6.mid_piece, bf16[320,896]{1,0:T(8,128)(2,1)S(1)} %collective-permute-done.13.end_piece, f32[512,896]{1,0:T(8,128)S(1)} %get-tuple-element.21.so_far, ...), custom_call_target="tpu_custom_call" | custom-call | flops 513802240 | bytes 2752512 | tf_op jit(solution)/shard_map/pallas_call | solution.py:264
  70.1 0.0 copy-start.1
  70.1 1.6 %collective-permute-start.14 = (bf16[160,896]{1,0:T(8,128)(2,1)S(1)}, bf16[160,896]{1,0:T(8,128)(2,1)S(1)}, u32[]{:S(2)}, u32[]{:S(2)}) collective-permute-start(bf16[160,896]{1,0:T(8,128)(2,1)S(1)} %get-tuple-element.27), channel_id=1, source_target_pairs={{0,4},{1,5},{2,6},{3,7},{4,0},{5,1},{6,2},{7,3},{8,12},{9,13},{10,... | collective-permute-start | bytes 860168 | tf_op jit(solution)/shard_map/ppermute | solution.py:456
  71.7 3.3 %collective-permute-done.10.end_piece = bf16[192,896]{1,0:T(8,128)(2,1)S(1)} collective-permute-done((bf16[192,896]{1,0:T(8,128)(2,1)S(1)}, bf16[192,896]{1,0:T(8,128)(2,1)S(1)}, u32[]{:S(2)}, u32[]{:S(2)}) %collective-permute-start.10) | collective-permute-done | bytes 344096 | tf_op jit(solution)/shard_map/ppermute | solution.py:422
  75.0 1.2 %shard_map.88 = (f32[96,896]{1,0:T(8,128)S(1)}, bf16[96,896]{1,0:T(8,128)(2,1)S(1)}) custom-call(s32[25]{0:T(128)S(1)} %concatenate.3.facts, bf16[192,896]{1,0:T(8,128)(2,1)S(1)} %collective-permute-done.7.mid_piece, bf16[192,896]{1,0:T(8,128)(2,1)S(1)} %collective-permute-done.10.end_piece, f32[512,896]{1,0:T(8,128)S(1)} %get-tuple-element.21.so_far, ...), custom_call_target="tpu_custom_call" | custom-call | flops 308281344 | bytes 2293760 | tf_op jit(solution)/shard_map/pallas_call | solution.py:264
  76.2 1.6 %collective-permute-start.11 = (bf16[96,896]{1,0:T(8,128)(2,1)S(1)}, bf16[96,896]{1,0:T(8,128)(2,1)S(1)}, u32[]{:S(2)}, u32[]{:S(2)}) collective-permute-start(bf16[96,896]{1,0:T(8,128)(2,1)S(1)} %get-tuple-element.24), channel_id=1, source_target_pairs={{0,4},{1,5},{2,6},{3,7},{4,0},{5,1},{6,2},{7,3},{8,12},{9,13},{10,... | collective-permute-start | bytes 516104 | tf_op jit(solution)/shard_map/ppermute | solution.py:456
  77.8 0.0 collective-permute-done.12.pool_other
  77.8 0.0 copy-done.1
  77.8 0.6 shard_map.89.aligned
  78.5 0.0 collective-permute-done.14.other_q
  78.5 2.2 %shard_map.91.refs_0_ = bf16[256,896]{1,0:T(8,128)(2,1)} custom-call(s32[25]{0:T(128)S(1)} %concatenate.3.facts, f32[160,896]{1,0:T(8,128)S(1)} %get-tuple-element.26.own_q, bf16[160,896]{1,0:T(8,128)(2,1)S(1)} %collective-permute-done.14.other_q, bf16[2,4,512,256]{3,2,1,0:T(8,128)(2,1)S(1)} %shard_map.89.aligned), custom_call_target="tpu_custom_call" | custom-call | flops 293601280 | bytes 3670016 | tf_op jit(solution)/shard_map/pallas_call | solution.py:394
  80.7 1.0 %collective-permute-done.11.other_q = bf16[96,896]{1,0:T(8,128)(2,1)S(1)} collective-permute-done((bf16[96,896]{1,0:T(8,128)(2,1)S(1)}, bf16[96,896]{1,0:T(8,128)(2,1)S(1)}, u32[]{:S(2)}, u32[]{:S(2)}) %collective-permute-start.11) | collective-permute-done | bytes 172064 | tf_op jit(solution)/shard_map/ppermute | solution.py:456
  81.7 2.1 %shard_map.92 = bf16[256,896]{1,0:T(8,128)(2,1)} custom-call(s32[25]{0:T(128)S(1)} %concatenate.3.facts, f32[96,896]{1,0:T(8,128)S(1)} %get-tuple-element.23.own_q, bf16[96,896]{1,0:T(8,128)(2,1)S(1)} %collective-permute-done.11.other_q, bf16[2,4,512,256]{3,2,1,0:T(8,128)(2,1)S(1)} %shard_map.89.aligned, ...), custom_call_target="tpu_custom_call", output_to_operand_aliasing={{}: (4, {})} | custom-call | flops 176160768 | bytes 3670016 | tf_op jit(solution)/shard_map/pallas_call | solution.py:394
  (4 shorter events, 0.0 us)
Async XLA Ops:
  0.6 12.0 %collective-permute-start.1 = (bf16[512,896]{1,0:T(8,128)(2,1)}, bf16[512,896]{1,0:T(8,128)(2,1)S(1)}, u32[]{:S(2)}, u32[]{:S(2)}) collective-permute-start(bf16[512,896]{1,0:T(8,128)(2,1)} %refs_0_.1), channel_id=1, source_target_pairs={{1,2},{2,1},{5,6},{6,5},{9,10},{10,9},{13,14},{14,13},{17,18},{18,... | collective-permute-start | bytes 2752520 | tf_op jit(solution)/shard_map/ppermute | solution.py:417
  1.4 26.1 %collective-permute-start = (bf16[512,896]{1,0:T(8,128)(2,1)}, bf16[512,896]{1,0:T(8,128)(2,1)S(1)}, u32[]{:S(2)}, u32[]{:S(2)}) collective-permute-start(bf16[512,896]{1,0:T(8,128)(2,1)} %refs_0_.1), channel_id=1, source_target_pairs={{0,1},{1,0},{2,3},{3,2},{4,5},{5,4},{6,7},{7,6},{8,9},{9,8},{10,11... | collective-permute-start | bytes 2752520 | tf_op jit(solution)/shard_map/ppermute | solution.py:416
  9.3 43.1 %copy-start.5 = (s32[1,8]{1,0:T(1,128)S(1)}, s32[1,8]{1,0:T(1,128)}, u32[]{:S(2)}) copy-start(s32[1,8]{1,0:T(1,128)} %param.11) | copy-start | bytes 100
  9.3 44.5 %copy-start.2 = (bf16[2,128,896]{2,1,0:T(8,128)(2,1)S(1)}, bf16[2,128,896]{2,1,0:T(8,128)(2,1)}, u32[]{:S(2)}) copy-start(bf16[2,128,896]{2,1,0:T(8,128)(2,1)} %pool_own.1) | copy-start | bytes 1376260
  9.3 36.4 %collective-permute-start.3 = (bf16[448,1792]{1,0:T(8,128)(2,1)S(1)}, bf16[448,1792]{1,0:T(8,128)(2,1)}, u32[]{:S(2)}, u32[]{:S(2)}) collective-permute-start(bf16[448,1792]{1,0:T(8,128)(2,1)S(1)} %convert_element_type.2), channel_id=1, source_target_pairs={{0,16},{1,17},{2,18},{3,19},{4,0},{5,1},{6,2},{7,3},{8,24},{9,25},... | collective-permute-start | bytes 4816904 | tf_op jit(solution)/shard_map/ppermute | solution.py:432
  10.8 34.9 %collective-permute-start.4 = (bf16[448,1792]{1,0:T(8,128)(2,1)S(1)}, bf16[448,1792]{1,0:T(8,128)(2,1)}, u32[]{:S(2)}, u32[]{:S(2)}) collective-permute-start(bf16[448,1792]{1,0:T(8,128)(2,1)S(1)} %convert_element_type.2), channel_id=1, source_target_pairs={{0,0},{1,1},{2,2},{3,3},{4,16},{5,17},{6,18},{7,19},{8,8},{9,9},{1... | collective-permute-start | bytes 4816904 | tf_op jit(solution)/shard_map/ppermute | solution.py:433
  12.7 36.0 %copy-start.3 = (bf16[512,896]{1,0:T(8,128)(2,1)}, bf16[512,896]{1,0:T(8,128)(2,1)S(1)}, u32[]{:S(2)}) copy-start(bf16[512,896]{1,0:T(8,128)(2,1)S(1)} %collective-permute-done.1.refs_2_) | copy-start | bytes 2752516
  12.7 36.0 %collective-permute-start.2 = (bf16[512,896]{1,0:T(8,128)(2,1)S(1)}, bf16[512,896]{1,0:T(8,128)(2,1)S(1)}, u32[]{:S(2)}, u32[]{:S(2)}) collective-permute-start(bf16[512,896]{1,0:T(8,128)(2,1)S(1)} %collective-permute-done.1.refs_2_), channel_id=1, source_target_pairs={{1,0},{2,3},{5,4},{6,7},{9,8},{10,11},{13,12},{14,15},{17,16},{18,... | collective-permute-start | bytes 2752520 | tf_op jit(solution)/shard_map/ppermute | solution.py:418
  27.5 28.0 %copy-start = (bf16[512,896]{1,0:T(8,128)(2,1)}, bf16[512,896]{1,0:T(8,128)(2,1)S(1)}, u32[]{:S(2)}) copy-start(bf16[512,896]{1,0:T(8,128)(2,1)S(1)} %collective-permute-done.piece.refs_1_) | copy-start | bytes 2752516
  27.6 1.4 %collective-permute-start.7 = (bf16[192,896]{1,0:T(8,128)(2,1)S(1)}, bf16[192,896]{1,0:T(8,128)(2,1)S(1)}, u32[]{:S(2)}, u32[]{:S(2)}) collective-permute-start(bf16[192,896]{1,0:T(8,128)(2,1)S(1)} %get-tuple-element.16), channel_id=1, source_target_pairs={{1,2},{2,1},{5,6},{6,5},{9,10},{10,9},{13,14},{14,13},{17,18},{18,... | collective-permute-start | bytes 1032200 | tf_op jit(solution)/shard_map/ppermute | solution.py:421
  28.3 2.6 %collective-permute-start.6 = (bf16[320,896]{1,0:T(8,128)(2,1)S(1)}, bf16[320,896]{1,0:T(8,128)(2,1)S(1)}, u32[]{:S(2)}, u32[]{:S(2)}) collective-permute-start(bf16[320,896]{1,0:T(8,128)(2,1)S(1)} %get-tuple-element.15), channel_id=1, source_target_pairs={{1,2},{2,1},{5,6},{6,5},{9,10},{10,9},{13,14},{14,13},{17,18},{18,... | collective-permute-start | bytes 1720328 | tf_op jit(solution)/shard_map/ppermute | solution.py:420
  29.0 1.9 %collective-permute-start.5 = (bf16[256,896]{1,0:T(8,128)(2,1)S(1)}, bf16[256,896]{1,0:T(8,128)(2,1)S(1)}, u32[]{:S(2)}, u32[]{:S(2)}) collective-permute-start(bf16[256,896]{1,0:T(8,128)(2,1)S(1)} %slice.4), channel_id=1, source_target_pairs={{0,8},{1,9},{2,10},{3,11},{4,12},{5,13},{6,14},{7,15},{8,0},{9,1},... | collective-permute-start | bytes 1376264 | tf_op jit(solution)/shard_map/ppermute | solution.py:428
  48.7 1.0 %copy-start.4 = (bf16[512,896]{1,0:T(8,128)(2,1)}, bf16[512,896]{1,0:T(8,128)(2,1)S(1)}, u32[]{:S(2)}) copy-start(bf16[512,896]{1,0:T(8,128)(2,1)S(1)} %collective-permute-done.2.refs_3_) | copy-start | bytes 2752516
  48.7 6.8 %collective-permute-start.8 = (bf16[448,1792]{1,0:T(8,128)(2,1)}, bf16[448,1792]{1,0:T(8,128)(2,1)}, u32[]{:S(2)}, u32[]{:S(2)}) collective-permute-start(bf16[448,1792]{1,0:T(8,128)(2,1)} %collective-permute-done.3.refs_4_), channel_id=1, source_target_pairs={{0,8},{1,9},{2,10},{3,11},{4,12},{5,13},{6,14},{7,15},{8,0},{9,1},... | collective-permute-start | bytes 4816904 | tf_op jit(solution)/shard_map/ppermute | solution.py:437
  48.7 6.8 %collective-permute-start.9 = (bf16[448,1792]{1,0:T(8,128)(2,1)}, bf16[448,1792]{1,0:T(8,128)(2,1)}, u32[]{:S(2)}, u32[]{:S(2)}) collective-permute-start(bf16[448,1792]{1,0:T(8,128)(2,1)} %collective-permute-done.4.refs_5_), channel_id=1, source_target_pairs={{0,8},{1,9},{2,10},{3,11},{4,12},{5,13},{6,14},{7,15},{8,0},{9,1},... | collective-permute-start | bytes 4816904 | tf_op jit(solution)/shard_map/ppermute | solution.py:438
  49.7 18.9 %collective-permute-start.13 = (bf16[320,896]{1,0:T(8,128)(2,1)S(1)}, bf16[320,896]{1,0:T(8,128)(2,1)S(1)}, u32[]{:S(2)}, u32[]{:S(2)}) collective-permute-start(bf16[320,896]{1,0:T(8,128)(2,1)S(1)} %collective-permute-done.6.mid_piece), channel_id=1, source_target_pairs={{1,0},{2,3},{5,4},{6,7},{9,8},{10,11},{13,12},{14,15},{17,16},{18,... | collective-permute-start | bytes 1720328 | tf_op jit(solution)/shard_map/ppermute | solution.py:422
  52.5 22.5 %collective-permute-start.10 = (bf16[192,896]{1,0:T(8,128)(2,1)S(1)}, bf16[192,896]{1,0:T(8,128)(2,1)S(1)}, u32[]{:S(2)}, u32[]{:S(2)}) collective-permute-start(bf16[192,896]{1,0:T(8,128)(2,1)S(1)} %collective-permute-done.7.mid_piece), channel_id=1, source_target_pairs={{1,0},{2,3},{5,4},{6,7},{9,8},{10,11},{13,12},{14,15},{17,16},{18,... | collective-permute-start | bytes 1032200 | tf_op jit(solution)/shard_map/ppermute | solution.py:422
  53.8 24.0 %collective-permute-start.12 = (bf16[2,128,896]{2,1,0:T(8,128)(2,1)S(1)}, bf16[2,128,896]{2,1,0:T(8,128)(2,1)S(1)}, u32[]{:S(2)}, u32[]{:S(2)}) collective-permute-start(bf16[2,128,896]{2,1,0:T(8,128)(2,1)S(1)} %copy-done.2), channel_id=1, source_target_pairs={{0,4},{1,5},{2,6},{3,7},{4,0},{5,1},{6,2},{7,3},{8,12},{9,13},{10,... | collective-permute-start | bytes 1376264 | tf_op jit(solution)/shard_map/ppermute | solution.py:439
  70.1 7.7 %copy-start.1 = (bf16[2,256,896]{2,1,0:T(8,128)(2,1)S(1)}, bf16[2,256,896]{2,1,0:T(8,128)(2,1)}, u32[]{:S(2)}) copy-start(bf16[2,256,896]{2,1,0:T(8,128)(2,1)} %prompt.1) | copy-start | bytes 2752516
  70.1 8.3 %collective-permute-start.14 = (bf16[160,896]{1,0:T(8,128)(2,1)S(1)}, bf16[160,896]{1,0:T(8,128)(2,1)S(1)}, u32[]{:S(2)}, u32[]{:S(2)}) collective-permute-start(bf16[160,896]{1,0:T(8,128)(2,1)S(1)} %get-tuple-element.27), channel_id=1, source_target_pairs={{0,4},{1,5},{2,6},{3,7},{4,0},{5,1},{6,2},{7,3},{8,12},{9,13},{10,... | collective-permute-start | bytes 860168 | tf_op jit(solution)/shard_map/ppermute | solution.py:456
  76.2 5.5 %collective-permute-start.11 = (bf16[96,896]{1,0:T(8,128)(2,1)S(1)}, bf16[96,896]{1,0:T(8,128)(2,1)S(1)}, u32[]{:S(2)}, u32[]{:S(2)}) collective-permute-start(bf16[96,896]{1,0:T(8,128)(2,1)S(1)} %get-tuple-element.24), channel_id=1, source_target_pairs={{0,4},{1,5},{2,6},{3,7},{4,0},{5,1},{6,2},{7,3},{8,12},{9,13},{10,... | collective-permute-start | bytes 516104 | tf_op jit(solution)/shard_map/ppermute | solution.py:456

commit v4 on v3

--- a/solution.py
+++ b/solution.py
@@ -423,7 +423,7 @@
 
     token = []
     late = []
-    piece = near[:256]
+    piece = mid_near[0][:192]
     for _ in range(1):
         piece = send(piece, perm=CORE_MOVE)
     token.append(piece)

time: 84.1 us -> 84 us (level)
  starting transfers between devices: 20.5 us -> 17.7 us
  waiting for transfers between devices: 41.7 us -> 44.4 us
    ppermute x1, waiting for transfers between devices: 2.95 us -> 6.93 us  [square_body(): end_own = send(mid_own, perm=END_MOVE)]
    ppermute x1, starting transfers between devices: 5.86 us -> 3.09 us  [square_body(): near = send(tokens, perm=PAIR_MOVE)]
    ppermute x1, waiting for transfers between devices: 1.8 us -> 0.01 us  [square_body(): piece = send(piece, perm=CORE_MOVE)]
    ppermute x2, waiting for transfers between devices: 7.54 us -> 6.03 us  [square_body(): end_near = [send(piece, perm=END_MOVE) for piece in mid_near]]
    ppermute x1, waiting for transfers between devices: 14.8 us -> 16 us  [square_body(): ring = [send(piece, perm=RING_MOVE) for piece in own_w]]
    ppermute x1, waiting for transfers between devices: 13.5 us -> 14.4 us  [square_body(): near = send(tokens, perm=PAIR_MOVE)]
  transfers between devices with their start and end apart: 15 -> 15, of which waited for: 7 -> 6; matrix products, arithmetic and copies ran while one was open for 3% -> 3% of each run, Pallas kernels for 17% -> 17%
where the time goes in v4:
time: 84 us; the launch traced here: 83.7 us
  waiting for transfers between devices  44.4 us (53%)
  starting transfers between devices  17.7 us (21%)
  Pallas kernels  16.6 us (20%)
  between operations  2.23 us (3%)
  other arithmetic  2.07 us (2%)
    ppermute x1, waiting for transfers between devices, square_body(): ring = [send(piece, perm=RING_MOVE) for piece in own_w]  16 us
    ppermute x1, waiting for transfers between devices, square_body(): near = send(tokens, perm=PAIR_MOVE)  14.4 us
    pallas_call x1, Pallas kernels, query_part(): pl.pallas_call(query_kernel, out_shape=(pltpu.VMEM((rows, heads), F32), p...  8.9 us
    ppermute x1, waiting for transfers between devices, square_body(): end_own = send(mid_own, perm=END_MOVE)  6.93 us
    ppermute x2, waiting for transfers between devices, square_body(): end_near = [send(piece, perm=END_MOVE) for piece in mid_near]  6.03 us
    pallas_call x2, Pallas kernels, attend(): pl.pallas_call(functools.partial(attend_kernel, first_row, pool_keys), ou...  4.29 us
    ppermute x2, starting transfers between devices, square_body(): other_q = [send(piece, perm=BLK_MOVE) for piece in send_q]  3.17 us
    ppermute x1, starting transfers between devices, square_body(): near = send(tokens, perm=PAIR_MOVE)  3.09 us
  transfers between devices with their start and end apart: 15, of which 6 were waited for; matrix products, arithmetic and copies ran while one was open for 3% of the time, Pallas kernels for 17%

profile of v4, /device:TPU:0, one launch (start us, length us, event | category | flops | bytes accessed | tf_op | source)
XLA Modules:
  0.0 83.7 jit_solution(9539179194993755434)
XLA Ops:
  0.6 3.1 %collective-permute-start = (bf16[512,896]{1,0:T(8,128)(2,1)}, bf16[512,896]{1,0:T(8,128)(2,1)S(1)}, u32[]{:S(2)}, u32[]{:S(2)}) collective-permute-start(bf16[512,896]{1,0:T(8,128)(2,1)} %refs_0_.1), channel_id=1, source_target_pairs={{0,1},{1,0},{2,3},{3,2},{4,5},{5,4},{6,7},{7,6},{8,9},{9,8},{10,11... | collective-permute-start | bytes 2752520 | tf_op jit(solution)/shard_map/ppermute | solution.py:416
  3.7 0.7 collective-permute-start.1
  4.4 2.1 %convert_element_type.2 = bf16[448,1792]{1,0:T(8,128)(2,1)S(1)} convert(f32[448,1792]{1,0:T(8,128)} %param.8) | non-fusion elementwise | flops 802816 | bytes 4816896 | tf_op jit(solution)/shard_map/convert_element_type | solution.py:431
  6.5 0.0 copy-start.5
  6.5 0.0 copy-start.2
  6.5 1.5 %collective-permute-start.3 = (bf16[448,1792]{1,0:T(8,128)(2,1)S(1)}, bf16[448,1792]{1,0:T(8,128)(2,1)}, u32[]{:S(2)}, u32[]{:S(2)}) collective-permute-start(bf16[448,1792]{1,0:T(8,128)(2,1)S(1)} %convert_element_type.2), channel_id=1, source_target_pairs={{0,16},{1,17},{2,18},{3,19},{4,0},{5,1},{6,2},{7,3},{8,24},{9,25},... | collective-permute-start | bytes 4816904 | tf_op jit(solution)/shard_map/ppermute | solution.py:432
  8.1 1.8 %collective-permute-start.4 = (bf16[448,1792]{1,0:T(8,128)(2,1)S(1)}, bf16[448,1792]{1,0:T(8,128)(2,1)}, u32[]{:S(2)}, u32[]{:S(2)}) collective-permute-start(bf16[448,1792]{1,0:T(8,128)(2,1)S(1)} %convert_element_type.2), channel_id=1, source_target_pairs={{0,0},{1,1},{2,2},{3,3},{4,16},{5,17},{6,18},{7,19},{8,8},{9,9},{1... | collective-permute-start | bytes 4816904 | tf_op jit(solution)/shard_map/ppermute | solution.py:433
  9.9 14.4 %collective-permute-done.piece.refs_1_ = bf16[512,896]{1,0:T(8,128)(2,1)S(1)} collective-permute-done((bf16[512,896]{1,0:T(8,128)(2,1)}, bf16[512,896]{1,0:T(8,128)(2,1)S(1)}, u32[]{:S(2)}, u32[]{:S(2)}) %collective-permute-start) | collective-permute-done | bytes 917536 | tf_op jit(solution)/shard_map/ppermute | solution.py:416
  24.3 0.1 shard_map.86
  24.4 0.7 collective-permute-start.5
  25.1 0.0 collective-permute-done.1.refs_2_
  25.1 0.0 copy-start.3
  25.1 1.3 %collective-permute-start.2 = (bf16[512,896]{1,0:T(8,128)(2,1)S(1)}, bf16[512,896]{1,0:T(8,128)(2,1)S(1)}, u32[]{:S(2)}, u32[]{:S(2)}) collective-permute-start(bf16[512,896]{1,0:T(8,128)(2,1)S(1)} %collective-permute-done.1.refs_2_), channel_id=1, source_target_pairs={{1,0},{2,3},{5,4},{6,7},{9,8},{10,11},{13,12},{14,15},{17,16},{18,... | collective-permute-start | bytes 2752520 | tf_op jit(solution)/shard_map/ppermute | solution.py:418
  26.4 0.7 collective-permute-start.7
  27.1 0.0 collective-permute-done.5.mid_piece
  27.1 0.1 collective-permute-start.6
  27.2 0.0 collective-permute-done.7.mid_piece
  27.2 16.0 %collective-permute-done.3.refs_4_ = bf16[448,1792]{1,0:T(8,128)(2,1)} collective-permute-done((bf16[448,1792]{1,0:T(8,128)(2,1)S(1)}, bf16[448,1792]{1,0:T(8,128)(2,1)}, u32[]{:S(2)}, u32[]{:S(2)}) %collective-permute-start.3) | collective-permute-done | bytes 1605664 | tf_op jit(solution)/shard_map/ppermute | solution.py:432
  43.2 0.0 collective-permute-done.4.refs_5_
  43.2 0.0 collective-permute-done.6.refs_8_
  43.2 6.9 %collective-permute-done.2.refs_3_ = bf16[512,896]{1,0:T(8,128)(2,1)S(1)} collective-permute-done((bf16[512,896]{1,0:T(8,128)(2,1)S(1)}, bf16[512,896]{1,0:T(8,128)(2,1)S(1)}, u32[]{:S(2)}, u32[]{:S(2)}) %collective-permute-start.2) | collective-permute-done | bytes 917536 | tf_op jit(solution)/shard_map/ppermute | solution.py:418
  50.2 0.0 collective-permute-start.8
  50.2 0.0 copy-done.3
  50.2 0.5 collective-permute-start.9
  50.7 0.5 copy-done.4
  51.2 1.3 %collective-permute-start.13 = (bf16[320,896]{1,0:T(8,128)(2,1)S(1)}, bf16[320,896]{1,0:T(8,128)(2,1)S(1)}, u32[]{:S(2)}, u32[]{:S(2)}) collective-permute-start(bf16[320,896]{1,0:T(8,128)(2,1)S(1)} %collective-permute-done.5.mid_piece), channel_id=1, source_target_pairs={{1,0},{2,3},{5,4},{6,7},{9,8},{10,11},{13,12},{14,15},{17,16},{18,... | collective-permute-start | bytes 1720328 | tf_op jit(solution)/shard_map/ppermute | solution.py:422
  53.9 0.0 copy-done.5
  53.9 0.1 concatenate.3.facts
  54.0 1.3 %collective-permute-start.10 = (bf16[192,896]{1,0:T(8,128)(2,1)S(1)}, bf16[192,896]{1,0:T(8,128)(2,1)S(1)}, u32[]{:S(2)}, u32[]{:S(2)}) collective-permute-start(bf16[192,896]{1,0:T(8,128)(2,1)S(1)} %collective-permute-done.7.mid_piece), channel_id=1, source_target_pairs={{1,0},{2,3},{5,4},{6,7},{9,8},{10,11},{13,12},{14,15},{17,16},{18,... | collective-permute-start | bytes 1032200 | tf_op jit(solution)/shard_map/ppermute | solution.py:422
  55.3 0.0 copy-done.2
  55.3 1.6 %collective-permute-start.12 = (bf16[2,128,896]{2,1,0:T(8,128)(2,1)S(1)}, bf16[2,128,896]{2,1,0:T(8,128)(2,1)S(1)}, u32[]{:S(2)}, u32[]{:S(2)}) collective-permute-start(bf16[2,128,896]{2,1,0:T(8,128)(2,1)S(1)} %copy-done.2), channel_id=1, source_target_pairs={{0,4},{1,5},{2,6},{3,7},{4,0},{5,1},{6,2},{7,3},{8,12},{9,13},{10,... | collective-permute-start | bytes 1376264 | tf_op jit(solution)/shard_map/ppermute | solution.py:439
  56.9 0.0 collective-permute-done.8.refs_6_
  56.9 0.0 collective-permute-done.9.refs_7_
  56.9 0.0 copy-done
  56.9 8.9 %shard_map.87 = (f32[512,896]{1,0:T(8,128)S(1)}, bf16[896,896]{1,0:T(8,128)(2,1)S(1)}, bf16[896,3584]{1,0:T(8,128)(2,1)}) custom-call(s32[25]{0:T(128)S(1)} %concatenate.3.facts, bf16[512,896]{1,0:T(8,128)(2,1)} %refs_0_.1, bf16[512,896]{1,0:T(8,128)(2,1)} %copy-done, bf16[512,896]{1,0:T(8,128)(2,1)} %copy-done.3, bf16[512,896]{1,0:T(8,128)(2,1)} %copy-done.4, ...), custom_call_target="tpu_custom_call" | custom-call | flops 2466250752 | bytes 16515072 | tf_op jit(solution)/shard_map/pallas_call | solution.py:215
  65.8 3.2 %collective-permute-done.13.end_piece = bf16[320,896]{1,0:T(8,128)(2,1)S(1)} collective-permute-done((bf16[320,896]{1,0:T(8,128)(2,1)S(1)}, bf16[320,896]{1,0:T(8,128)(2,1)S(1)}, u32[]{:S(2)}, u32[]{:S(2)}) %collective-permute-start.13) | collective-permute-done | bytes 573472 | tf_op jit(solution)/shard_map/ppermute | solution.py:422
  69.0 1.5 %shard_map.90 = (f32[160,896]{1,0:T(8,128)S(1)}, bf16[160,896]{1,0:T(8,128)(2,1)S(1)}) custom-call(s32[25]{0:T(128)S(1)} %concatenate.3.facts, bf16[320,896]{1,0:T(8,128)(2,1)S(1)} %collective-permute-done.5.mid_piece, bf16[320,896]{1,0:T(8,128)(2,1)S(1)} %collective-permute-done.13.end_piece, f32[512,896]{1,0:T(8,128)S(1)} %get-tuple-element.21.so_far, ...), custom_call_target="tpu_custom_call" | custom-call | flops 513802240 | bytes 2752512 | tf_op jit(solution)/shard_map/pallas_call | solution.py:264
  70.5 0.0 copy-start.1
  70.5 1.6 %collective-permute-start.14 = (bf16[160,896]{1,0:T(8,128)(2,1)S(1)}, bf16[160,896]{1,0:T(8,128)(2,1)S(1)}, u32[]{:S(2)}, u32[]{:S(2)}) collective-permute-start(bf16[160,896]{1,0:T(8,128)(2,1)S(1)} %get-tuple-element.27), channel_id=1, source_target_pairs={{0,4},{1,5},{2,6},{3,7},{4,0},{5,1},{6,2},{7,3},{8,12},{9,13},{10,... | collective-permute-start | bytes 860168 | tf_op jit(solution)/shard_map/ppermute | solution.py:456
  72.1 2.8 %collective-permute-done.10.end_piece = bf16[192,896]{1,0:T(8,128)(2,1)S(1)} collective-permute-done((bf16[192,896]{1,0:T(8,128)(2,1)S(1)}, bf16[192,896]{1,0:T(8,128)(2,1)S(1)}, u32[]{:S(2)}, u32[]{:S(2)}) %collective-permute-start.10) | collective-permute-done | bytes 344096 | tf_op jit(solution)/shard_map/ppermute | solution.py:422
  74.9 1.3 %shard_map.88 = (f32[96,896]{1,0:T(8,128)S(1)}, bf16[96,896]{1,0:T(8,128)(2,1)S(1)}) custom-call(s32[25]{0:T(128)S(1)} %concatenate.3.facts, bf16[192,896]{1,0:T(8,128)(2,1)S(1)} %collective-permute-done.7.mid_piece, bf16[192,896]{1,0:T(8,128)(2,1)S(1)} %collective-permute-done.10.end_piece, f32[512,896]{1,0:T(8,128)S(1)} %get-tuple-element.21.so_far, ...), custom_call_target="tpu_custom_call" | custom-call | flops 308281344 | bytes 2293760 | tf_op jit(solution)/shard_map/pallas_call | solution.py:264
  76.2 1.6 %collective-permute-start.11 = (bf16[96,896]{1,0:T(8,128)(2,1)S(1)}, bf16[96,896]{1,0:T(8,128)(2,1)S(1)}, u32[]{:S(2)}, u32[]{:S(2)}) collective-permute-start(bf16[96,896]{1,0:T(8,128)(2,1)S(1)} %get-tuple-element.24), channel_id=1, source_target_pairs={{0,4},{1,5},{2,6},{3,7},{4,0},{5,1},{6,2},{7,3},{8,12},{9,13},{10,... | collective-permute-start | bytes 516104 | tf_op jit(solution)/shard_map/ppermute | solution.py:456
  77.8 0.0 collective-permute-done.12.pool_other
  77.8 0.6 shard_map.89.aligned
  78.4 0.0 collective-permute-done.14.other_q
  78.4 2.2 %shard_map.91.refs_0_ = bf16[256,896]{1,0:T(8,128)(2,1)} custom-call(s32[25]{0:T(128)S(1)} %concatenate.3.facts, f32[160,896]{1,0:T(8,128)S(1)} %get-tuple-element.26.own_q, bf16[160,896]{1,0:T(8,128)(2,1)S(1)} %collective-permute-done.14.other_q, bf16[2,4,512,256]{3,2,1,0:T(8,128)(2,1)S(1)} %shard_map.89.aligned), custom_call_target="tpu_custom_call" | custom-call | flops 293601280 | bytes 3670016 | tf_op jit(solution)/shard_map/pallas_call | solution.py:394
  80.6 1.0 %collective-permute-done.11.other_q = bf16[96,896]{1,0:T(8,128)(2,1)S(1)} collective-permute-done((bf16[96,896]{1,0:T(8,128)(2,1)S(1)}, bf16[96,896]{1,0:T(8,128)(2,1)S(1)}, u32[]{:S(2)}, u32[]{:S(2)}) %collective-permute-start.11) | collective-permute-done | bytes 172064 | tf_op jit(solution)/shard_map/ppermute | solution.py:456
  81.6 2.1 %shard_map.92 = bf16[256,896]{1,0:T(8,128)(2,1)} custom-call(s32[25]{0:T(128)S(1)} %concatenate.3.facts, f32[96,896]{1,0:T(8,128)S(1)} %get-tuple-element.23.own_q, bf16[96,896]{1,0:T(8,128)(2,1)S(1)} %collective-permute-done.11.other_q, bf16[2,4,512,256]{3,2,1,0:T(8,128)(2,1)S(1)} %shard_map.89.aligned, ...), custom_call_target="tpu_custom_call", output_to_operand_aliasing={{}: (4, {})} | custom-call | flops 176160768 | bytes 3670016 | tf_op jit(solution)/shard_map/pallas_call | solution.py:394
  (4 shorter events, 0.0 us)
Async XLA Ops:
  0.6 23.7 %collective-permute-start = (bf16[512,896]{1,0:T(8,128)(2,1)}, bf16[512,896]{1,0:T(8,128)(2,1)S(1)}, u32[]{:S(2)}, u32[]{:S(2)}) collective-permute-start(bf16[512,896]{1,0:T(8,128)(2,1)} %refs_0_.1), channel_id=1, source_target_pairs={{0,1},{1,0},{2,3},{3,2},{4,5},{5,4},{6,7},{7,6},{8,9},{9,8},{10,11... | collective-permute-start | bytes 2752520 | tf_op jit(solution)/shard_map/ppermute | solution.py:416
  3.7 21.3 %collective-permute-start.1 = (bf16[512,896]{1,0:T(8,128)(2,1)}, bf16[512,896]{1,0:T(8,128)(2,1)S(1)}, u32[]{:S(2)}, u32[]{:S(2)}) collective-permute-start(bf16[512,896]{1,0:T(8,128)(2,1)} %refs_0_.1), channel_id=1, source_target_pairs={{1,2},{2,1},{5,6},{6,5},{9,10},{10,9},{13,14},{14,13},{17,18},{18,... | collective-permute-start | bytes 2752520 | tf_op jit(solution)/shard_map/ppermute | solution.py:417
  6.5 47.4 %copy-start.5 = (s32[1,8]{1,0:T(1,128)S(1)}, s32[1,8]{1,0:T(1,128)}, u32[]{:S(2)}) copy-start(s32[1,8]{1,0:T(1,128)} %param.11) | copy-start | bytes 100
  6.5 48.8 %copy-start.2 = (bf16[2,128,896]{2,1,0:T(8,128)(2,1)S(1)}, bf16[2,128,896]{2,1,0:T(8,128)(2,1)}, u32[]{:S(2)}) copy-start(bf16[2,128,896]{2,1,0:T(8,128)(2,1)} %pool_own.1) | copy-start | bytes 1376260
  6.5 36.7 %collective-permute-start.3 = (bf16[448,1792]{1,0:T(8,128)(2,1)S(1)}, bf16[448,1792]{1,0:T(8,128)(2,1)}, u32[]{:S(2)}, u32[]{:S(2)}) collective-permute-start(bf16[448,1792]{1,0:T(8,128)(2,1)S(1)} %convert_element_type.2), channel_id=1, source_target_pairs={{0,16},{1,17},{2,18},{3,19},{4,0},{5,1},{6,2},{7,3},{8,24},{9,25},... | collective-permute-start | bytes 4816904 | tf_op jit(solution)/shard_map/ppermute | solution.py:432
  8.1 35.2 %collective-permute-start.4 = (bf16[448,1792]{1,0:T(8,128)(2,1)S(1)}, bf16[448,1792]{1,0:T(8,128)(2,1)}, u32[]{:S(2)}, u32[]{:S(2)}) collective-permute-start(bf16[448,1792]{1,0:T(8,128)(2,1)S(1)} %convert_element_type.2), channel_id=1, source_target_pairs={{0,0},{1,1},{2,2},{3,3},{4,16},{5,17},{6,18},{7,19},{8,8},{9,9},{1... | collective-permute-start | bytes 4816904 | tf_op jit(solution)/shard_map/ppermute | solution.py:433
  24.3 32.6 %copy-start = (bf16[512,896]{1,0:T(8,128)(2,1)}, bf16[512,896]{1,0:T(8,128)(2,1)S(1)}, u32[]{:S(2)}) copy-start(bf16[512,896]{1,0:T(8,128)(2,1)S(1)} %collective-permute-done.piece.refs_1_) | copy-start | bytes 2752516
  24.4 2.7 %collective-permute-start.5 = (bf16[320,896]{1,0:T(8,128)(2,1)S(1)}, bf16[320,896]{1,0:T(8,128)(2,1)S(1)}, u32[]{:S(2)}, u32[]{:S(2)}) collective-permute-start(bf16[320,896]{1,0:T(8,128)(2,1)S(1)} %get-tuple-element.15), channel_id=1, source_target_pairs={{1,2},{2,1},{5,6},{6,5},{9,10},{10,9},{13,14},{14,13},{17,18},{18,... | collective-permute-start | bytes 1720328 | tf_op jit(solution)/shard_map/ppermute | solution.py:420
  25.1 25.1 %copy-start.3 = (bf16[512,896]{1,0:T(8,128)(2,1)}, bf16[512,896]{1,0:T(8,128)(2,1)S(1)}, u32[]{:S(2)}) copy-start(bf16[512,896]{1,0:T(8,128)(2,1)S(1)} %collective-permute-done.1.refs_2_) | copy-start | bytes 2752516
  25.1 25.1 %collective-permute-start.2 = (bf16[512,896]{1,0:T(8,128)(2,1)S(1)}, bf16[512,896]{1,0:T(8,128)(2,1)S(1)}, u32[]{:S(2)}, u32[]{:S(2)}) collective-permute-start(bf16[512,896]{1,0:T(8,128)(2,1)S(1)} %collective-permute-done.1.refs_2_), channel_id=1, source_target_pairs={{1,0},{2,3},{5,4},{6,7},{9,8},{10,11},{13,12},{14,15},{17,16},{18,... | collective-permute-start | bytes 2752520 | tf_op jit(solution)/shard_map/ppermute | solution.py:418
  26.4 0.8 collective-permute-start.7
  27.1 16.1 %collective-permute-start.6 = (bf16[192,896]{1,0:T(8,128)(2,1)S(1)}, bf16[192,896]{1,0:T(8,128)(2,1)S(1)}, u32[]{:S(2)}, u32[]{:S(2)}) collective-permute-start(bf16[192,896]{1,0:T(8,128)(2,1)S(1)} %slice.4), channel_id=1, source_target_pairs={{0,8},{1,9},{2,10},{3,11},{4,12},{5,13},{6,14},{7,15},{8,0},{9,1},... | collective-permute-start | bytes 1032200 | tf_op jit(solution)/shard_map/ppermute | solution.py:428
  50.2 1.0 %copy-start.4 = (bf16[512,896]{1,0:T(8,128)(2,1)}, bf16[512,896]{1,0:T(8,128)(2,1)S(1)}, u32[]{:S(2)}) copy-start(bf16[512,896]{1,0:T(8,128)(2,1)S(1)} %collective-permute-done.2.refs_3_) | copy-start | bytes 2752516
  50.2 6.7 %collective-permute-start.8 = (bf16[448,1792]{1,0:T(8,128)(2,1)}, bf16[448,1792]{1,0:T(8,128)(2,1)}, u32[]{:S(2)}, u32[]{:S(2)}) collective-permute-start(bf16[448,1792]{1,0:T(8,128)(2,1)} %collective-permute-done.3.refs_4_), channel_id=1, source_target_pairs={{0,8},{1,9},{2,10},{3,11},{4,12},{5,13},{6,14},{7,15},{8,0},{9,1},... | collective-permute-start | bytes 4816904 | tf_op jit(solution)/shard_map/ppermute | solution.py:437
  50.2 6.7 %collective-permute-start.9 = (bf16[448,1792]{1,0:T(8,128)(2,1)}, bf16[448,1792]{1,0:T(8,128)(2,1)}, u32[]{:S(2)}, u32[]{:S(2)}) collective-permute-start(bf16[448,1792]{1,0:T(8,128)(2,1)} %collective-permute-done.4.refs_5_), channel_id=1, source_target_pairs={{0,8},{1,9},{2,10},{3,11},{4,12},{5,13},{6,14},{7,15},{8,0},{9,1},... | collective-permute-start | bytes 4816904 | tf_op jit(solution)/shard_map/ppermute | solution.py:438
  51.2 17.8 %collective-permute-start.13 = (bf16[320,896]{1,0:T(8,128)(2,1)S(1)}, bf16[320,896]{1,0:T(8,128)(2,1)S(1)}, u32[]{:S(2)}, u32[]{:S(2)}) collective-permute-start(bf16[320,896]{1,0:T(8,128)(2,1)S(1)} %collective-permute-done.5.mid_piece), channel_id=1, source_target_pairs={{1,0},{2,3},{5,4},{6,7},{9,8},{10,11},{13,12},{14,15},{17,16},{18,... | collective-permute-start | bytes 1720328 | tf_op jit(solution)/shard_map/ppermute | solution.py:422
  54.0 20.9 %collective-permute-start.10 = (bf16[192,896]{1,0:T(8,128)(2,1)S(1)}, bf16[192,896]{1,0:T(8,128)(2,1)S(1)}, u32[]{:S(2)}, u32[]{:S(2)}) collective-permute-start(bf16[192,896]{1,0:T(8,128)(2,1)S(1)} %collective-permute-done.7.mid_piece), channel_id=1, source_target_pairs={{1,0},{2,3},{5,4},{6,7},{9,8},{10,11},{13,12},{14,15},{17,16},{18,... | collective-permute-start | bytes 1032200 | tf_op jit(solution)/shard_map/ppermute | solution.py:422
  55.3 22.5 %collective-permute-start.12 = (bf16[2,128,896]{2,1,0:T(8,128)(2,1)S(1)}, bf16[2,128,896]{2,1,0:T(8,128)(2,1)S(1)}, u32[]{:S(2)}, u32[]{:S(2)}) collective-permute-start(bf16[2,128,896]{2,1,0:T(8,128)(2,1)S(1)} %copy-done.2), channel_id=1, source_target_pairs={{0,4},{1,5},{2,6},{3,7},{4,0},{5,1},{6,2},{7,3},{8,12},{9,13},{10,... | collective-permute-start | bytes 1376264 | tf_op jit(solution)/shard_map/ppermute | solution.py:439
  70.5 7.3 %copy-start.1 = (bf16[2,256,896]{2,1,0:T(8,128)(2,1)S(1)}, bf16[2,256,896]{2,1,0:T(8,128)(2,1)}, u32[]{:S(2)}) copy-start(bf16[2,256,896]{2,1,0:T(8,128)(2,1)} %prompt.1) | copy-start | bytes 2752516
  70.5 7.9 %collective-permute-start.14 = (bf16[160,896]{1,0:T(8,128)(2,1)S(1)}, bf16[160,896]{1,0:T(8,128)(2,1)S(1)}, u32[]{:S(2)}, u32[]{:S(2)}) collective-permute-start(bf16[160,896]{1,0:T(8,128)(2,1)S(1)} %get-tuple-element.27), channel_id=1, source_target_pairs={{0,4},{1,5},{2,6},{3,7},{4,0},{5,1},{6,2},{7,3},{8,12},{9,13},{10,... | collective-permute-start | bytes 860168 | tf_op jit(solution)/shard_map/ppermute | solution.py:456
  76.2 5.5 %collective-permute-start.11 = (bf16[96,896]{1,0:T(8,128)(2,1)S(1)}, bf16[96,896]{1,0:T(8,128)(2,1)S(1)}, u32[]{:S(2)}, u32[]{:S(2)}) collective-permute-start(bf16[96,896]{1,0:T(8,128)(2,1)S(1)} %get-tuple-element.24), channel_id=1, source_target_pairs={{0,4},{1,5},{2,6},{3,7},{4,0},{5,1},{6,2},{7,3},{8,12},{9,13},{10,... | collective-permute-start | bytes 516104 | tf_op jit(solution)/shard_map/ppermute | solution.py:456

commit v5 on v4

--- a/solution.py
+++ b/solution.py
@@ -255,6 +255,34 @@
     def _():
         own[...] = lower
         send[...] = upper.astype(BF16)
+
+
+def side_kernel(first_row, sent, facts, mid_piece, end_piece, so_far, weights, out):
+    half, whole = out.shape[0], so_far.shape[0] // 2
+    request = 1 - facts[0] if sent else facts[0]
+    here = pl.ds(pl.multiple_of(request * half, 16), half)
+    piece = jnp.where(facts[1] == 1, mid_piece[here, :], end_piece[here, :])
+    part = lax.dot_general(piece, weights[...], NT, preferred_element_type=F32)
+    before = so_far[pl.ds(pl.multiple_of(request * whole + first_row, 16), half), :]
+    out[...] = (before + part).astype(out.dtype)
+
+
+def query_side(first_row, sent, facts, mid_piece, end_piece, so_far, weights):
+    rows, depth = mid_piece.shape
+    heads = weights.shape[0]
+    vmem = pl.BlockSpec(memory_space=pltpu.VMEM)
+    return pl.pallas_call(
+        functools.partial(side_kernel, first_row, sent),
+        out_shape=jax.ShapeDtypeStruct((rows // 2, heads), BF16 if sent else F32),
+        in_specs=[pl.BlockSpec(memory_space=pltpu.SMEM)] + [vmem] * 4,
+        out_specs=vmem,
+        compiler_params=pltpu.CompilerParams(vmem_limit_bytes=6 * 1024 * 1024),
+        cost_estimate=pl.CostEstimate(
+            flops=rows * depth * heads,
+            bytes_accessed=2 * (rows + heads) * depth,
+            transcendentals=0,
+        ),
+    )(facts, mid_piece, end_piece, so_far, weights)
 
 
 def query_last(first_row, facts, mid_piece, end_piece, so_far, weights):
@@ -450,9 +478,12 @@
     so_far, last_w, server_q = query_part(
         facts, (tokens, near, mid_own, end_own), (*ring, *cross, *ring_other, *cross_other), token + late
     )
-    own_q, send_q = zip(
-        *(query_last(c * CUT, facts, mid_near[c], end_near[c], so_far, last_w) for c in range(2))
-    )
+    first_own, first_send = query_last(0, facts, mid_near[0], end_near[0], so_far, last_w)
+    last_own, last_send = (
+        query_side(CUT, sent, facts, mid_near[1], end_near[1], so_far, last_w)
+        for sent in (False, True)
+    )
+    own_q, send_q = (first_own, last_own), (first_send, last_send)
     other_q = [send(piece, perm=BLK_MOVE) for piece in send_q]
 
     aligned = align(prompt_kv, kv_pool, pool_other)

time: 84 us -> 84.1 us (level)
  Pallas kernels: 16.6 us -> 17.7 us
  waiting for transfers between devices: 44.4 us -> 43.4 us
    pallas_call x0 -> x2, Pallas kernels: none -> 2.29 us  [query_side(): pl.pallas_call(functools.partial(side_kernel, first_row, sent), out_shape...]
    pallas_call x2 -> x1, Pallas kernels: 2.73 us -> 1.47 us  [query_last(): pl.pallas_call(functools.partial(last_kernel, first_row), out_shape=(jax....]
    ppermute x2, waiting for transfers between devices: 1.01 us -> 0.01 us  [square_body(): other_q = [send(piece, perm=BLK_MOVE) for piece in send_q]]
  transfers between devices with their start and end apart: 15 -> 15, of which waited for: 6 -> 5; matrix products, arithmetic and copies ran while one was open for 3% -> 3% of each run, Pallas kernels for 17% -> 19%
where the time goes in v5:
time: 84.1 us; the launch traced here: 83.8 us
  waiting for transfers between devices  43.4 us (52%)
  starting transfers between devices  17.7 us (21%)
  Pallas kernels  17.7 us (21%)
  between operations  2.23 us (3%)
  other arithmetic  2.07 us (2%)
    ppermute x1, waiting for transfers between devices, square_body(): ring = [send(piece, perm=RING_MOVE) for piece in own_w]  16 us
    ppermute x1, waiting for transfers between devices, square_body(): near = send(tokens, perm=PAIR_MOVE)  14.4 us
    pallas_call x1, Pallas kernels, query_part(): pl.pallas_call(query_kernel, out_shape=(pltpu.VMEM((rows, heads), F32), p...  8.9 us
    ppermute x1, waiting for transfers between devices, square_body(): end_own = send(mid_own, perm=END_MOVE)  6.93 us
    ppermute x2, waiting for transfers between devices, square_body(): end_near = [send(piece, perm=END_MOVE) for piece in mid_near]  6.05 us
    pallas_call x2, Pallas kernels, attend(): pl.pallas_call(functools.partial(attend_kernel, first_row, pool_keys), ou...  4.31 us
    ppermute x2, starting transfers between devices, square_body(): other_q = [send(piece, perm=BLK_MOVE) for piece in send_q]  3.16 us
    ppermute x1, starting transfers between devices, square_body(): near = send(tokens, perm=PAIR_MOVE)  3.09 us
  transfers between devices with their start and end apart: 15, of which 5 were waited for; matrix products, arithmetic and copies ran while one was open for 3% of the time, Pallas kernels for 19%

profile of v5, /device:TPU:0, one launch (start us, length us, event | category | flops | bytes accessed | tf_op | source)
XLA Modules:
  0.0 83.8 jit_solution(17552355984834968074)
XLA Ops:
  0.6 3.1 %collective-permute-start = (bf16[512,896]{1,0:T(8,128)(2,1)}, bf16[512,896]{1,0:T(8,128)(2,1)S(1)}, u32[]{:S(2)}, u32[]{:S(2)}) collective-permute-start(bf16[512,896]{1,0:T(8,128)(2,1)} %refs_0_.1), channel_id=1, source_target_pairs={{0,1},{1,0},{2,3},{3,2},{4,5},{5,4},{6,7},{7,6},{8,9},{9,8},{10,11... | collective-permute-start | bytes 2752520 | tf_op jit(solution)/shard_map/ppermute | solution.py:444
  3.7 0.7 collective-permute-start.1
  4.4 2.1 %convert_element_type.2 = bf16[448,1792]{1,0:T(8,128)(2,1)S(1)} convert(f32[448,1792]{1,0:T(8,128)} %param.8) | non-fusion elementwise | flops 802816 | bytes 4816896 | tf_op jit(solution)/shard_map/convert_element_type | solution.py:459
  6.5 0.0 copy-start.5
  6.5 0.0 copy-start.2
  6.5 1.5 %collective-permute-start.3 = (bf16[448,1792]{1,0:T(8,128)(2,1)S(1)}, bf16[448,1792]{1,0:T(8,128)(2,1)}, u32[]{:S(2)}, u32[]{:S(2)}) collective-permute-start(bf16[448,1792]{1,0:T(8,128)(2,1)S(1)} %convert_element_type.2), channel_id=1, source_target_pairs={{0,16},{1,17},{2,18},{3,19},{4,0},{5,1},{6,2},{7,3},{8,24},{9,25},... | collective-permute-start | bytes 4816904 | tf_op jit(solution)/shard_map/ppermute | solution.py:460
  8.1 1.8 %collective-permute-start.4 = (bf16[448,1792]{1,0:T(8,128)(2,1)S(1)}, bf16[448,1792]{1,0:T(8,128)(2,1)}, u32[]{:S(2)}, u32[]{:S(2)}) collective-permute-start(bf16[448,1792]{1,0:T(8,128)(2,1)S(1)} %convert_element_type.2), channel_id=1, source_target_pairs={{0,0},{1,1},{2,2},{3,3},{4,16},{5,17},{6,18},{7,19},{8,8},{9,9},{1... | collective-permute-start | bytes 4816904 | tf_op jit(solution)/shard_map/ppermute | solution.py:461
  9.9 14.4 %collective-permute-done.piece.refs_1_ = bf16[512,896]{1,0:T(8,128)(2,1)S(1)} collective-permute-done((bf16[512,896]{1,0:T(8,128)(2,1)}, bf16[512,896]{1,0:T(8,128)(2,1)S(1)}, u32[]{:S(2)}, u32[]{:S(2)}) %collective-permute-start) | collective-permute-done | bytes 917536 | tf_op jit(solution)/shard_map/ppermute | solution.py:444
  24.3 0.1 shard_map.86
  24.4 0.7 collective-permute-start.5
  25.1 0.0 collective-permute-done.1.refs_2_
  25.1 0.0 copy-start.3
  25.1 1.3 %collective-permute-start.2 = (bf16[512,896]{1,0:T(8,128)(2,1)S(1)}, bf16[512,896]{1,0:T(8,128)(2,1)S(1)}, u32[]{:S(2)}, u32[]{:S(2)}) collective-permute-start(bf16[512,896]{1,0:T(8,128)(2,1)S(1)} %collective-permute-done.1.refs_2_), channel_id=1, source_target_pairs={{1,0},{2,3},{5,4},{6,7},{9,8},{10,11},{13,12},{14,15},{17,16},{18,... | collective-permute-start | bytes 2752520 | tf_op jit(solution)/shard_map/ppermute | solution.py:446
  26.4 0.7 collective-permute-start.7
  27.1 0.0 collective-permute-done.5.mid_piece
  27.1 0.1 collective-permute-start.6
  27.2 0.0 collective-permute-done.7.mid_piece
  27.2 16.0 %collective-permute-done.3.refs_4_ = bf16[448,1792]{1,0:T(8,128)(2,1)} collective-permute-done((bf16[448,1792]{1,0:T(8,128)(2,1)S(1)}, bf16[448,1792]{1,0:T(8,128)(2,1)}, u32[]{:S(2)}, u32[]{:S(2)}) %collective-permute-start.3) | collective-permute-done | bytes 1605664 | tf_op jit(solution)/shard_map/ppermute | solution.py:460
  43.2 0.0 collective-permute-done.4.refs_5_
  43.2 0.0 collective-permute-done.6.refs_8_
  43.2 6.9 %collective-permute-done.2.refs_3_ = bf16[512,896]{1,0:T(8,128)(2,1)S(1)} collective-permute-done((bf16[512,896]{1,0:T(8,128)(2,1)S(1)}, bf16[512,896]{1,0:T(8,128)(2,1)S(1)}, u32[]{:S(2)}, u32[]{:S(2)}) %collective-permute-start.2) | collective-permute-done | bytes 917536 | tf_op jit(solution)/shard_map/ppermute | solution.py:446
  50.2 0.0 collective-permute-start.8
  50.2 0.0 copy-done.3
  50.2 0.5 collective-permute-start.9
  50.7 0.5 copy-done.4
  51.2 1.3 %collective-permute-start.13 = (bf16[320,896]{1,0:T(8,128)(2,1)S(1)}, bf16[320,896]{1,0:T(8,128)(2,1)S(1)}, u32[]{:S(2)}, u32[]{:S(2)}) collective-permute-start(bf16[320,896]{1,0:T(8,128)(2,1)S(1)} %collective-permute-done.5.mid_piece), channel_id=1, source_target_pairs={{1,0},{2,3},{5,4},{6,7},{9,8},{10,11},{13,12},{14,15},{17,16},{18,... | collective-permute-start | bytes 1720328 | tf_op jit(solution)/shard_map/ppermute | solution.py:450
  53.9 0.0 copy-done.5
  53.9 0.1 concatenate.3.facts
  54.0 1.3 %collective-permute-start.10 = (bf16[192,896]{1,0:T(8,128)(2,1)S(1)}, bf16[192,896]{1,0:T(8,128)(2,1)S(1)}, u32[]{:S(2)}, u32[]{:S(2)}) collective-permute-start(bf16[192,896]{1,0:T(8,128)(2,1)S(1)} %collective-permute-done.7.mid_piece), channel_id=1, source_target_pairs={{1,0},{2,3},{5,4},{6,7},{9,8},{10,11},{13,12},{14,15},{17,16},{18,... | collective-permute-start | bytes 1032200 | tf_op jit(solution)/shard_map/ppermute | solution.py:450
  55.3 0.0 copy-done.2
  55.3 1.6 %collective-permute-start.12 = (bf16[2,128,896]{2,1,0:T(8,128)(2,1)S(1)}, bf16[2,128,896]{2,1,0:T(8,128)(2,1)S(1)}, u32[]{:S(2)}, u32[]{:S(2)}) collective-permute-start(bf16[2,128,896]{2,1,0:T(8,128)(2,1)S(1)} %copy-done.2), channel_id=1, source_target_pairs={{0,4},{1,5},{2,6},{3,7},{4,0},{5,1},{6,2},{7,3},{8,12},{9,13},{10,... | collective-permute-start | bytes 1376264 | tf_op jit(solution)/shard_map/ppermute | solution.py:467
  56.9 0.0 collective-permute-done.8.refs_6_
  56.9 0.0 collective-permute-done.9.refs_7_
  56.9 8.9 %shard_map.87 = (f32[512,896]{1,0:T(8,128)S(1)}, bf16[896,896]{1,0:T(8,128)(2,1)S(1)}, bf16[896,3584]{1,0:T(8,128)(2,1)}) custom-call(s32[25]{0:T(128)S(1)} %concatenate.3.facts, bf16[512,896]{1,0:T(8,128)(2,1)} %refs_0_.1, bf16[512,896]{1,0:T(8,128)(2,1)} %copy-done, bf16[512,896]{1,0:T(8,128)(2,1)} %copy-done.3, bf16[512,896]{1,0:T(8,128)(2,1)} %copy-done.4, ...), custom_call_target="tpu_custom_call" | custom-call | flops 2466250752 | bytes 16515072 | tf_op jit(solution)/shard_map/pallas_call | solution.py:215
  65.8 3.2 %collective-permute-done.13.end_piece = bf16[320,896]{1,0:T(8,128)(2,1)S(1)} collective-permute-done((bf16[320,896]{1,0:T(8,128)(2,1)S(1)}, bf16[320,896]{1,0:T(8,128)(2,1)S(1)}, u32[]{:S(2)}, u32[]{:S(2)}) %collective-permute-start.13) | collective-permute-done | bytes 573472 | tf_op jit(solution)/shard_map/ppermute | solution.py:450
  69.0 1.5 %shard_map.91 = (f32[160,896]{1,0:T(8,128)S(1)}, bf16[160,896]{1,0:T(8,128)(2,1)S(1)}) custom-call(s32[25]{0:T(128)S(1)} %concatenate.3.facts, bf16[320,896]{1,0:T(8,128)(2,1)S(1)} %collective-permute-done.5.mid_piece, bf16[320,896]{1,0:T(8,128)(2,1)S(1)} %collective-permute-done.13.end_piece, f32[512,896]{1,0:T(8,128)S(1)} %get-tuple-element.19.so_far, ...), custom_call_target="tpu_custom_call" | custom-call | flops 513802240 | bytes 2752512 | tf_op jit(solution)/shard_map/pallas_call | solution.py:292
  70.4 0.0 copy-start.1
  70.5 1.6 %collective-permute-start.14 = (bf16[160,896]{1,0:T(8,128)(2,1)S(1)}, bf16[160,896]{1,0:T(8,128)(2,1)S(1)}, u32[]{:S(2)}, u32[]{:S(2)}) collective-permute-start(bf16[160,896]{1,0:T(8,128)(2,1)S(1)} %get-tuple-element.23), channel_id=1, source_target_pairs={{0,4},{1,5},{2,6},{3,7},{4,0},{5,1},{6,2},{7,3},{8,12},{9,13},{10,... | collective-permute-start | bytes 860168 | tf_op jit(solution)/shard_map/ppermute | solution.py:487
  72.0 2.9 %collective-permute-done.10.end_piece = bf16[192,896]{1,0:T(8,128)(2,1)S(1)} collective-permute-done((bf16[192,896]{1,0:T(8,128)(2,1)S(1)}, bf16[192,896]{1,0:T(8,128)(2,1)S(1)}, u32[]{:S(2)}, u32[]{:S(2)}) %collective-permute-start.10) | collective-permute-done | bytes 344096 | tf_op jit(solution)/shard_map/ppermute | solution.py:450
  74.9 1.1 %shard_map.89 = bf16[96,896]{1,0:T(8,128)(2,1)S(1)} custom-call(s32[25]{0:T(128)S(1)} %concatenate.3.facts, bf16[192,896]{1,0:T(8,128)(2,1)S(1)} %collective-permute-done.7.mid_piece, bf16[192,896]{1,0:T(8,128)(2,1)S(1)} %collective-permute-done.10.end_piece, f32[512,896]{1,0:T(8,128)S(1)} %get-tuple-element.19.so_far, ...), custom_call_target="tpu_custom_call" | custom-call | flops 154140672 | bytes 1949696 | tf_op jit(solution)/shard_map/pallas_call | solution.py:274
  76.1 1.6 %collective-permute-start.11 = (bf16[96,896]{1,0:T(8,128)(2,1)S(1)}, bf16[96,896]{1,0:T(8,128)(2,1)S(1)}, u32[]{:S(2)}, u32[]{:S(2)}) collective-permute-start(bf16[96,896]{1,0:T(8,128)(2,1)S(1)} %shard_map.89), channel_id=1, source_target_pairs={{0,4},{1,5},{2,6},{3,7},{4,0},{5,1},{6,2},{7,3},{8,12},{9,13},{10,... | collective-permute-start | bytes 516104 | tf_op jit(solution)/shard_map/ppermute | solution.py:487
  77.6 0.0 collective-permute-done.12.pool_other
  77.7 0.6 shard_map.90.aligned
  78.3 1.1 %shard_map.88.own_q = f32[96,896]{1,0:T(8,128)S(1)} custom-call(s32[25]{0:T(128)S(1)} %concatenate.3.facts, bf16[192,896]{1,0:T(8,128)(2,1)S(1)} %collective-permute-done.7.mid_piece, bf16[192,896]{1,0:T(8,128)(2,1)S(1)} %collective-permute-done.10.end_piece, f32[512,896]{1,0:T(8,128)S(1)} %get-tuple-element.19.so_far, ...), custom_call_target="tpu_custom_call" | custom-call | flops 154140672 | bytes 1949696 | tf_op jit(solution)/shard_map/pallas_call | solution.py:274
  79.4 0.0 collective-permute-done.14.other_q
  79.5 2.2 %shard_map.92.refs_0_ = bf16[256,896]{1,0:T(8,128)(2,1)} custom-call(s32[25]{0:T(128)S(1)} %concatenate.3.facts, f32[160,896]{1,0:T(8,128)S(1)} %get-tuple-element.22.own_q, bf16[160,896]{1,0:T(8,128)(2,1)S(1)} %collective-permute-done.14.other_q, bf16[2,4,512,256]{3,2,1,0:T(8,128)(2,1)S(1)} %shard_map.90.aligned), custom_call_target="tpu_custom_call" | custom-call | flops 293601280 | bytes 3670016 | tf_op jit(solution)/shard_map/pallas_call | solution.py:422
  81.7 0.0 collective-permute-done.11.other_q
  81.7 2.1 %shard_map.93 = bf16[256,896]{1,0:T(8,128)(2,1)} custom-call(s32[25]{0:T(128)S(1)} %concatenate.3.facts, f32[96,896]{1,0:T(8,128)S(1)} %shard_map.88.own_q, bf16[96,896]{1,0:T(8,128)(2,1)S(1)} %collective-permute-done.11.other_q, bf16[2,4,512,256]{3,2,1,0:T(8,128)(2,1)S(1)} %shard_map.90.aligned, ...), custom_call_target="tpu_custom_call", output_to_operand_aliasing={{}: (4, {})} | custom-call | flops 176160768 | bytes 3670016 | tf_op jit(solution)/shard_map/pallas_call | solution.py:422
  (5 shorter events, 0.0 us)
Async XLA Ops:
  0.6 23.7 %collective-permute-start = (bf16[512,896]{1,0:T(8,128)(2,1)}, bf16[512,896]{1,0:T(8,128)(2,1)S(1)}, u32[]{:S(2)}, u32[]{:S(2)}) collective-permute-start(bf16[512,896]{1,0:T(8,128)(2,1)} %refs_0_.1), channel_id=1, source_target_pairs={{0,1},{1,0},{2,3},{3,2},{4,5},{5,4},{6,7},{7,6},{8,9},{9,8},{10,11... | collective-permute-start | bytes 2752520 | tf_op jit(solution)/shard_map/ppermute | solution.py:444
  3.7 21.3 %collective-permute-start.1 = (bf16[512,896]{1,0:T(8,128)(2,1)}, bf16[512,896]{1,0:T(8,128)(2,1)S(1)}, u32[]{:S(2)}, u32[]{:S(2)}) collective-permute-start(bf16[512,896]{1,0:T(8,128)(2,1)} %refs_0_.1), channel_id=1, source_target_pairs={{1,2},{2,1},{5,6},{6,5},{9,10},{10,9},{13,14},{14,13},{17,18},{18,... | collective-permute-start | bytes 2752520 | tf_op jit(solution)/shard_map/ppermute | solution.py:445
  6.5 47.4 %copy-start.5 = (s32[1,8]{1,0:T(1,128)S(1)}, s32[1,8]{1,0:T(1,128)}, u32[]{:S(2)}) copy-start(s32[1,8]{1,0:T(1,128)} %param.11) | copy-start | bytes 100
  6.5 48.8 %copy-start.2 = (bf16[2,128,896]{2,1,0:T(8,128)(2,1)S(1)}, bf16[2,128,896]{2,1,0:T(8,128)(2,1)}, u32[]{:S(2)}) copy-start(bf16[2,128,896]{2,1,0:T(8,128)(2,1)} %pool_own.1) | copy-start | bytes 1376260
  6.5 36.7 %collective-permute-start.3 = (bf16[448,1792]{1,0:T(8,128)(2,1)S(1)}, bf16[448,1792]{1,0:T(8,128)(2,1)}, u32[]{:S(2)}, u32[]{:S(2)}) collective-permute-start(bf16[448,1792]{1,0:T(8,128)(2,1)S(1)} %convert_element_type.2), channel_id=1, source_target_pairs={{0,16},{1,17},{2,18},{3,19},{4,0},{5,1},{6,2},{7,3},{8,24},{9,25},... | collective-permute-start | bytes 4816904 | tf_op jit(solution)/shard_map/ppermute | solution.py:460
  8.1 35.2 %collective-permute-start.4 = (bf16[448,1792]{1,0:T(8,128)(2,1)S(1)}, bf16[448,1792]{1,0:T(8,128)(2,1)}, u32[]{:S(2)}, u32[]{:S(2)}) collective-permute-start(bf16[448,1792]{1,0:T(8,128)(2,1)S(1)} %convert_element_type.2), channel_id=1, source_target_pairs={{0,0},{1,1},{2,2},{3,3},{4,16},{5,17},{6,18},{7,19},{8,8},{9,9},{1... | collective-permute-start | bytes 4816904 | tf_op jit(solution)/shard_map/ppermute | solution.py:461
  24.3 32.6 %copy-start = (bf16[512,896]{1,0:T(8,128)(2,1)}, bf16[512,896]{1,0:T(8,128)(2,1)S(1)}, u32[]{:S(2)}) copy-start(bf16[512,896]{1,0:T(8,128)(2,1)S(1)} %collective-permute-done.piece.refs_1_) | copy-start | bytes 2752516
  24.4 2.7 %collective-permute-start.5 = (bf16[320,896]{1,0:T(8,128)(2,1)S(1)}, bf16[320,896]{1,0:T(8,128)(2,1)S(1)}, u32[]{:S(2)}, u32[]{:S(2)}) collective-permute-start(bf16[320,896]{1,0:T(8,128)(2,1)S(1)} %get-tuple-element.13), channel_id=1, source_target_pairs={{1,2},{2,1},{5,6},{6,5},{9,10},{10,9},{13,14},{14,13},{17,18},{18,... | collective-permute-start | bytes 1720328 | tf_op jit(solution)/shard_map/ppermute | solution.py:448
  25.1 25.1 %copy-start.3 = (bf16[512,896]{1,0:T(8,128)(2,1)}, bf16[512,896]{1,0:T(8,128)(2,1)S(1)}, u32[]{:S(2)}) copy-start(bf16[512,896]{1,0:T(8,128)(2,1)S(1)} %collective-permute-done.1.refs_2_) | copy-start | bytes 2752516
  25.1 25.1 %collective-permute-start.2 = (bf16[512,896]{1,0:T(8,128)(2,1)S(1)}, bf16[512,896]{1,0:T(8,128)(2,1)S(1)}, u32[]{:S(2)}, u32[]{:S(2)}) collective-permute-start(bf16[512,896]{1,0:T(8,128)(2,1)S(1)} %collective-permute-done.1.refs_2_), channel_id=1, source_target_pairs={{1,0},{2,3},{5,4},{6,7},{9,8},{10,11},{13,12},{14,15},{17,16},{18,... | collective-permute-start | bytes 2752520 | tf_op jit(solution)/shard_map/ppermute | solution.py:446
  26.4 0.8 collective-permute-start.7
  27.1 16.1 %collective-permute-start.6 = (bf16[192,896]{1,0:T(8,128)(2,1)S(1)}, bf16[192,896]{1,0:T(8,128)(2,1)S(1)}, u32[]{:S(2)}, u32[]{:S(2)}) collective-permute-start(bf16[192,896]{1,0:T(8,128)(2,1)S(1)} %slice.4), channel_id=1, source_target_pairs={{0,8},{1,9},{2,10},{3,11},{4,12},{5,13},{6,14},{7,15},{8,0},{9,1},... | collective-permute-start | bytes 1032200 | tf_op jit(solution)/shard_map/ppermute | solution.py:456
  50.2 1.0 %copy-start.4 = (bf16[512,896]{1,0:T(8,128)(2,1)}, bf16[512,896]{1,0:T(8,128)(2,1)S(1)}, u32[]{:S(2)}) copy-start(bf16[512,896]{1,0:T(8,128)(2,1)S(1)} %collective-permute-done.2.refs_3_) | copy-start | bytes 2752516
  50.2 6.7 %collective-permute-start.8 = (bf16[448,1792]{1,0:T(8,128)(2,1)}, bf16[448,1792]{1,0:T(8,128)(2,1)}, u32[]{:S(2)}, u32[]{:S(2)}) collective-permute-start(bf16[448,1792]{1,0:T(8,128)(2,1)} %collective-permute-done.3.refs_4_), channel_id=1, source_target_pairs={{0,8},{1,9},{2,10},{3,11},{4,12},{5,13},{6,14},{7,15},{8,0},{9,1},... | collective-permute-start | bytes 4816904 | tf_op jit(solution)/shard_map/ppermute | solution.py:465
  50.2 6.7 %collective-permute-start.9 = (bf16[448,1792]{1,0:T(8,128)(2,1)}, bf16[448,1792]{1,0:T(8,128)(2,1)}, u32[]{:S(2)}, u32[]{:S(2)}) collective-permute-start(bf16[448,1792]{1,0:T(8,128)(2,1)} %collective-permute-done.4.refs_5_), channel_id=1, source_target_pairs={{0,8},{1,9},{2,10},{3,11},{4,12},{5,13},{6,14},{7,15},{8,0},{9,1},... | collective-permute-start | bytes 4816904 | tf_op jit(solution)/shard_map/ppermute | solution.py:466
  51.2 17.8 %collective-permute-start.13 = (bf16[320,896]{1,0:T(8,128)(2,1)S(1)}, bf16[320,896]{1,0:T(8,128)(2,1)S(1)}, u32[]{:S(2)}, u32[]{:S(2)}) collective-permute-start(bf16[320,896]{1,0:T(8,128)(2,1)S(1)} %collective-permute-done.5.mid_piece), channel_id=1, source_target_pairs={{1,0},{2,3},{5,4},{6,7},{9,8},{10,11},{13,12},{14,15},{17,16},{18,... | collective-permute-start | bytes 1720328 | tf_op jit(solution)/shard_map/ppermute | solution.py:450
  54.0 20.9 %collective-permute-start.10 = (bf16[192,896]{1,0:T(8,128)(2,1)S(1)}, bf16[192,896]{1,0:T(8,128)(2,1)S(1)}, u32[]{:S(2)}, u32[]{:S(2)}) collective-permute-start(bf16[192,896]{1,0:T(8,128)(2,1)S(1)} %collective-permute-done.7.mid_piece), channel_id=1, source_target_pairs={{1,0},{2,3},{5,4},{6,7},{9,8},{10,11},{13,12},{14,15},{17,16},{18,... | collective-permute-start | bytes 1032200 | tf_op jit(solution)/shard_map/ppermute | solution.py:450
  55.3 22.4 %collective-permute-start.12 = (bf16[2,128,896]{2,1,0:T(8,128)(2,1)S(1)}, bf16[2,128,896]{2,1,0:T(8,128)(2,1)S(1)}, u32[]{:S(2)}, u32[]{:S(2)}) collective-permute-start(bf16[2,128,896]{2,1,0:T(8,128)(2,1)S(1)} %copy-done.2), channel_id=1, source_target_pairs={{0,4},{1,5},{2,6},{3,7},{4,0},{5,1},{6,2},{7,3},{8,12},{9,13},{10,... | collective-permute-start | bytes 1376264 | tf_op jit(solution)/shard_map/ppermute | solution.py:467
  70.4 7.2 %copy-start.1 = (bf16[2,256,896]{2,1,0:T(8,128)(2,1)S(1)}, bf16[2,256,896]{2,1,0:T(8,128)(2,1)}, u32[]{:S(2)}) copy-start(bf16[2,256,896]{2,1,0:T(8,128)(2,1)} %prompt.1) | copy-start | bytes 2752516
  70.5 9.0 %collective-permute-start.14 = (bf16[160,896]{1,0:T(8,128)(2,1)S(1)}, bf16[160,896]{1,0:T(8,128)(2,1)S(1)}, u32[]{:S(2)}, u32[]{:S(2)}) collective-permute-start(bf16[160,896]{1,0:T(8,128)(2,1)S(1)} %get-tuple-element.23), channel_id=1, source_target_pairs={{0,4},{1,5},{2,6},{3,7},{4,0},{5,1},{6,2},{7,3},{8,12},{9,13},{10,... | collective-permute-start | bytes 860168 | tf_op jit(solution)/shard_map/ppermute | solution.py:487
  76.1 5.6 %collective-permute-start.11 = (bf16[96,896]{1,0:T(8,128)(2,1)S(1)}, bf16[96,896]{1,0:T(8,128)(2,1)S(1)}, u32[]{:S(2)}, u32[]{:S(2)}) collective-permute-start(bf16[96,896]{1,0:T(8,128)(2,1)S(1)} %shard_map.89), channel_id=1, source_target_pairs={{0,4},{1,5},{2,6},{3,7},{4,0},{5,1},{6,2},{7,3},{8,12},{9,13},{10,... | collective-permute-start | bytes 516104 | tf_op jit(solution)/shard_map/ppermute | solution.py:487

commit v6 on v4

--- a/solution.py
+++ b/solution.py
@@ -353,6 +353,19 @@
             lax.dot_general(head_q, aligned[0, head, :keys], NT, preferred_element_type=F32)
         )
     tiles = [None] * (width // 128)
+    early = 2 * HD // 128 * 128
+    copies = [
+        pltpu.make_async_copy(
+            done.at[:, low:high], out.at[pl.ds(first_row, rows), low:high], sem.at[at]
+        )
+        for at, (low, high) in enumerate(((0, early), (early, width)))
+    ]
+
+    def leave(copy, first, last):
+        for tile in range(first, last):
+            done[:, tile * 128 : (tile + 1) * 128] = tiles[tile].astype(BF16)
+        copy.start()
+
     for head in range(heads):
         low, high, offset = window(head, width)
         scores = jnp.where(seen, raw[head] * HD**-0.5, -1e30)
@@ -374,11 +387,11 @@
                 tiles[tile] = jnp.where(
                     lanes[:, :128] < head * HD - tile * 128, tiles[tile], part
                 )
-    for tile, part in enumerate(tiles):
-        done[:, tile * 128 : (tile + 1) * 128] = part.astype(BF16)
-    copy = pltpu.make_async_copy(done, out.at[pl.ds(first_row, rows)], sem)
-    copy.start()
-    copy.wait()
+        if head == 1:
+            leave(copies[0], 0, early // 128)
+    leave(copies[1], early // 128, len(tiles))
+    for copy in copies:
+        copy.wait()
 
 
 def attend(first_row, pool_keys, facts, own_q, other_q, aligned, before=None):
@@ -398,7 +411,7 @@
         out_specs=pl.BlockSpec(memory_space=pl.ANY),
         scratch_shapes=[
             pltpu.VMEM((rows, width), BF16),
-            pltpu.SemaphoreType.DMA(()),
+            pltpu.SemaphoreType.DMA((2,)),
         ],
         input_output_aliases={} if before is None else {4: 0},
         compiler_params=pltpu.CompilerParams(vmem_limit_bytes=8 * 1024 * 1024),

time: 84 us -> 84 us (level)
  no operation moved by 1% of the time
where the time goes in v6:
time: 84 us; the launch traced here: 83.7 us
  waiting for transfers between devices  44.5 us (53%)
  starting transfers between devices  17.7 us (21%)
  Pallas kernels  16.6 us (20%)
  between operations  2.23 us (3%)
  other arithmetic  2.07 us (2%)
    ppermute x1, waiting for transfers between devices, square_body(): ring = [send(piece, perm=RING_MOVE) for piece in own_w]  16 us
    ppermute x1, waiting for transfers between devices, square_body(): near = send(tokens, perm=PAIR_MOVE)  14.4 us
    pallas_call x1, Pallas kernels, query_part(): pl.pallas_call(query_kernel, out_shape=(pltpu.VMEM((rows, heads), F32), p...  8.9 us
    ppermute x1, waiting for transfers between devices, square_body(): end_own = send(mid_own, perm=END_MOVE)  6.93 us
    ppermute x2, waiting for transfers between devices, square_body(): end_near = [send(piece, perm=END_MOVE) for piece in mid_near]  6.03 us
    pallas_call x2, Pallas kernels, attend(): pl.pallas_call(functools.partial(attend_kernel, first_row, pool_keys), ou...  4.24 us
    ppermute x2, starting transfers between devices, square_body(): other_q = [send(piece, perm=BLK_MOVE) for piece in send_q]  3.17 us
    ppermute x1, starting transfers between devices, square_body(): near = send(tokens, perm=PAIR_MOVE)  3.09 us
  transfers between devices with their start and end apart: 15, of which 6 were waited for; matrix products, arithmetic and copies ran while one was open for 3% of the time, Pallas kernels for 17%

profile of v6, /device:TPU:0, one launch (start us, length us, event | category | flops | bytes accessed | tf_op | source)
XLA Modules:
  0.0 83.7 jit_solution(10297807496334779582)
XLA Ops:
  0.6 3.1 %collective-permute-start = (bf16[512,896]{1,0:T(8,128)(2,1)}, bf16[512,896]{1,0:T(8,128)(2,1)S(1)}, u32[]{:S(2)}, u32[]{:S(2)}) collective-permute-start(bf16[512,896]{1,0:T(8,128)(2,1)} %refs_0_.1), channel_id=1, source_target_pairs={{0,1},{1,0},{2,3},{3,2},{4,5},{5,4},{6,7},{7,6},{8,9},{9,8},{10,11... | collective-permute-start | bytes 2752520 | tf_op jit(solution)/shard_map/ppermute | solution.py:429
  3.7 0.7 collective-permute-start.1
  4.4 2.1 %convert_element_type.2 = bf16[448,1792]{1,0:T(8,128)(2,1)S(1)} convert(f32[448,1792]{1,0:T(8,128)} %param.8) | non-fusion elementwise | flops 802816 | bytes 4816896 | tf_op jit(solution)/shard_map/convert_element_type | solution.py:444
  6.5 0.0 copy-start.5
  6.5 0.0 copy-start.2
  6.5 1.5 %collective-permute-start.3 = (bf16[448,1792]{1,0:T(8,128)(2,1)S(1)}, bf16[448,1792]{1,0:T(8,128)(2,1)}, u32[]{:S(2)}, u32[]{:S(2)}) collective-permute-start(bf16[448,1792]{1,0:T(8,128)(2,1)S(1)} %convert_element_type.2), channel_id=1, source_target_pairs={{0,16},{1,17},{2,18},{3,19},{4,0},{5,1},{6,2},{7,3},{8,24},{9,25},... | collective-permute-start | bytes 4816904 | tf_op jit(solution)/shard_map/ppermute | solution.py:445
  8.1 1.8 %collective-permute-start.4 = (bf16[448,1792]{1,0:T(8,128)(2,1)S(1)}, bf16[448,1792]{1,0:T(8,128)(2,1)}, u32[]{:S(2)}, u32[]{:S(2)}) collective-permute-start(bf16[448,1792]{1,0:T(8,128)(2,1)S(1)} %convert_element_type.2), channel_id=1, source_target_pairs={{0,0},{1,1},{2,2},{3,3},{4,16},{5,17},{6,18},{7,19},{8,8},{9,9},{1... | collective-permute-start | bytes 4816904 | tf_op jit(solution)/shard_map/ppermute | solution.py:446
  9.9 14.4 %collective-permute-done.piece.refs_1_ = bf16[512,896]{1,0:T(8,128)(2,1)S(1)} collective-permute-done((bf16[512,896]{1,0:T(8,128)(2,1)}, bf16[512,896]{1,0:T(8,128)(2,1)S(1)}, u32[]{:S(2)}, u32[]{:S(2)}) %collective-permute-start) | collective-permute-done | bytes 917536 | tf_op jit(solution)/shard_map/ppermute | solution.py:429
  24.3 0.1 shard_map.86
  24.4 0.7 collective-permute-start.5
  25.1 0.0 collective-permute-done.1.refs_2_
  25.1 0.0 copy-start.3
  25.1 1.3 %collective-permute-start.2 = (bf16[512,896]{1,0:T(8,128)(2,1)S(1)}, bf16[512,896]{1,0:T(8,128)(2,1)S(1)}, u32[]{:S(2)}, u32[]{:S(2)}) collective-permute-start(bf16[512,896]{1,0:T(8,128)(2,1)S(1)} %collective-permute-done.1.refs_2_), channel_id=1, source_target_pairs={{1,0},{2,3},{5,4},{6,7},{9,8},{10,11},{13,12},{14,15},{17,16},{18,... | collective-permute-start | bytes 2752520 | tf_op jit(solution)/shard_map/ppermute | solution.py:431
  26.4 0.7 collective-permute-start.7
  27.1 0.0 collective-permute-done.5.mid_piece
  27.1 0.1 collective-permute-start.6
  27.2 0.0 collective-permute-done.7.mid_piece
  27.2 16.0 %collective-permute-done.3.refs_4_ = bf16[448,1792]{1,0:T(8,128)(2,1)} collective-permute-done((bf16[448,1792]{1,0:T(8,128)(2,1)S(1)}, bf16[448,1792]{1,0:T(8,128)(2,1)}, u32[]{:S(2)}, u32[]{:S(2)}) %collective-permute-start.3) | collective-permute-done | bytes 1605664 | tf_op jit(solution)/shard_map/ppermute | solution.py:445
  43.2 0.0 collective-permute-done.4.refs_5_
  43.2 0.0 collective-permute-done.6.refs_8_
  43.2 6.9 %collective-permute-done.2.refs_3_ = bf16[512,896]{1,0:T(8,128)(2,1)S(1)} collective-permute-done((bf16[512,896]{1,0:T(8,128)(2,1)S(1)}, bf16[512,896]{1,0:T(8,128)(2,1)S(1)}, u32[]{:S(2)}, u32[]{:S(2)}) %collective-permute-start.2) | collective-permute-done | bytes 917536 | tf_op jit(solution)/shard_map/ppermute | solution.py:431
  50.2 0.0 collective-permute-start.8
  50.2 0.0 copy-done.3
  50.2 0.5 collective-permute-start.9
  50.7 0.5 copy-done.4
  51.2 1.3 %collective-permute-start.13 = (bf16[320,896]{1,0:T(8,128)(2,1)S(1)}, bf16[320,896]{1,0:T(8,128)(2,1)S(1)}, u32[]{:S(2)}, u32[]{:S(2)}) collective-permute-start(bf16[320,896]{1,0:T(8,128)(2,1)S(1)} %collective-permute-done.5.mid_piece), channel_id=1, source_target_pairs={{1,0},{2,3},{5,4},{6,7},{9,8},{10,11},{13,12},{14,15},{17,16},{18,... | collective-permute-start | bytes 1720328 | tf_op jit(solution)/shard_map/ppermute | solution.py:435
  53.9 0.0 copy-done.5
  53.9 0.1 concatenate.3.facts
  54.0 1.3 %collective-permute-start.10 = (bf16[192,896]{1,0:T(8,128)(2,1)S(1)}, bf16[192,896]{1,0:T(8,128)(2,1)S(1)}, u32[]{:S(2)}, u32[]{:S(2)}) collective-permute-start(bf16[192,896]{1,0:T(8,128)(2,1)S(1)} %collective-permute-done.7.mid_piece), channel_id=1, source_target_pairs={{1,0},{2,3},{5,4},{6,7},{9,8},{10,11},{13,12},{14,15},{17,16},{18,... | collective-permute-start | bytes 1032200 | tf_op jit(solution)/shard_map/ppermute | solution.py:435
  55.3 0.0 copy-done.2
  55.3 1.6 %collective-permute-start.12 = (bf16[2,128,896]{2,1,0:T(8,128)(2,1)S(1)}, bf16[2,128,896]{2,1,0:T(8,128)(2,1)S(1)}, u32[]{:S(2)}, u32[]{:S(2)}) collective-permute-start(bf16[2,128,896]{2,1,0:T(8,128)(2,1)S(1)} %copy-done.2), channel_id=1, source_target_pairs={{0,4},{1,5},{2,6},{3,7},{4,0},{5,1},{6,2},{7,3},{8,12},{9,13},{10,... | collective-permute-start | bytes 1376264 | tf_op jit(solution)/shard_map/ppermute | solution.py:452
  56.9 0.0 collective-permute-done.8.refs_6_
  56.9 0.0 collective-permute-done.9.refs_7_
  56.9 0.0 copy-done
  56.9 8.9 %shard_map.87 = (f32[512,896]{1,0:T(8,128)S(1)}, bf16[896,896]{1,0:T(8,128)(2,1)S(1)}, bf16[896,3584]{1,0:T(8,128)(2,1)}) custom-call(s32[25]{0:T(128)S(1)} %concatenate.3.facts, bf16[512,896]{1,0:T(8,128)(2,1)} %refs_0_.1, bf16[512,896]{1,0:T(8,128)(2,1)} %copy-done, bf16[512,896]{1,0:T(8,128)(2,1)} %copy-done.3, bf16[512,896]{1,0:T(8,128)(2,1)} %copy-done.4, ...), custom_call_target="tpu_custom_call" | custom-call | flops 2466250752 | bytes 16515072 | tf_op jit(solution)/shard_map/pallas_call | solution.py:215
  65.8 3.2 %collective-permute-done.13.end_piece = bf16[320,896]{1,0:T(8,128)(2,1)S(1)} collective-permute-done((bf16[320,896]{1,0:T(8,128)(2,1)S(1)}, bf16[320,896]{1,0:T(8,128)(2,1)S(1)}, u32[]{:S(2)}, u32[]{:S(2)}) %collective-permute-start.13) | collective-permute-done | bytes 573472 | tf_op jit(solution)/shard_map/ppermute | solution.py:435
  69.0 1.5 %shard_map.90 = (f32[160,896]{1,0:T(8,128)S(1)}, bf16[160,896]{1,0:T(8,128)(2,1)S(1)}) custom-call(s32[25]{0:T(128)S(1)} %concatenate.3.facts, bf16[320,896]{1,0:T(8,128)(2,1)S(1)} %collective-permute-done.5.mid_piece, bf16[320,896]{1,0:T(8,128)(2,1)S(1)} %collective-permute-done.13.end_piece, f32[512,896]{1,0:T(8,128)S(1)} %get-tuple-element.21.so_far, ...), custom_call_target="tpu_custom_call" | custom-call | flops 513802240 | bytes 2752512 | tf_op jit(solution)/shard_map/pallas_call | solution.py:264
  70.5 0.0 copy-start.1
  70.5 1.6 %collective-permute-start.14 = (bf16[160,896]{1,0:T(8,128)(2,1)S(1)}, bf16[160,896]{1,0:T(8,128)(2,1)S(1)}, u32[]{:S(2)}, u32[]{:S(2)}) collective-permute-start(bf16[160,896]{1,0:T(8,128)(2,1)S(1)} %get-tuple-element.27), channel_id=1, source_target_pairs={{0,4},{1,5},{2,6},{3,7},{4,0},{5,1},{6,2},{7,3},{8,12},{9,13},{10,... | collective-permute-start | bytes 860168 | tf_op jit(solution)/shard_map/ppermute | solution.py:469
  72.1 2.8 %collective-permute-done.10.end_piece = bf16[192,896]{1,0:T(8,128)(2,1)S(1)} collective-permute-done((bf16[192,896]{1,0:T(8,128)(2,1)S(1)}, bf16[192,896]{1,0:T(8,128)(2,1)S(1)}, u32[]{:S(2)}, u32[]{:S(2)}) %collective-permute-start.10) | collective-permute-done | bytes 344096 | tf_op jit(solution)/shard_map/ppermute | solution.py:435
  74.9 1.3 %shard_map.88 = (f32[96,896]{1,0:T(8,128)S(1)}, bf16[96,896]{1,0:T(8,128)(2,1)S(1)}) custom-call(s32[25]{0:T(128)S(1)} %concatenate.3.facts, bf16[192,896]{1,0:T(8,128)(2,1)S(1)} %collective-permute-done.7.mid_piece, bf16[192,896]{1,0:T(8,128)(2,1)S(1)} %collective-permute-done.10.end_piece, f32[512,896]{1,0:T(8,128)S(1)} %get-tuple-element.21.so_far, ...), custom_call_target="tpu_custom_call" | custom-call | flops 308281344 | bytes 2293760 | tf_op jit(solution)/shard_map/pallas_call | solution.py:264
  76.2 1.6 %collective-permute-start.11 = (bf16[96,896]{1,0:T(8,128)(2,1)S(1)}, bf16[96,896]{1,0:T(8,128)(2,1)S(1)}, u32[]{:S(2)}, u32[]{:S(2)}) collective-permute-start(bf16[96,896]{1,0:T(8,128)(2,1)S(1)} %get-tuple-element.24), channel_id=1, source_target_pairs={{0,4},{1,5},{2,6},{3,7},{4,0},{5,1},{6,2},{7,3},{8,12},{9,13},{10,... | collective-permute-start | bytes 516104 | tf_op jit(solution)/shard_map/ppermute | solution.py:469
  77.8 0.0 collective-permute-done.12.pool_other
  77.8 0.6 shard_map.89.aligned
  78.4 0.0 collective-permute-done.14.other_q
  78.4 2.2 %shard_map.91.refs_0_ = bf16[256,896]{1,0:T(8,128)(2,1)} custom-call(s32[25]{0:T(128)S(1)} %concatenate.3.facts, f32[160,896]{1,0:T(8,128)S(1)} %get-tuple-element.26.own_q, bf16[160,896]{1,0:T(8,128)(2,1)S(1)} %collective-permute-done.14.other_q, bf16[2,4,512,256]{3,2,1,0:T(8,128)(2,1)S(1)} %shard_map.89.aligned), custom_call_target="tpu_custom_call" | custom-call | flops 293601280 | bytes 3670016 | tf_op jit(solution)/shard_map/pallas_call | solution.py:407
  80.6 1.0 %collective-permute-done.11.other_q = bf16[96,896]{1,0:T(8,128)(2,1)S(1)} collective-permute-done((bf16[96,896]{1,0:T(8,128)(2,1)S(1)}, bf16[96,896]{1,0:T(8,128)(2,1)S(1)}, u32[]{:S(2)}, u32[]{:S(2)}) %collective-permute-start.11) | collective-permute-done | bytes 172064 | tf_op jit(solution)/shard_map/ppermute | solution.py:469
  81.6 2.1 %shard_map.92 = bf16[256,896]{1,0:T(8,128)(2,1)} custom-call(s32[25]{0:T(128)S(1)} %concatenate.3.facts, f32[96,896]{1,0:T(8,128)S(1)} %get-tuple-element.23.own_q, bf16[96,896]{1,0:T(8,128)(2,1)S(1)} %collective-permute-done.11.other_q, bf16[2,4,512,256]{3,2,1,0:T(8,128)(2,1)S(1)} %shard_map.89.aligned, ...), custom_call_target="tpu_custom_call", output_to_operand_aliasing={{}: (4, {})} | custom-call | flops 176160768 | bytes 3670016 | tf_op jit(solution)/shard_map/pallas_call | solution.py:407
  (4 shorter events, 0.0 us)
Async XLA Ops:
  0.6 23.7 %collective-permute-start = (bf16[512,896]{1,0:T(8,128)(2,1)}, bf16[512,896]{1,0:T(8,128)(2,1)S(1)}, u32[]{:S(2)}, u32[]{:S(2)}) collective-permute-start(bf16[512,896]{1,0:T(8,128)(2,1)} %refs_0_.1), channel_id=1, source_target_pairs={{0,1},{1,0},{2,3},{3,2},{4,5},{5,4},{6,7},{7,6},{8,9},{9,8},{10,11... | collective-permute-start | bytes 2752520 | tf_op jit(solution)/shard_map/ppermute | solution.py:429
  3.7 21.3 %collective-permute-start.1 = (bf16[512,896]{1,0:T(8,128)(2,1)}, bf16[512,896]{1,0:T(8,128)(2,1)S(1)}, u32[]{:S(2)}, u32[]{:S(2)}) collective-permute-start(bf16[512,896]{1,0:T(8,128)(2,1)} %refs_0_.1), channel_id=1, source_target_pairs={{1,2},{2,1},{5,6},{6,5},{9,10},{10,9},{13,14},{14,13},{17,18},{18,... | collective-permute-start | bytes 2752520 | tf_op jit(solution)/shard_map/ppermute | solution.py:430
  6.5 47.4 %copy-start.5 = (s32[1,8]{1,0:T(1,128)S(1)}, s32[1,8]{1,0:T(1,128)}, u32[]{:S(2)}) copy-start(s32[1,8]{1,0:T(1,128)} %param.11) | copy-start | bytes 100
  6.5 48.8 %copy-start.2 = (bf16[2,128,896]{2,1,0:T(8,128)(2,1)S(1)}, bf16[2,128,896]{2,1,0:T(8,128)(2,1)}, u32[]{:S(2)}) copy-start(bf16[2,128,896]{2,1,0:T(8,128)(2,1)} %pool_own.1) | copy-start | bytes 1376260
  6.5 36.7 %collective-permute-start.3 = (bf16[448,1792]{1,0:T(8,128)(2,1)S(1)}, bf16[448,1792]{1,0:T(8,128)(2,1)}, u32[]{:S(2)}, u32[]{:S(2)}) collective-permute-start(bf16[448,1792]{1,0:T(8,128)(2,1)S(1)} %convert_element_type.2), channel_id=1, source_target_pairs={{0,16},{1,17},{2,18},{3,19},{4,0},{5,1},{6,2},{7,3},{8,24},{9,25},... | collective-permute-start | bytes 4816904 | tf_op jit(solution)/shard_map/ppermute | solution.py:445
  8.1 35.2 %collective-permute-start.4 = (bf16[448,1792]{1,0:T(8,128)(2,1)S(1)}, bf16[448,1792]{1,0:T(8,128)(2,1)}, u32[]{:S(2)}, u32[]{:S(2)}) collective-permute-start(bf16[448,1792]{1,0:T(8,128)(2,1)S(1)} %convert_element_type.2), channel_id=1, source_target_pairs={{0,0},{1,1},{2,2},{3,3},{4,16},{5,17},{6,18},{7,19},{8,8},{9,9},{1... | collective-permute-start | bytes 4816904 | tf_op jit(solution)/shard_map/ppermute | solution.py:446
  24.3 32.6 %copy-start = (bf16[512,896]{1,0:T(8,128)(2,1)}, bf16[512,896]{1,0:T(8,128)(2,1)S(1)}, u32[]{:S(2)}) copy-start(bf16[512,896]{1,0:T(8,128)(2,1)S(1)} %collective-permute-done.piece.refs_1_) | copy-start | bytes 2752516
  24.4 2.7 %collective-permute-start.5 = (bf16[320,896]{1,0:T(8,128)(2,1)S(1)}, bf16[320,896]{1,0:T(8,128)(2,1)S(1)}, u32[]{:S(2)}, u32[]{:S(2)}) collective-permute-start(bf16[320,896]{1,0:T(8,128)(2,1)S(1)} %get-tuple-element.15), channel_id=1, source_target_pairs={{1,2},{2,1},{5,6},{6,5},{9,10},{10,9},{13,14},{14,13},{17,18},{18,... | collective-permute-start | bytes 1720328 | tf_op jit(solution)/shard_map/ppermute | solution.py:433
  25.1 25.1 %copy-start.3 = (bf16[512,896]{1,0:T(8,128)(2,1)}, bf16[512,896]{1,0:T(8,128)(2,1)S(1)}, u32[]{:S(2)}) copy-start(bf16[512,896]{1,0:T(8,128)(2,1)S(1)} %collective-permute-done.1.refs_2_) | copy-start | bytes 2752516
  25.1 25.1 %collective-permute-start.2 = (bf16[512,896]{1,0:T(8,128)(2,1)S(1)}, bf16[512,896]{1,0:T(8,128)(2,1)S(1)}, u32[]{:S(2)}, u32[]{:S(2)}) collective-permute-start(bf16[512,896]{1,0:T(8,128)(2,1)S(1)} %collective-permute-done.1.refs_2_), channel_id=1, source_target_pairs={{1,0},{2,3},{5,4},{6,7},{9,8},{10,11},{13,12},{14,15},{17,16},{18,... | collective-permute-start | bytes 2752520 | tf_op jit(solution)/shard_map/ppermute | solution.py:431
  26.4 0.8 collective-permute-start.7
  27.1 16.1 %collective-permute-start.6 = (bf16[192,896]{1,0:T(8,128)(2,1)S(1)}, bf16[192,896]{1,0:T(8,128)(2,1)S(1)}, u32[]{:S(2)}, u32[]{:S(2)}) collective-permute-start(bf16[192,896]{1,0:T(8,128)(2,1)S(1)} %slice.4), channel_id=1, source_target_pairs={{0,8},{1,9},{2,10},{3,11},{4,12},{5,13},{6,14},{7,15},{8,0},{9,1},... | collective-permute-start | bytes 1032200 | tf_op jit(solution)/shard_map/ppermute | solution.py:441
  50.2 1.0 %copy-start.4 = (bf16[512,896]{1,0:T(8,128)(2,1)}, bf16[512,896]{1,0:T(8,128)(2,1)S(1)}, u32[]{:S(2)}) copy-start(bf16[512,896]{1,0:T(8,128)(2,1)S(1)} %collective-permute-done.2.refs_3_) | copy-start | bytes 2752516
  50.2 6.7 %collective-permute-start.8 = (bf16[448,1792]{1,0:T(8,128)(2,1)}, bf16[448,1792]{1,0:T(8,128)(2,1)}, u32[]{:S(2)}, u32[]{:S(2)}) collective-permute-start(bf16[448,1792]{1,0:T(8,128)(2,1)} %collective-permute-done.3.refs_4_), channel_id=1, source_target_pairs={{0,8},{1,9},{2,10},{3,11},{4,12},{5,13},{6,14},{7,15},{8,0},{9,1},... | collective-permute-start | bytes 4816904 | tf_op jit(solution)/shard_map/ppermute | solution.py:450
  50.2 6.7 %collective-permute-start.9 = (bf16[448,1792]{1,0:T(8,128)(2,1)}, bf16[448,1792]{1,0:T(8,128)(2,1)}, u32[]{:S(2)}, u32[]{:S(2)}) collective-permute-start(bf16[448,1792]{1,0:T(8,128)(2,1)} %collective-permute-done.4.refs_5_), channel_id=1, source_target_pairs={{0,8},{1,9},{2,10},{3,11},{4,12},{5,13},{6,14},{7,15},{8,0},{9,1},... | collective-permute-start | bytes 4816904 | tf_op jit(solution)/shard_map/ppermute | solution.py:451
  51.2 17.8 %collective-permute-start.13 = (bf16[320,896]{1,0:T(8,128)(2,1)S(1)}, bf16[320,896]{1,0:T(8,128)(2,1)S(1)}, u32[]{:S(2)}, u32[]{:S(2)}) collective-permute-start(bf16[320,896]{1,0:T(8,128)(2,1)S(1)} %collective-permute-done.5.mid_piece), channel_id=1, source_target_pairs={{1,0},{2,3},{5,4},{6,7},{9,8},{10,11},{13,12},{14,15},{17,16},{18,... | collective-permute-start | bytes 1720328 | tf_op jit(solution)/shard_map/ppermute | solution.py:435
  54.0 20.9 %collective-permute-start.10 = (bf16[192,896]{1,0:T(8,128)(2,1)S(1)}, bf16[192,896]{1,0:T(8,128)(2,1)S(1)}, u32[]{:S(2)}, u32[]{:S(2)}) collective-permute-start(bf16[192,896]{1,0:T(8,128)(2,1)S(1)} %collective-permute-done.7.mid_piece), channel_id=1, source_target_pairs={{1,0},{2,3},{5,4},{6,7},{9,8},{10,11},{13,12},{14,15},{17,16},{18,... | collective-permute-start | bytes 1032200 | tf_op jit(solution)/shard_map/ppermute | solution.py:435
  55.3 22.5 %collective-permute-start.12 = (bf16[2,128,896]{2,1,0:T(8,128)(2,1)S(1)}, bf16[2,128,896]{2,1,0:T(8,128)(2,1)S(1)}, u32[]{:S(2)}, u32[]{:S(2)}) collective-permute-start(bf16[2,128,896]{2,1,0:T(8,128)(2,1)S(1)} %copy-done.2), channel_id=1, source_target_pairs={{0,4},{1,5},{2,6},{3,7},{4,0},{5,1},{6,2},{7,3},{8,12},{9,13},{10,... | collective-permute-start | bytes 1376264 | tf_op jit(solution)/shard_map/ppermute | solution.py:452
  70.5 7.3 %copy-start.1 = (bf16[2,256,896]{2,1,0:T(8,128)(2,1)S(1)}, bf16[2,256,896]{2,1,0:T(8,128)(2,1)}, u32[]{:S(2)}) copy-start(bf16[2,256,896]{2,1,0:T(8,128)(2,1)} %prompt.1) | copy-start | bytes 2752516
  70.5 7.9 %collective-permute-start.14 = (bf16[160,896]{1,0:T(8,128)(2,1)S(1)}, bf16[160,896]{1,0:T(8,128)(2,1)S(1)}, u32[]{:S(2)}, u32[]{:S(2)}) collective-permute-start(bf16[160,896]{1,0:T(8,128)(2,1)S(1)} %get-tuple-element.27), channel_id=1, source_target_pairs={{0,4},{1,5},{2,6},{3,7},{4,0},{5,1},{6,2},{7,3},{8,12},{9,13},{10,... | collective-permute-start | bytes 860168 | tf_op jit(solution)/shard_map/ppermute | solution.py:469
  76.2 5.5 %collective-permute-start.11 = (bf16[96,896]{1,0:T(8,128)(2,1)S(1)}, bf16[96,896]{1,0:T(8,128)(2,1)S(1)}, u32[]{:S(2)}, u32[]{:S(2)}) collective-permute-start(bf16[96,896]{1,0:T(8,128)(2,1)S(1)} %get-tuple-element.24), channel_id=1, source_target_pairs={{0,4},{1,5},{2,6},{3,7},{4,0},{5,1},{6,2},{7,3},{8,12},{9,13},{10,... | collective-permute-start | bytes 516104 | tf_op jit(solution)/shard_map/ppermute | solution.py:469
